TPU v7x, 32 devices: a whole 2x2x4 slice. The times are simulated.
32 devices in a mesh: basis: 16 (over z, x, core), band: 2 (over y).
Axes of the slice: x: 2, y: 2, z: 4, core: 2. Of those that a mesh axis runs over, the one named last changes fastest.
Arguments:
- matching: bfloat16 [162, 40960], P(None, 'basis'), may hold values from -6 to 6
- vectors: bfloat16 [40960, 4096], P('basis', 'band'), may hold values from -0.03125 to 0.03125
- weights: float32 [4096], P('band'), may hold values from 4.8828126e-05 to 0.00048828125
- gaunt_index: int32 [3, 4096], replicated, may hold values from 0 to 80
- gaunt_value: float32 [4096], replicated, may hold values from -4 to 4
Outputs:
- density_matrix: float32 [162, 162], replicated
- density: float32 [4, 81], replicated
All inputs are finite; a program needn't handle non-finite values.
Results may differ from a plain program's by a relative error of at most 0.0003.
Values sent between devices are 32-bit elements; how exact they have to be, the bound alone decides.
No kernel may reach another device: no remote copies, remote signals or barrier semaphores. Data moves between devices by JAX's collectives and lax.ppermute only.
A program may use at most 64 MiB of HBM per device.

v0:
```python
import jax
import jax.numpy as jnp
from jax import lax
from jax.sharding import PartitionSpec as P


def weighted_pairs(coeffs, band_weights):
    scaled = coeffs * band_weights[None, :]
    return lax.dot_general(
        scaled,
        coeffs,
        (((1,), (1,)), ((), ())),
        precision=lax.Precision.HIGHEST,
        preferred_element_type=jnp.float32,
    )


def gaunt_density(density_matrix, gaunt_index, gaunt_value):
    harmonics = density_matrix.shape[0] // 2
    codes = jnp.arange(harmonics, dtype=jnp.int32)[:, None]
    first_table = (gaunt_index[0][None, :] == codes).astype(jnp.float32)
    second_table = (gaunt_index[1][None, :] == codes).astype(jnp.float32)
    target_table = (gaunt_index[2][None, :] == codes).astype(jnp.float32)
    collected = []
    for radial in range(2):
        for other in range(2):
            block = density_matrix[
                radial * harmonics : (radial + 1) * harmonics,
                other * harmonics : (other + 1) * harmonics,
            ]
            spread = jnp.dot(
                block,
                second_table,
                precision=lax.Precision.HIGHEST,
                preferred_element_type=jnp.float32,
            )
            picked = jnp.sum(spread * first_table, axis=0)
            collected.append(picked * gaunt_value)
    values = jnp.stack(collected)
    return lax.dot_general(
        values,
        target_table,
        (((1,), (1,)), ((), ())),
        precision=lax.Precision.HIGHEST,
        preferred_element_type=jnp.float32,
    )


def body(matching, vectors, weights, gaunt_index, gaunt_value):
    partial_value = jnp.dot(matching, vectors, preferred_element_type=jnp.float32)
    summed = lax.psum(partial_value, "basis")
    local_terms = weighted_pairs(summed, weights)
    density_matrix = lax.psum(local_terms, "band")
    density = gaunt_density(density_matrix, gaunt_index, gaunt_value)
    return (density_matrix, density)


def solution(mesh):
    return jax.shard_map(
        body,
        mesh=mesh,
        in_specs=(P(None, "basis"), P("basis", "band"), P("band"), P(), P()),
        out_specs=(P(), P()),
        check_vma=False,
    )
```

profile of v0, /device:TPU:0, one launch (start us, length us, event | category | flops | bytes accessed | tf_op | source)
XLA Modules:
  0.0 151.2 jit_solution(6665116308786736758)
XLA Ops:
  7.2 0.0 copy-start
  7.2 0.0 copy-start.4
  7.2 0.0 all-reduce.3.cloned.1.call-start
  7.2 1.1 copy-done
  8.3 7.1 %fusion.27 = f32[162,2048]{1,0:T(8,128)} fusion(bf16[162,2560]{1,0:T(8,128)(2,1)S(1)} %copy-done, bf16[2560,2048]{1,0:T(8,128)(2,1)} %param.6), kind=kOutput, calls=%fused_computation.34 | convolution fusion | flops 1698693120 | bytes 12642304 | tf_op jit(solution)/shard_map/dot_general | solution.py:50
  15.4 0.0 all-reduce.3.cloned.1.call-update
  15.4 0.0 copy-start.2
  15.4 0.0 all-reduce.5.cloned.1.call-start
  15.5 97.3 %all-reduce.3.cloned.1.call-done = f32[162,2048]{1,0:T(8,128)} async-done(((f32[162,2048]{1,0:T(8,128)}), f32[162,2048]{1,0:T(8,128)}) %all-reduce.3.cloned.1.call-update) | async-done | bytes 1327120 | tf_op jit(solution)/shard_map/psum | solution.py:51
  112.8 0.0 copy-done.4
  112.8 3.8 %fusion = f32[162,162]{1,0:T(8,128)} fusion(f32[162,2048]{1,0:T(8,128)} %all-reduce.3.cloned.1.call-done, f32[2048]{0:T(1024)S(1)} %copy-done.4), kind=kOutput, calls=%fused_computation.4 | convolution fusion | flops 645304320 | bytes 1440272 | tf_op jit(solution)/shard_map/dot_general | solution.py:9
  116.6 0.0 all-reduce.5.cloned.1.call-update
  116.6 0.0 copy-done.2
  116.6 21.0 %all-reduce.5.cloned.1.call-done = f32[162,162]{1,0:T(8,128)} async-done(((f32[162,162]{1,0:T(8,128)}), f32[162,162]{1,0:T(8,128)}) %all-reduce.5.cloned.1.call-update) | async-done | bytes 104992 | tf_op jit(solution)/shard_map/psum | solution.py:53
  137.6 0.0 copy-start.1
  137.6 1.7 %fusion.3 = f32[4096]{0:T(1024)S(1)} fusion(s32[4096]{0:T(1024)S(1)} %bitcast.19, s32[4096]{0:T(1024)S(1)} %bitcast.15, f32[162,162]{1,0:T(8,128)} %all-reduce.5.cloned.1.call-done), kind=kOutput, calls=%fused_computation.10 | convolution fusion | flops 323809280 | bytes 94208 | tf_op jit(solution)/shard_map/dot_general | solution.py:31
  139.4 0.0 copy-done.1
  139.4 0.9 fusion.4
  140.3 0.0 copy-start.3
  140.3 0.9 fusion.6
  141.3 0.9 fusion.5
  142.2 0.0 copy-done.3
  142.3 1.4 fusion.2
  143.6 0.7 copy.9
  (2 shorter events, 0.0 us)
Async XLA Ops:
  7.2 1.2 copy-start
  7.2 105.6 %copy-start.4 = (f32[2048]{0:T(1024)S(1)}, f32[2048]{0:T(1024)}, u32[]{:S(2)}) copy-start(f32[2048]{0:T(1024)} %param.7) | copy-start | bytes 24580
  7.2 105.6 %all-reduce.3.cloned.1.call-start = ((), (), s32[]{:S(2)}) async-start(), calls=%async_computation | async-start | bytes 2752512 | tf_op jit(solution)/shard_map/psum | solution.py:51
  15.4 101.2 %copy-start.2 = (s32[3,4096]{1,0:T(4,128)S(1)}, s32[3,4096]{1,0:T(4,128)}, u32[]{:S(2)}) copy-start(s32[3,4096]{1,0:T(4,128)} %param.8) | copy-start | bytes 147460
  15.4 122.2 %all-reduce.5.cloned.1.call-start = ((), (), s32[]{:S(2)}) async-start(), calls=%async_computation.1 | async-start | bytes 344064 | tf_op jit(solution)/shard_map/psum | solution.py:53
  137.6 1.8 %copy-start.1 = (f32[162,162]{1,0:T(8,128)S(1)}, f32[162,162]{1,0:T(8,128)}, u32[]{:S(2)}) copy-start(f32[162,162]{1,0:T(8,128)} %all-reduce.5.cloned.1.call-done) | copy-start | bytes 314932
  140.3 1.9 %copy-start.3 = (f32[4096]{0:T(1024)S(1)}, f32[4096]{0:T(1024)}, u32[]{:S(2)}) copy-start(f32[4096]{0:T(1024)} %param.9) | copy-start | bytes 49156
Sparse Core Ops, SparseCore 0:
  15.5 97.2 all-reduce.2
  116.7 20.8 all-reduce.4
where the time goes:
time: 151 us
  waiting for transfers between devices  118 us (78%)
  matrix products  16.8 us (11%)
  between operations  14.1 us (9%)
  local copies, waits for them, and re-layouts  1.83 us (1%)
    psum x1, waiting for transfers between devices, body(): summed = lax.psum(partial_value, 'basis')  97.3 us
    psum x1, waiting for transfers between devices, body(): density_matrix = lax.psum(local_terms, 'band')  21 us
    dot_general x1, matrix products, body(): jnp.dot(matching, vectors, preferred_element_type=jnp.float32)  7.05 us
    dot_general x4, matrix products, gaunt_density(): jnp.dot(block, second_table, precision=lax.Precision.HIGHEST, preferred_e...  4.53 us
    dot_general x1, matrix products, weighted_pairs(): lax.dot_general(scaled, coeffs, (((1,), (1,)), ((), ())), precision=lax.P...  3.78 us
  transfers between devices with their start and end apart: 2, of which 2 were waited for; matrix products, arithmetic and copies ran while one was open for 0% of the time, Pallas kernels for 0%

commit v1 on v0

--- a/solution.py
+++ b/solution.py
@@ -1,7 +1,13 @@
+import functools
+
 import jax
 import jax.numpy as jnp
 from jax import lax
+from jax.experimental import pallas as pl
+from jax.experimental.pallas import tpu as pltpu
 from jax.sharding import PartitionSpec as P
+
+BLOCK = 256
 
 
 def weighted_pairs(coeffs, band_weights):
@@ -46,18 +52,130 @@
     )
 
 
-def body(matching, vectors, weights, gaunt_index, gaunt_value):
+def product_kernel(blocks, part_ref, matching_hbm, vectors_hbm, out_ref, matching, vectors, matching_sem, sems):
+    start = part_ref[0] * (blocks * BLOCK)
+    first = pltpu.make_async_copy(matching_hbm, matching, matching_sem)
+    first.start()
+    copies = []
+    for at in range(blocks):
+        columns = pl.ds(pl.multiple_of(start + at * BLOCK, BLOCK), BLOCK)
+        copies.append(pltpu.make_async_copy(vectors_hbm.at[:, columns], vectors.at[at], sems.at[at]))
+        copies[-1].start()
+    first.wait()
+    for at in range(blocks):
+        copies[at].wait()
+        out_ref[:, at * BLOCK : (at + 1) * BLOCK] = jnp.dot(
+            matching[...], vectors[at], preferred_element_type=jnp.float32
+        )
+
+
+def product(matching, vectors, part, columns):
+    channels, depth = matching.shape
+    blocks = columns // BLOCK
+    return pl.pallas_call(
+        functools.partial(product_kernel, blocks),
+        out_shape=jax.ShapeDtypeStruct((channels, columns), jnp.float32),
+        in_specs=[
+            pl.BlockSpec(memory_space=pltpu.SMEM),
+            pl.BlockSpec(memory_space=pltpu.HBM),
+            pl.BlockSpec(memory_space=pltpu.HBM),
+        ],
+        out_specs=pl.BlockSpec(memory_space=pltpu.VMEM),
+        scratch_shapes=[
+            pltpu.VMEM((channels, depth), matching.dtype),
+            pltpu.VMEM((blocks, depth, BLOCK), vectors.dtype),
+            pltpu.SemaphoreType.DMA,
+            pltpu.SemaphoreType.DMA((blocks,)),
+        ],
+        compiler_params=pltpu.CompilerParams(vmem_limit_bytes=58 * 2**20),
+        cost_estimate=pl.CostEstimate(
+            flops=2 * channels * depth * columns,
+            bytes_accessed=2 * depth * (columns + channels) + 4 * channels * columns,
+            transcendentals=0,
+        ),
+        name="product",
+    )(part.reshape(1), matching, vectors)
+
+
+def plain_body(matching, vectors, weights, gaunt_index, gaunt_value):
     partial_value = jnp.dot(matching, vectors, preferred_element_type=jnp.float32)
     summed = lax.psum(partial_value, "basis")
     local_terms = weighted_pairs(summed, weights)
     density_matrix = lax.psum(local_terms, "band")
-    density = gaunt_density(density_matrix, gaunt_index, gaunt_value)
-    return (density_matrix, density)
+    return (density_matrix, gaunt_density(density_matrix, gaunt_index, gaunt_value))
+
+
+def halves(block, bit):
+    middle = block.shape[1] // 2
+    low, high = block[:, :middle], block[:, middle:]
+    return jnp.where(bit == 1, low, high), jnp.where(bit == 1, high, low)
+
+
+def body(basis, band, matching, vectors, weights, gaunt_index, gaunt_value):
+    index = lax.axis_index("basis")
+    levels = basis.bit_length() - 1
+    columns = vectors.shape[1]
+    bits = [(index >> level) & 1 for level in range(levels)]
+    own = functools.reduce(jnp.bitwise_xor, bits)
+
+    def exchange(block, mask, band_mask=0):
+        pairs = [
+            (i * band + j, (i ^ mask) * band + (j ^ band_mask))
+            for i in range(basis)
+            for j in range(band)
+        ]
+        return lax.ppermute(block, ("basis", "band"), pairs)
+
+    leaving = product(matching, vectors, 1 - own, columns // 2)
+    arriving = exchange(leaving, 1)
+    staying = product(matching, vectors, own, columns // 2)
+    total = staying + arriving
+    width = columns // 4
+    sent_a, kept_a = halves(total[:, :width], bits[1])
+    sent_b, kept_b = halves(total[:, width:], bits[2])
+    come_a, come_b = exchange(sent_a, 3), exchange(sent_b, 5)
+    sent_a, kept_a = halves(kept_a + come_a, bits[2])
+    sent_b, kept_b = halves(kept_b + come_b, bits[1])
+    come_a, come_b = exchange(sent_a, 5), exchange(sent_b, 3)
+    block = jnp.concatenate([kept_a + come_a, kept_b + come_b], axis=1)
+    width = columns // 16
+    begin = own * (columns // 2)
+    block_weights = jnp.concatenate(
+        [
+            lax.dynamic_slice_in_dim(weights, begin + (2 * bits[1] + bits[2]) * width, width),
+            lax.dynamic_slice_in_dim(weights, begin + columns // 4 + (2 * bits[2] + bits[1]) * width, width),
+        ]
+    )
+    for level in range(3, levels - 1):
+        sent, kept = halves(block, bits[level])
+        block = kept + exchange(sent, 1 | (1 << level))
+        middle = block_weights.shape[0] // 2
+        block_weights = jnp.where(bits[level] == 1, block_weights[middle:], block_weights[:middle])
+    block = block + exchange(block, 1 | (1 << (levels - 1)))
+
+    terms = weighted_pairs(block, block_weights)
+    terms = terms + exchange(terms, 1)
+    step = 1
+    while step < band:
+        terms = terms + exchange(terms, 1, step)
+        step *= 2
+    for level in range(1, levels - 1):
+        terms = terms + exchange(terms, 1 | (1 << level))
+    return (terms, gaunt_density(terms, gaunt_index, gaunt_value))
 
 
 def solution(mesh):
+    basis, band = mesh.shape["basis"], mesh.shape["band"]
+
+    def choose(*arrays):
+        columns = arrays[1].shape[1]
+        powers = basis & (basis - 1) == 0 and band & (band - 1) == 0 and basis >= 16
+        if powers and columns % (2 * BLOCK) == 0 and columns % (16 * 128) == 0:
+            return body(basis, band, *arrays)
+        return plain_body(*arrays)
+
     return jax.shard_map(
-        body,
+        choose,
         mesh=mesh,
         in_specs=(P(None, "basis"), P("basis", "band"), P("band"), P(), P()),
         out_specs=(P(), P()),

time: 151 us -> 66.7 us (0.44)
  waiting for transfers between devices: 118 us -> 35.3 us
  between operations: 14.1 us -> 0.83 us
  Pallas kernels: 0 us -> 11.5 us
  matrix products: 16.8 us -> 5.41 us
  starting transfers between devices: 0.08 us -> 11 us
    psum x2 -> x0, waiting for transfers between devices: 118 us -> none  [the longest x1 97.3 us: body(): summed = lax.psum(partial_value, 'basis')]
    ppermute x0 -> x10, waiting for transfers between devices: none -> 35.3 us  [exchange(): return lax.ppermute(block, ('basis', 'band'), pairs)]
    pallas_call x0 -> x2, Pallas kernels: none -> 11.5 us  [product(): pl.pallas_call(functools.partial(product_kernel, blocks), out_shape=jax.S...]
    ppermute x0 -> x10, starting transfers between devices: none -> 11 us  [exchange(): return lax.ppermute(block, ('basis', 'band'), pairs)]
    dot_general x1 -> x0, matrix products: 7.05 us -> none  [body(): jnp.dot(matching, vectors, preferred_element_type=jnp.float32)]
    dot_general x1, matrix products: 3.78 us -> 0.32 us  [weighted_pairs(): lax.dot_general(scaled, coeffs, (((1,), (1,)), ((), ())), precision=lax.P...]
    unnamed x11 -> x6, local copies, waits for them, and re-layouts: 1.79 us -> 0.02 us
  transfers between devices with their start and end apart: 2 -> 10, of which waited for: 2 -> 9; matrix products, arithmetic and copies ran while one was open for 0% -> 1% of each run, Pallas kernels for 0% -> 9%
where the time goes in v1:
time: 66.7 us; the launch traced here: 66.4 us
  waiting for transfers between devices  35.3 us (53%)
  Pallas kernels  11.5 us (17%)
  starting transfers between devices  11 us (16%)
  matrix products  5.41 us (8%)
  other arithmetic  1.48 us (2%)
  local copies, waits for them, and re-layouts  0.89 us (1%)
  between operations  0.83 us (1%)
    ppermute x10, waiting for transfers between devices, exchange(): return lax.ppermute(block, ('basis', 'band'), pairs)  35.3 us
    pallas_call x2, Pallas kernels, product(): pl.pallas_call(functools.partial(product_kernel, blocks), out_shape=jax.S...  11.5 us
    ppermute x10, starting transfers between devices, exchange(): return lax.ppermute(block, ('basis', 'band'), pairs)  11 us
    dot_general x4, matrix products, gaunt_density(): jnp.dot(block, second_table, precision=lax.Precision.HIGHEST, preferred_e...  3.69 us
    dot_general x1, matrix products, gaunt_density(): lax.dot_general(values, target_table, (((1,), (1,)), ((), ())), precision...  1.39 us
  transfers between devices with their start and end apart: 10, of which 9 were waited for; matrix products, arithmetic and copies ran while one was open for 1% of the time, Pallas kernels for 9%

profile of v1, /device:TPU:0, one launch (start us, length us, event | category | flops | bytes accessed | tf_op | source)
XLA Modules:
  0.0 66.4 jit_solution(14937259514152707473)
XLA Ops:
  0.6 5.8 %product.3 = f32[162,1024]{1,0:T(8,128)} custom-call(s32[1]{0:T(128)} %bitcast.1.part_ref, bf16[162,2560]{1,0:T(8,128)(2,1)} %matching_hbm.3, bf16[2560,2048]{1,0:T(8,128)(2,1)} %vectors_hbm.3), custom_call_target="tpu_custom_call" | custom-call | flops 849346560 | bytes 6735872 | tf_op jit(solution)/shard_map/product/pallas_call | solution.py:75
  6.9 5.7 %product.2 = f32[162,1024]{1,0:T(8,128)} custom-call(s32[1]{0:T(128)} %bitcast.part_ref, bf16[162,2560]{1,0:T(8,128)(2,1)} %matching_hbm.3, bf16[2560,2048]{1,0:T(8,128)(2,1)} %vectors_hbm.3), custom_call_target="tpu_custom_call" | custom-call | flops 849346560 | bytes 6735872 | tf_op jit(solution)/shard_map/product/pallas_call | solution.py:75
  12.7 1.2 %add.51 = f32[162,1024]{1,0:T(8,128)S(1)} add(f32[162,1024]{1,0:T(8,128)} %product.2, f32[162,1024]{1,0:T(8,128)S(1)} %collective-permute-done) | non-fusion elementwise | flops 165888 | bytes 1990656 | tf_op jit(solution)/shard_map/add | solution.py:132
  13.9 2.7 %collective-permute-start.1 = (f32[162,256]{1,0:T(8,128)S(1)}, f32[162,256]{1,0:T(8,128)S(1)}, u32[]{:S(2)}, u32[]{:S(2)}) collective-permute-start(f32[162,256]{1,0:T(8,128)S(1)} %get-tuple-element.4), channel_id=1, source_target_pairs={{0,6},{1,7},{2,4},{3,5},{4,2},{5,3},{6,0},{7,1},{8,14},{9,15},{10,... | collective-permute-start | bytes 497672 | tf_op jit(solution)/shard_map/ppermute | solution.py:127
  16.6 1.2 %collective-permute-start.3 = (f32[162,256]{1,0:T(8,128)S(1)}, f32[162,256]{1,0:T(8,128)S(1)}, u32[]{:S(2)}, u32[]{:S(2)}) collective-permute-start(f32[162,256]{1,0:T(8,128)S(1)} %get-tuple-element.5), channel_id=1, source_target_pairs={{0,10},{1,11},{2,8},{3,9},{4,14},{5,15},{6,12},{7,13},{8,2},{9,3},... | collective-permute-start | bytes 497672 | tf_op jit(solution)/shard_map/ppermute | solution.py:127
  17.8 3.5 %collective-permute-done.1 = f32[162,256]{1,0:T(8,128)S(1)} collective-permute-done((f32[162,256]{1,0:T(8,128)S(1)}, f32[162,256]{1,0:T(8,128)S(1)}, u32[]{:S(2)}, u32[]{:S(2)}) %collective-permute-start.1) | collective-permute-done | bytes 165920 | tf_op jit(solution)/shard_map/ppermute | solution.py:127
  21.3 1.7 %collective-permute-done.3 = f32[162,256]{1,0:T(8,128)S(1)} collective-permute-done((f32[162,256]{1,0:T(8,128)S(1)}, f32[162,256]{1,0:T(8,128)S(1)}, u32[]{:S(2)}, u32[]{:S(2)}) %collective-permute-start.3) | collective-permute-done | bytes 165920 | tf_op jit(solution)/shard_map/ppermute | solution.py:127
  23.1 1.4 %collective-permute-start.2 = (f32[162,128]{1,0:T(8,128)S(1)}, f32[162,128]{1,0:T(8,128)S(1)}, u32[]{:S(2)}, u32[]{:S(2)}) collective-permute-start(f32[162,128]{1,0:T(8,128)S(1)} %slice_select_fusion.3), channel_id=1, source_target_pairs={{0,10},{1,11},{2,8},{3,9},{4,14},{5,15},{6,12},{7,13},{8,2},{9,3},... | collective-permute-start | bytes 248840 | tf_op jit(solution)/shard_map/ppermute | solution.py:127
  24.5 0.6 collective-permute-start.4
  25.2 2.6 %collective-permute-done.2 = f32[162,128]{1,0:T(8,128)S(1)} collective-permute-done((f32[162,128]{1,0:T(8,128)S(1)}, f32[162,128]{1,0:T(8,128)S(1)}, u32[]{:S(2)}, u32[]{:S(2)}) %collective-permute-start.2) | collective-permute-done | bytes 82976 | tf_op jit(solution)/shard_map/ppermute | solution.py:127
  27.8 1.1 %collective-permute-done.4 = f32[162,128]{1,0:T(8,128)S(1)} collective-permute-done((f32[162,128]{1,0:T(8,128)S(1)}, f32[162,128]{1,0:T(8,128)S(1)}, u32[]{:S(2)}, u32[]{:S(2)}) %collective-permute-start.4) | collective-permute-done | bytes 82976 | tf_op jit(solution)/shard_map/ppermute | solution.py:127
  28.9 2.6 %collective-permute-start.5 = (f32[162,256]{1,0:T(8,128)S(1)}, f32[162,256]{1,0:T(8,128)S(1)}, u32[]{:S(2)}, u32[]{:S(2)}) collective-permute-start(f32[162,256]{1,0:T(8,128)S(1)} %pad_maximum_fusion), channel_id=1, source_target_pairs={{0,18},{1,19},{2,16},{3,17},{4,22},{5,23},{6,20},{7,21},{8,26},{9,... | collective-permute-start | bytes 497672 | tf_op jit(solution)/shard_map/ppermute | solution.py:127
  31.5 0.8 %fusion.28 = (f32[128]{0:T(128)S(1)}, f32[128]{0:T(128)S(1)}) fusion(f32[2048]{0:T(1024)} %param.7, s32[]{:T(128)S(6)} %select_n.62, s32[]{:T(128)S(6)} %select_n.63), kind=kLoop, calls=%fused_computation.45 | loop fusion | bytes 2056 | tf_op jit(solution)/shard_map/dynamic_slice | solution.py:145
  32.4 7.7 %collective-permute-done.5 = f32[162,256]{1,0:T(8,128)S(1)} collective-permute-done((f32[162,256]{1,0:T(8,128)S(1)}, f32[162,256]{1,0:T(8,128)S(1)}, u32[]{:S(2)}, u32[]{:S(2)}) %collective-permute-start.5) | collective-permute-done | bytes 165920 | tf_op jit(solution)/shard_map/ppermute | solution.py:127
  40.6 1.3 %collective-permute-done.6 = f32[162,162]{1,0:T(8,128)S(1)} collective-permute-done((f32[162,162]{1,0:T(8,128)S(1)}, f32[162,162]{1,0:T(8,128)S(1)}, u32[]{:S(2)}, u32[]{:S(2)}) %collective-permute-start.6) | collective-permute-done | bytes 105008 | tf_op jit(solution)/shard_map/ppermute | solution.py:127
  41.9 1.3 %collective-permute-start.7 = (f32[162,162]{1,0:T(8,128)S(1)}, f32[162,162]{1,0:T(8,128)S(1)}, u32[]{:S(2)}, u32[]{:S(2)}) collective-permute-start(f32[162,162]{1,0:T(8,128)S(1)} %add.64), channel_id=1, source_target_pairs={{0,3},{1,2},{2,1},{3,0},{4,7},{5,6},{6,5},{7,4},{8,11},{9,10},{10,... | collective-permute-start | bytes 314936 | tf_op jit(solution)/shard_map/ppermute | solution.py:127
  43.3 5.1 %collective-permute-done.7 = f32[162,162]{1,0:T(8,128)S(1)} collective-permute-done((f32[162,162]{1,0:T(8,128)S(1)}, f32[162,162]{1,0:T(8,128)S(1)}, u32[]{:S(2)}, u32[]{:S(2)}) %collective-permute-start.7) | collective-permute-done | bytes 105008 | tf_op jit(solution)/shard_map/ppermute | solution.py:127
  48.8 6.0 %collective-permute-done.8 = f32[162,162]{1,0:T(8,128)S(1)} collective-permute-done((f32[162,162]{1,0:T(8,128)S(1)}, f32[162,162]{1,0:T(8,128)S(1)}, u32[]{:S(2)}, u32[]{:S(2)}) %collective-permute-start.8) | collective-permute-done | bytes 105008 | tf_op jit(solution)/shard_map/ppermute | solution.py:127
  55.0 6.3 %collective-permute-done.9 = f32[162,162]{1,0:T(8,128)S(1)} collective-permute-done((f32[162,162]{1,0:T(8,128)S(1)}, f32[162,162]{1,0:T(8,128)S(1)}, u32[]{:S(2)}, u32[]{:S(2)}) %collective-permute-start.9) | collective-permute-done | bytes 105008 | tf_op jit(solution)/shard_map/ppermute | solution.py:127
  61.3 0.9 %fusion.3 = f32[4096]{0:T(1024)S(1)} fusion(s32[4096]{0:T(1024)S(1)} %bitcast.18, s32[4096]{0:T(1024)S(1)} %bitcast.14, f32[162,162]{1,0:T(8,128)S(1)} %add.67), kind=kOutput, calls=%fused_computation.10 | convolution fusion | flops 323809280 | bytes 94208 | tf_op jit(solution)/shard_map/dot_general | solution.py:37
  62.2 0.9 %fusion.4 = f32[4096]{0:T(1024)S(1)} fusion(s32[4096]{0:T(1024)S(1)} %bitcast.19, s32[4096]{0:T(1024)S(1)} %bitcast.15, f32[162,162]{1,0:T(8,128)S(1)} %add.67), kind=kOutput, calls=%fused_computation.11 | convolution fusion | flops 323809280 | bytes 94208 | tf_op jit(solution)/shard_map/dot_general | solution.py:37
  63.2 0.9 %fusion.2 = f32[4096]{0:T(1024)S(1)} fusion(s32[4096]{0:T(1024)S(1)} %bitcast.20, s32[4096]{0:T(1024)S(1)} %bitcast.16, f32[162,162]{1,0:T(8,128)S(1)} %add.67), kind=kOutput, calls=%fused_computation.9 | convolution fusion | flops 323809280 | bytes 94208 | tf_op jit(solution)/shard_map/dot_general | solution.py:37
  64.1 0.9 %fusion.1 = f32[4096]{0:T(1024)S(1)} fusion(s32[4096]{0:T(1024)S(1)} %bitcast.21, s32[4096]{0:T(1024)S(1)} %bitcast.17, f32[162,162]{1,0:T(8,128)S(1)} %add.67), kind=kOutput, calls=%fused_computation.8 | convolution fusion | flops 323809280 | bytes 94208 | tf_op jit(solution)/shard_map/dot_general | solution.py:37
  65.1 1.4 %fusion = f32[4,81]{1,0:T(4,128)} fusion(s32[4096]{0:T(1024)S(1)} %bitcast.13, f32[1,4096]{1,0:T(1,128)S(1)} %bitcast.11, f32[1,4096]{1,0:T(1,128)S(1)} %bitcast.12, f32[1,4096]{1,0:T(1,128)S(1)} %bitcast.10, f32[1,4096]{1,0:T(1,128)S(1)} %bitcast.9), kind=kOutput, calls=%fused_computation.7 | convolution fusion | flops 16306176 | bytes 83216 | tf_op jit(solution)/shard_map/dot_general | solution.py:46
  (26 shorter events, 1.9 us)
Async XLA Ops:
  6.4 6.3 %collective-permute-start = (f32[162,1024]{1,0:T(8,128)}, f32[162,1024]{1,0:T(8,128)S(1)}, u32[]{:S(2)}, u32[]{:S(2)}) collective-permute-start(f32[162,1024]{1,0:T(8,128)} %product.3), channel_id=1, source_target_pairs={{0,2},{1,3},{2,0},{3,1},{4,6},{5,7},{6,4},{7,5},{8,10},{9,11},{10,... | collective-permute-start | bytes 1990664 | tf_op jit(solution)/shard_map/ppermute | solution.py:127
  13.9 7.4 %collective-permute-start.1 = (f32[162,256]{1,0:T(8,128)S(1)}, f32[162,256]{1,0:T(8,128)S(1)}, u32[]{:S(2)}, u32[]{:S(2)}) collective-permute-start(f32[162,256]{1,0:T(8,128)S(1)} %get-tuple-element.4), channel_id=1, source_target_pairs={{0,6},{1,7},{2,4},{3,5},{4,2},{5,3},{6,0},{7,1},{8,14},{9,15},{10,... | collective-permute-start | bytes 497672 | tf_op jit(solution)/shard_map/ppermute | solution.py:127
  16.6 6.5 %collective-permute-start.3 = (f32[162,256]{1,0:T(8,128)S(1)}, f32[162,256]{1,0:T(8,128)S(1)}, u32[]{:S(2)}, u32[]{:S(2)}) collective-permute-start(f32[162,256]{1,0:T(8,128)S(1)} %get-tuple-element.5), channel_id=1, source_target_pairs={{0,10},{1,11},{2,8},{3,9},{4,14},{5,15},{6,12},{7,13},{8,2},{9,3},... | collective-permute-start | bytes 497672 | tf_op jit(solution)/shard_map/ppermute | solution.py:127
  23.1 4.6 %collective-permute-start.2 = (f32[162,128]{1,0:T(8,128)S(1)}, f32[162,128]{1,0:T(8,128)S(1)}, u32[]{:S(2)}, u32[]{:S(2)}) collective-permute-start(f32[162,128]{1,0:T(8,128)S(1)} %slice_select_fusion.3), channel_id=1, source_target_pairs={{0,10},{1,11},{2,8},{3,9},{4,14},{5,15},{6,12},{7,13},{8,2},{9,3},... | collective-permute-start | bytes 248840 | tf_op jit(solution)/shard_map/ppermute | solution.py:127
  24.5 4.3 %collective-permute-start.4 = (f32[162,128]{1,0:T(8,128)S(1)}, f32[162,128]{1,0:T(8,128)S(1)}, u32[]{:S(2)}, u32[]{:S(2)}) collective-permute-start(f32[162,128]{1,0:T(8,128)S(1)} %slice_select_fusion.2), channel_id=1, source_target_pairs={{0,6},{1,7},{2,4},{3,5},{4,2},{5,3},{6,0},{7,1},{8,14},{9,15},{10,... | collective-permute-start | bytes 248840 | tf_op jit(solution)/shard_map/ppermute | solution.py:127
  28.9 26.0 %copy-start.1 = (s32[3,4096]{1,0:T(4,128)S(1)}, s32[3,4096]{1,0:T(4,128)}, u32[]{:S(2)}) copy-start(s32[3,4096]{1,0:T(4,128)} %param.8) | copy-start | bytes 147460
  28.9 11.2 %collective-permute-start.5 = (f32[162,256]{1,0:T(8,128)S(1)}, f32[162,256]{1,0:T(8,128)S(1)}, u32[]{:S(2)}, u32[]{:S(2)}) collective-permute-start(f32[162,256]{1,0:T(8,128)S(1)} %pad_maximum_fusion), channel_id=1, source_target_pairs={{0,18},{1,19},{2,16},{3,17},{4,22},{5,23},{6,20},{7,21},{8,26},{9,... | collective-permute-start | bytes 497672 | tf_op jit(solution)/shard_map/ppermute | solution.py:127
  40.5 1.5 %collective-permute-start.6 = (f32[162,162]{1,0:T(8,128)S(1)}, f32[162,162]{1,0:T(8,128)S(1)}, u32[]{:S(2)}, u32[]{:S(2)}) collective-permute-start(f32[162,162]{1,0:T(8,128)S(1)} %fusion.10), channel_id=1, source_target_pairs={{0,2},{1,3},{2,0},{3,1},{4,6},{5,7},{6,4},{7,5},{8,10},{9,11},{10,... | collective-permute-start | bytes 314936 | tf_op jit(solution)/shard_map/ppermute | solution.py:127
  41.9 6.4 %collective-permute-start.7 = (f32[162,162]{1,0:T(8,128)S(1)}, f32[162,162]{1,0:T(8,128)S(1)}, u32[]{:S(2)}, u32[]{:S(2)}) collective-permute-start(f32[162,162]{1,0:T(8,128)S(1)} %add.64), channel_id=1, source_target_pairs={{0,3},{1,2},{2,1},{3,0},{4,7},{5,6},{6,5},{7,4},{8,11},{9,10},{10,... | collective-permute-start | bytes 314936 | tf_op jit(solution)/shard_map/ppermute | solution.py:127
  48.4 6.4 %collective-permute-start.8 = (f32[162,162]{1,0:T(8,128)S(1)}, f32[162,162]{1,0:T(8,128)S(1)}, u32[]{:S(2)}, u32[]{:S(2)}) collective-permute-start(f32[162,162]{1,0:T(8,128)S(1)} %add.65), channel_id=1, source_target_pairs={{0,6},{1,7},{2,4},{3,5},{4,2},{5,3},{6,0},{7,1},{8,14},{9,15},{10,... | collective-permute-start | bytes 314936 | tf_op jit(solution)/shard_map/ppermute | solution.py:127
  54.8 6.4 %collective-permute-start.9 = (f32[162,162]{1,0:T(8,128)S(1)}, f32[162,162]{1,0:T(8,128)S(1)}, u32[]{:S(2)}, u32[]{:S(2)}) collective-permute-start(f32[162,162]{1,0:T(8,128)S(1)} %add.66), channel_id=1, source_target_pairs={{0,10},{1,11},{2,8},{3,9},{4,14},{5,15},{6,12},{7,13},{8,2},{9,3},... | collective-permute-start | bytes 314936 | tf_op jit(solution)/shard_map/ppermute | solution.py:127
  61.3 2.8 %copy-start = (f32[162,162]{1,0:T(8,128)}, f32[162,162]{1,0:T(8,128)S(1)}, u32[]{:S(2)}) copy-start(f32[162,162]{1,0:T(8,128)S(1)} %add.67) | copy-start | bytes 314932
  63.2 1.9 %copy-start.2 = (f32[4096]{0:T(1024)S(1)}, f32[4096]{0:T(1024)}, u32[]{:S(2)}) copy-start(f32[4096]{0:T(1024)} %param.9) | copy-start | bytes 49156

commit v2 on v1

--- a/solution.py
+++ b/solution.py
@@ -7,7 +7,8 @@
 from jax.experimental.pallas import tpu as pltpu
 from jax.sharding import PartitionSpec as P
 
-BLOCK = 256
+LANES = 128
+VMEM_LIMIT = 55 * 2**20
 
 
 def weighted_pairs(coeffs, band_weights):
@@ -52,49 +53,218 @@
     )
 
 
-def product_kernel(blocks, part_ref, matching_hbm, vectors_hbm, out_ref, matching, vectors, matching_sem, sems):
-    start = part_ref[0] * (blocks * BLOCK)
-    first = pltpu.make_async_copy(matching_hbm, matching, matching_sem)
+def split_columns(ref, part, columns):
+    return ref.at[:, pl.ds(pl.multiple_of(part * columns, 128), columns)]
+
+
+def leaving_kernel(columns, part_ref, matching_hbm, vectors_hbm, out_ref, matching, ahead, vectors, sems):
+    depth = vectors.shape[0]
+    middle = depth // 2
+    mine = split_columns(vectors_hbm, part_ref[0], columns)
+    other = split_columns(vectors_hbm, 1 - part_ref[0], columns)
+    first = pltpu.make_async_copy(matching_hbm, matching, sems.at[0])
+    upper = pltpu.make_async_copy(mine.at[:middle], vectors.at[:middle], sems.at[1])
+    lower = pltpu.make_async_copy(mine.at[middle:], vectors.at[middle:], sems.at[2])
+    later = pltpu.make_async_copy(other.at[:middle], ahead, sems.at[3])
     first.start()
-    copies = []
-    for at in range(blocks):
-        columns = pl.ds(pl.multiple_of(start + at * BLOCK, BLOCK), BLOCK)
-        copies.append(pltpu.make_async_copy(vectors_hbm.at[:, columns], vectors.at[at], sems.at[at]))
-        copies[-1].start()
+    upper.start()
+    lower.start()
+    later.start()
     first.wait()
-    for at in range(blocks):
-        copies[at].wait()
-        out_ref[:, at * BLOCK : (at + 1) * BLOCK] = jnp.dot(
-            matching[...], vectors[at], preferred_element_type=jnp.float32
+    upper.wait()
+    out_ref[...] = jnp.dot(matching[:, :middle], vectors[:middle], preferred_element_type=jnp.float32)
+    lower.wait()
+    out_ref[...] += jnp.dot(matching[:, middle:], vectors[middle:], preferred_element_type=jnp.float32)
+    later.wait()
+
+
+def staying_kernel(columns, part_ref, matching, ahead, vectors_hbm, out_ref, vectors, sem):
+    middle = ahead.shape[0]
+    mine = split_columns(vectors_hbm, part_ref[0], columns)
+    lower = pltpu.make_async_copy(mine.at[middle:], vectors, sem)
+    lower.start()
+    out_ref[...] = jnp.dot(matching[:, :middle], ahead[...], preferred_element_type=jnp.float32)
+    lower.wait()
+    out_ref[...] += jnp.dot(matching[:, middle:], vectors[...], preferred_element_type=jnp.float32)
+
+
+VMEM = pl.BlockSpec(memory_space=pltpu.VMEM)
+SMEM = pl.BlockSpec(memory_space=pltpu.SMEM)
+HBM = pl.BlockSpec(memory_space=pltpu.HBM)
+
+
+def cost(channels, depth, columns):
+    return pl.CostEstimate(
+        flops=2 * channels * depth * columns,
+        bytes_accessed=2 * depth * (columns + channels) + 4 * channels * columns,
+        transcendentals=0,
+    )
+
+
+def leaving_product(matching, vectors, part, columns):
+    channels, depth = matching.shape
+    return pl.pallas_call(
+        functools.partial(leaving_kernel, columns),
+        out_shape=(
+            jax.ShapeDtypeStruct((channels, columns), jnp.float32),
+            jax.ShapeDtypeStruct(matching.shape, matching.dtype),
+            jax.ShapeDtypeStruct((depth // 2, columns), vectors.dtype),
+        ),
+        in_specs=[SMEM, HBM, HBM],
+        out_specs=(VMEM, VMEM, VMEM),
+        scratch_shapes=[
+            pltpu.VMEM((depth, columns), vectors.dtype),
+            pltpu.SemaphoreType.DMA((4,)),
+        ],
+        compiler_params=pltpu.CompilerParams(vmem_limit_bytes=VMEM_LIMIT),
+        cost_estimate=cost(channels, depth, columns),
+        name="leaving_product",
+    )(part.reshape(1), matching, vectors)
+
+
+def staying_product(matching, ahead, vectors, part, columns):
+    channels, depth = matching.shape
+    return pl.pallas_call(
+        functools.partial(staying_kernel, columns),
+        out_shape=jax.ShapeDtypeStruct((channels, columns), jnp.float32),
+        in_specs=[SMEM, VMEM, VMEM, HBM],
+        out_specs=VMEM,
+        scratch_shapes=[
+            pltpu.VMEM((depth - depth // 2, columns), vectors.dtype),
+            pltpu.SemaphoreType.DMA,
+        ],
+        compiler_params=pltpu.CompilerParams(vmem_limit_bytes=VMEM_LIMIT),
+        cost_estimate=cost(channels, depth, columns),
+        name="staying_product",
+    )(part.reshape(1), matching, ahead, vectors)
+
+
+def tables_kernel(harmonics, index_ref, value_ref, second_ref, first_ref, target_ref):
+    entries = index_ref.shape[1]
+    wide = second_ref.shape[0]
+    rows = lax.broadcasted_iota(jnp.int32, (wide, entries), 0)
+    spot = index_ref[1:2, :]
+    hit = (rows == spot) | (rows == spot + harmonics) | (rows == spot + 2 * harmonics)
+    second_ref[...] = jnp.where(hit, 1.0, 0.0).astype(jnp.bfloat16)
+    rows = lax.broadcasted_iota(jnp.int32, (first_ref.shape[0], entries), 0)
+    first_ref[...] = jnp.where(rows == index_ref[0:1, :], value_ref[...], 0.0)
+    rows = lax.broadcasted_iota(jnp.int32, (target_ref.shape[0], entries), 0)
+    target_ref[...] = jnp.where(rows == index_ref[2:3, :], 1.0, 0.0).astype(jnp.bfloat16)
+
+
+def round_up(value, unit):
+    return -(-value // unit) * unit
+
+
+def gaunt_tables(gaunt_index, gaunt_value, harmonics):
+    entries = gaunt_value.shape[0]
+    rows = round_up(harmonics, 8)
+    wide = round_up(3 * harmonics, 128)
+    shapes = (
+        jax.ShapeDtypeStruct((wide, entries), jnp.bfloat16),
+        jax.ShapeDtypeStruct((rows, entries), jnp.float32),
+        jax.ShapeDtypeStruct((round_up(harmonics, 128), entries), jnp.bfloat16),
+    )
+    return pl.pallas_call(
+        functools.partial(tables_kernel, harmonics),
+        out_shape=shapes,
+        in_specs=[VMEM, VMEM],
+        out_specs=(VMEM, VMEM, VMEM),
+        compiler_params=pltpu.CompilerParams(vmem_limit_bytes=32 * 2**20),
+        cost_estimate=pl.CostEstimate(flops=8 * 2**20, bytes_accessed=5 * 2**20, transcendentals=0),
+        name="gaunt_tables",
+    )(gaunt_index, gaunt_value.reshape(1, entries))
+
+
+def thirds(value):
+    high = value.astype(jnp.bfloat16)
+    rest = value - high.astype(jnp.float32)
+    middle = rest.astype(jnp.bfloat16)
+    return high, middle, (rest - middle.astype(jnp.float32)).astype(jnp.bfloat16)
+
+
+def finish_kernel(tile, top_ref, bottom_ref, second_ref, first_ref, target_ref, matrix_ref, density_ref, left, values):
+    channels = matrix_ref.shape[0]
+    harmonics = channels // 2
+    extra = channels - LANES
+    half = top_ref.shape[0]
+    upper = jnp.concatenate([top_ref[...], bottom_ref[: LANES - half, :]], axis=0)
+    lower = bottom_ref[LANES - half : LANES - half + extra, :]
+    rows = lax.broadcasted_iota(jnp.int32, (LANES, LANES), 0)
+    lanes = lax.broadcasted_iota(jnp.int32, (LANES, LANES), 1)
+    corner_there = (rows < extra) & (lanes >= LANES // 2) & (lanes < LANES // 2 + extra)
+    main = jnp.where(corner_there, jnp.transpose(upper), upper)
+    corner = pltpu.roll(upper, LANES // 2, 1)
+    matrix_ref[:LANES, :LANES] = main
+    matrix_ref[LANES:, :LANES] = lower
+    side = bottom_ref.shape[0] - (LANES - half)
+    tall = jnp.concatenate(
+        [bottom_ref[LANES - half :, :], jnp.zeros((LANES - side, LANES), jnp.float32)], axis=0
+    )
+    matrix_ref[:LANES, LANES:] = jnp.transpose(tall)[:, :extra]
+    matrix_ref[LANES:, LANES:] = corner[:extra, :extra]
+
+    rows_in = first_ref.shape[0]
+    left[...] = jnp.zeros_like(left)
+    for radial in range(2):
+        for other in range(2):
+            block = matrix_ref[
+                radial * harmonics : (radial + 1) * harmonics, other * harmonics : (other + 1) * harmonics
+            ]
+            at = (2 * radial + other) * rows_in
+            for part, piece in enumerate(thirds(block)):
+                left[at : at + harmonics, part * harmonics : (part + 1) * harmonics] = piece.astype(jnp.float32)
+    stacked = left[...].astype(jnp.bfloat16)
+    values[...] = jnp.zeros_like(values)
+    entries = second_ref.shape[1]
+    for start in range(0, entries, tile):
+        columns = slice(start, start + tile)
+        spread = jnp.dot(stacked, second_ref[:, columns], preferred_element_type=jnp.float32)
+        for pair in range(4):
+            chosen = spread[pair * rows_in : (pair + 1) * rows_in, :] * first_ref[:, columns]
+            values[pair : pair + 1, columns] = jnp.sum(chosen, axis=0, keepdims=True)
+    total = jnp.zeros((8, target_ref.shape[0]), jnp.float32)
+    for piece in thirds(values[...]):
+        total = total + lax.dot_general(
+            piece, target_ref[...], (((1,), (1,)), ((), ())), preferred_element_type=jnp.float32
         )
-
-
-def product(matching, vectors, part, columns):
-    channels, depth = matching.shape
-    blocks = columns // BLOCK
+    density_ref[...] = total[:4, :harmonics]
+
+
+def finish(top, bottom, tables, channels):
+    second, first, target = tables
+    entries = second.shape[1]
+    harmonics = channels // 2
+    tile = 512 if entries % 512 == 0 else entries
     return pl.pallas_call(
-        functools.partial(product_kernel, blocks),
-        out_shape=jax.ShapeDtypeStruct((channels, columns), jnp.float32),
-        in_specs=[
-            pl.BlockSpec(memory_space=pltpu.SMEM),
-            pl.BlockSpec(memory_space=pltpu.HBM),
-            pl.BlockSpec(memory_space=pltpu.HBM),
+        functools.partial(finish_kernel, tile),
+        out_shape=(
+            jax.ShapeDtypeStruct((channels, channels), jnp.float32),
+            jax.ShapeDtypeStruct((4, harmonics), jnp.float32),
+        ),
+        in_specs=[VMEM] * 5,
+        out_specs=(VMEM, VMEM),
+        scratch_shapes=[
+            pltpu.VMEM((4 * first.shape[0], second.shape[0]), jnp.float32),
+            pltpu.VMEM((8, entries), jnp.float32),
         ],
-        out_specs=pl.BlockSpec(memory_space=pltpu.VMEM),
-        scratch_shapes=[
-            pltpu.VMEM((channels, depth), matching.dtype),
-            pltpu.VMEM((blocks, depth, BLOCK), vectors.dtype),
-            pltpu.SemaphoreType.DMA,
-            pltpu.SemaphoreType.DMA((blocks,)),
-        ],
-        compiler_params=pltpu.CompilerParams(vmem_limit_bytes=58 * 2**20),
-        cost_estimate=pl.CostEstimate(
-            flops=2 * channels * depth * columns,
-            bytes_accessed=2 * depth * (columns + channels) + 4 * channels * columns,
-            transcendentals=0,
-        ),
-        name="product",
-    )(part.reshape(1), matching, vectors)
+        compiler_params=pltpu.CompilerParams(vmem_limit_bytes=32 * 2**20),
+        name="finish",
+    )(top, bottom, second, first, target)
+
+
+def pack(matrix):
+    channels = matrix.shape[0]
+    extra = channels - LANES
+    half = LANES // 2
+    corner = jnp.pad(matrix[LANES:, LANES:], ((0, channels - extra), (half, LANES - half - extra)))
+    rows = lax.broadcasted_iota(jnp.int32, (channels, LANES), 0)
+    lanes = lax.broadcasted_iota(jnp.int32, (channels, LANES), 1)
+    there = (rows < extra) & (lanes >= half) & (lanes < half + extra)
+    packed = jnp.where(there, corner, matrix[:, :LANES])
+    height = round_up(channels, 16) // 2
+    height = round_up(height, 8)
+    return packed[:height], jnp.pad(packed[height:], ((0, 2 * height - channels), (0, 0)))
 
 
 def plain_body(matching, vectors, weights, gaunt_index, gaunt_value):
@@ -114,7 +284,7 @@
 def body(basis, band, matching, vectors, weights, gaunt_index, gaunt_value):
     index = lax.axis_index("basis")
     levels = basis.bit_length() - 1
-    columns = vectors.shape[1]
+    channels, columns = matching.shape[0], vectors.shape[1]
     bits = [(index >> level) & 1 for level in range(levels)]
     own = functools.reduce(jnp.bitwise_xor, bits)
 
@@ -126,9 +296,9 @@
         ]
         return lax.ppermute(block, ("basis", "band"), pairs)
 
-    leaving = product(matching, vectors, 1 - own, columns // 2)
+    leaving, matching, ahead = leaving_product(matching, vectors, 1 - own, columns // 2)
     arriving = exchange(leaving, 1)
-    staying = product(matching, vectors, own, columns // 2)
+    staying = staying_product(matching, ahead, vectors, own, columns // 2)
     total = staying + arriving
     width = columns // 4
     sent_a, kept_a = halves(total[:, :width], bits[1])
@@ -151,26 +321,37 @@
         block = kept + exchange(sent, 1 | (1 << level))
         middle = block_weights.shape[0] // 2
         block_weights = jnp.where(bits[level] == 1, block_weights[middle:], block_weights[:middle])
-    block = block + exchange(block, 1 | (1 << (levels - 1)))
-
-    terms = weighted_pairs(block, block_weights)
-    terms = terms + exchange(terms, 1)
+    tied = lax.optimization_barrier((block, gaunt_index, gaunt_value))
+    tables = gaunt_tables(tied[1], tied[2], channels // 2)
+    block = block + exchange(tied[0], 1 | (1 << (levels - 1)))
+
+    top, bottom = pack(weighted_pairs(block, block_weights))
+    which = own
+    for level in range(band.bit_length() - 1):
+        which = which ^ ((lax.axis_index("band") >> level) & 1)
+    sent = jnp.where(which == 1, top, bottom)
+    terms = jnp.where(which == 1, bottom, top) + exchange(sent, 1)
     step = 1
     while step < band:
         terms = terms + exchange(terms, 1, step)
         step *= 2
     for level in range(1, levels - 1):
         terms = terms + exchange(terms, 1 | (1 << level))
-    return (terms, gaunt_density(terms, gaunt_index, gaunt_value))
+    other = exchange(terms, 1)
+    top = jnp.where(which == 1, other, terms)
+    bottom = jnp.where(which == 1, terms, other)
+    return finish(top, bottom, tables, channels)
 
 
 def solution(mesh):
     basis, band = mesh.shape["basis"], mesh.shape["band"]
 
     def choose(*arrays):
+        channels, depth = arrays[0].shape
         columns = arrays[1].shape[1]
         powers = basis & (basis - 1) == 0 and band & (band - 1) == 0 and basis >= 16
-        if powers and columns % (2 * BLOCK) == 0 and columns % (16 * 128) == 0:
+        sizes = columns % (16 * LANES) == 0 and depth % 256 == 0
+        if powers and sizes and channels % 2 == 0 and LANES < channels <= LANES + LANES // 2:
             return body(basis, band, *arrays)
         return plain_body(*arrays)
 

time: 66.7 us -> 56.9 us (0.85)
  waiting for transfers between devices: 35.3 us -> 24.6 us
  matrix products: 5.41 us -> 0.33 us
  Pallas kernels: 11.5 us -> 16.1 us
  starting transfers between devices: 11 us -> 12.5 us
    ppermute x10 -> x11, waiting for transfers between devices: 35.3 us -> 24.6 us  [exchange(): return lax.ppermute(block, ('basis', 'band'), pairs)]
    dot_general x5 -> x0, matrix products: 5.09 us -> none  [the longest x4 3.69 us: gaunt_density(): jnp.dot(block, second_table, precision=lax.Precision.HIGHEST, preferred_e...]
    pallas_call x2 -> x4, Pallas kernels: 11.5 us -> 16.1 us  [the longest x1 5.57 us: leaving_product(): pl.pallas_call(functools.partial(leaving_kernel, columns), out_shape=(jax...]
    ppermute x10 -> x11, starting transfers between devices: 11 us -> 12.5 us  [exchange(): return lax.ppermute(block, ('basis', 'band'), pairs)]
  transfers between devices with their start and end apart: 10 -> 11, of which waited for: 9 -> 9; matrix products, arithmetic and copies ran while one was open for 1% -> 2% of each run, Pallas kernels for 9% -> 12%
where the time goes in v2:
time: 56.9 us; the launch traced here: 56.7 us
  waiting for transfers between devices  24.6 us (43%)
  Pallas kernels  16.1 us (28%)
  starting transfers between devices  12.5 us (22%)
  other arithmetic  1.53 us (3%)
  local copies, waits for them, and re-layouts  0.86 us (2%)
  between operations  0.81 us (1%)
    ppermute x11, waiting for transfers between devices, exchange(): return lax.ppermute(block, ('basis', 'band'), pairs)  24.6 us
    ppermute x11, starting transfers between devices, exchange(): return lax.ppermute(block, ('basis', 'band'), pairs)  12.5 us
    pallas_call x1, Pallas kernels, leaving_product(): pl.pallas_call(functools.partial(leaving_kernel, columns), out_shape=(jax...  5.57 us
    pallas_call x1, Pallas kernels, staying_product(): pl.pallas_call(functools.partial(staying_kernel, columns), out_shape=jax....  5.27 us
    pallas_call x1, Pallas kernels, finish(): pl.pallas_call(functools.partial(finish_kernel, tile), out_shape=(jax.Sha...  3.7 us
    pallas_call x1, Pallas kernels, gaunt_tables(): pl.pallas_call(functools.partial(tables_kernel, harmonics), out_shape=sha...  1.53 us
    add x1, other arithmetic, body(): total = staying + arriving  1.19 us
  transfers between devices with their start and end apart: 11, of which 9 were waited for; matrix products, arithmetic and copies ran while one was open for 2% of the time, Pallas kernels for 12%

profile of v2, /device:TPU:0, one launch (start us, length us, event | category | flops | bytes accessed | tf_op | source)
XLA Modules:
  0.0 56.7 jit_solution(8062233567575858958)
XLA Ops:
  0.6 5.6 %leaving_product.1 = (f32[162,1024]{1,0:T(8,128)}, bf16[162,2560]{1,0:T(8,128)(2,1)}, bf16[1280,1024]{1,0:T(8,128)(2,1)}) custom-call(s32[1]{0:T(128)} %bitcast.1.part_ref, bf16[162,2560]{1,0:T(8,128)(2,1)} %matching_hbm.1, bf16[2560,2048]{1,0:T(8,128)(2,1)} %vectors_hbm.3), custom_call_target="tpu_custom_call" | custom-call | flops 849346560 | bytes 6735872 | tf_op jit(solution)/shard_map/leaving_product/pallas_call | solution.py:106
  6.2 0.5 collective-permute-start
  6.7 5.3 %staying_product.1 = f32[162,1024]{1,0:T(8,128)} custom-call(s32[1]{0:T(128)} %bitcast.part_ref, bf16[162,2560]{1,0:T(8,128)(2,1)} %get-tuple-element.11.matching, bf16[1280,1024]{1,0:T(8,128)(2,1)} %get-tuple-element.12.ahead, bf16[2560,2048]{1,0:T(8,128)(2,1)} %vectors_hbm.3), custom_call_target="tpu_custom_call" | custom-call | flops 849346560 | bytes 6735872 | tf_op jit(solution)/shard_map/staying_product/pallas_call | solution.py:127
  12.0 1.2 %add.55 = f32[162,1024]{1,0:T(8,128)S(1)} add(f32[162,1024]{1,0:T(8,128)} %staying_product.1, f32[162,1024]{1,0:T(8,128)S(1)} %collective-permute-done) | non-fusion elementwise | flops 165888 | bytes 1990656 | tf_op jit(solution)/shard_map/add | solution.py:302
  13.3 2.7 %collective-permute-start.1 = (f32[162,256]{1,0:T(8,128)S(1)}, f32[162,256]{1,0:T(8,128)S(1)}, u32[]{:S(2)}, u32[]{:S(2)}) collective-permute-start(f32[162,256]{1,0:T(8,128)S(1)} %get-tuple-element.22), channel_id=1, source_target_pairs={{0,6},{1,7},{2,4},{3,5},{4,2},{5,3},{6,0},{7,1},{8,14},{9,15},{10,... | collective-permute-start | bytes 497672 | tf_op jit(solution)/shard_map/ppermute | solution.py:297
  16.0 1.2 %collective-permute-start.3 = (f32[162,256]{1,0:T(8,128)S(1)}, f32[162,256]{1,0:T(8,128)S(1)}, u32[]{:S(2)}, u32[]{:S(2)}) collective-permute-start(f32[162,256]{1,0:T(8,128)S(1)} %get-tuple-element.23), channel_id=1, source_target_pairs={{0,10},{1,11},{2,8},{3,9},{4,14},{5,15},{6,12},{7,13},{8,2},{9,3},... | collective-permute-start | bytes 497672 | tf_op jit(solution)/shard_map/ppermute | solution.py:297
  17.2 0.8 %fusion.4 = (f32[128]{0:T(128)S(1)}, f32[128]{0:T(128)S(1)}) fusion(f32[2048]{0:T(1024)} %param.7, s32[]{:T(128)S(6)} %select_n.87, s32[]{:T(128)S(6)} %select_n.88), kind=kLoop, calls=%fused_computation.22 | loop fusion | bytes 2056 | tf_op jit(solution)/shard_map/dynamic_slice | solution.py:315
  18.0 2.7 %collective-permute-done.1 = f32[162,256]{1,0:T(8,128)S(1)} collective-permute-done((f32[162,256]{1,0:T(8,128)S(1)}, f32[162,256]{1,0:T(8,128)S(1)}, u32[]{:S(2)}, u32[]{:S(2)}) %collective-permute-start.1) | collective-permute-done | bytes 165920 | tf_op jit(solution)/shard_map/ppermute | solution.py:297
  20.7 1.7 %collective-permute-done.3 = f32[162,256]{1,0:T(8,128)S(1)} collective-permute-done((f32[162,256]{1,0:T(8,128)S(1)}, f32[162,256]{1,0:T(8,128)S(1)}, u32[]{:S(2)}, u32[]{:S(2)}) %collective-permute-start.3) | collective-permute-done | bytes 165920 | tf_op jit(solution)/shard_map/ppermute | solution.py:297
  22.6 1.9 %collective-permute-start.2 = (f32[162,128]{1,0:T(8,128)S(1)}, f32[162,128]{1,0:T(8,128)S(1)}, u32[]{:S(2)}, u32[]{:S(2)}) collective-permute-start(f32[162,128]{1,0:T(8,128)S(1)} %slice_select_fusion.4), channel_id=1, source_target_pairs={{0,10},{1,11},{2,8},{3,9},{4,14},{5,15},{6,12},{7,13},{8,2},{9,3},... | collective-permute-start | bytes 248840 | tf_op jit(solution)/shard_map/ppermute | solution.py:297
  24.5 2.6 %collective-permute-done.4 = f32[162,128]{1,0:T(8,128)S(1)} collective-permute-done((f32[162,128]{1,0:T(8,128)S(1)}, f32[162,128]{1,0:T(8,128)S(1)}, u32[]{:S(2)}, u32[]{:S(2)}) %collective-permute-start.4) | collective-permute-done | bytes 82976 | tf_op jit(solution)/shard_map/ppermute | solution.py:297
  27.3 2.5 %collective-permute-start.5 = (f32[162,256]{1,0:T(8,128)S(1)}, f32[162,256]{1,0:T(8,128)S(1)}, u32[]{:S(2)}, u32[]{:S(2)}) collective-permute-start(f32[162,256]{1,0:T(8,128)S(1)} %pad_maximum_fusion), channel_id=1, source_target_pairs={{0,18},{1,19},{2,16},{3,17},{4,22},{5,23},{6,20},{7,21},{8,26},{9,... | collective-permute-start | bytes 497672 | tf_op jit(solution)/shard_map/ppermute | solution.py:297
  29.9 8.4 %collective-permute-done.5 = f32[162,256]{1,0:T(8,128)S(1)} collective-permute-done((f32[162,256]{1,0:T(8,128)S(1)}, f32[162,256]{1,0:T(8,128)S(1)}, u32[]{:S(2)}, u32[]{:S(2)}) %collective-permute-start.5) | collective-permute-done | bytes 165920 | tf_op jit(solution)/shard_map/ppermute | solution.py:297
  38.3 0.3 fusion
  38.8 0.2 collective-permute-start.6
  39.0 1.1 %collective-permute-done.6 = f32[88,128]{1,0:T(8,128)S(1)} collective-permute-done((f32[88,128]{1,0:T(8,128)S(1)}, f32[88,128]{1,0:T(8,128)S(1)}, u32[]{:S(2)}, u32[]{:S(2)}) %collective-permute-start.6) | collective-permute-done | bytes 45088 | tf_op jit(solution)/shard_map/ppermute | solution.py:297
  40.1 1.3 %collective-permute-start.7 = (f32[88,128]{1,0:T(8,128)S(1)}, f32[88,128]{1,0:T(8,128)S(1)}, u32[]{:S(2)}, u32[]{:S(2)}) collective-permute-start(f32[88,128]{1,0:T(8,128)S(1)} %select_add_fusion.4), channel_id=1, source_target_pairs={{0,3},{1,2},{2,1},{3,0},{4,7},{5,6},{6,5},{7,4},{8,11},{9,10},{10,... | collective-permute-start | bytes 135176 | tf_op jit(solution)/shard_map/ppermute | solution.py:297
  41.4 2.4 %collective-permute-done.7 = f32[88,128]{1,0:T(8,128)S(1)} collective-permute-done((f32[88,128]{1,0:T(8,128)S(1)}, f32[88,128]{1,0:T(8,128)S(1)}, u32[]{:S(2)}, u32[]{:S(2)}) %collective-permute-start.7) | collective-permute-done | bytes 45088 | tf_op jit(solution)/shard_map/ppermute | solution.py:297
  43.8 1.1 %collective-permute-start.8 = (f32[88,128]{1,0:T(8,128)S(1)}, f32[88,128]{1,0:T(8,128)S(1)}, u32[]{:S(2)}, u32[]{:S(2)}) collective-permute-start(f32[88,128]{1,0:T(8,128)S(1)} %add.69), channel_id=1, source_target_pairs={{0,6},{1,7},{2,4},{3,5},{4,2},{5,3},{6,0},{7,1},{8,14},{9,15},{10,... | collective-permute-start | bytes 135176 | tf_op jit(solution)/shard_map/ppermute | solution.py:297
  44.9 2.6 %collective-permute-done.8 = f32[88,128]{1,0:T(8,128)S(1)} collective-permute-done((f32[88,128]{1,0:T(8,128)S(1)}, f32[88,128]{1,0:T(8,128)S(1)}, u32[]{:S(2)}, u32[]{:S(2)}) %collective-permute-start.8) | collective-permute-done | bytes 45088 | tf_op jit(solution)/shard_map/ppermute | solution.py:297
  47.5 0.8 %collective-permute-start.9 = (f32[88,128]{1,0:T(8,128)S(1)}, f32[88,128]{1,0:T(8,128)S(1)}, u32[]{:S(2)}, u32[]{:S(2)}) collective-permute-start(f32[88,128]{1,0:T(8,128)S(1)} %add.70), channel_id=1, source_target_pairs={{0,10},{1,11},{2,8},{3,9},{4,14},{5,15},{6,12},{7,13},{8,2},{9,3},... | collective-permute-start | bytes 135176 | tf_op jit(solution)/shard_map/ppermute | solution.py:297
  48.3 2.9 %collective-permute-done.9 = f32[88,128]{1,0:T(8,128)S(1)} collective-permute-done((f32[88,128]{1,0:T(8,128)S(1)}, f32[88,128]{1,0:T(8,128)S(1)}, u32[]{:S(2)}, u32[]{:S(2)}) %collective-permute-start.9) | collective-permute-done | bytes 45088 | tf_op jit(solution)/shard_map/ppermute | solution.py:297
  51.4 1.5 %gaunt_tables.1 = (bf16[256,4096]{1,0:T(8,128)(2,1)S(1)}, f32[88,4096]{1,0:T(8,128)S(1)}, bf16[128,4096]{1,0:T(8,128)(2,1)S(1)}) custom-call(s32[3,4096]{1,0:T(4,128)S(1)} %copy-done, f32[1,4096]{1,0:T(1,128)S(1)} %bitcast.3), custom_call_target="tpu_custom_call" | custom-call | flops 8388608 | bytes 5242880 | tf_op jit(solution)/shard_map/gaunt_tables/pallas_call | solution.py:168
  53.0 3.7 %finish.1 = (f32[162,162]{1,0:T(8,128)}, f32[4,81]{1,0:T(4,128)}) custom-call(f32[88,128]{1,0:T(8,128)S(1)} %get-tuple-element.25.top_ref, f32[88,128]{1,0:T(8,128)S(1)} %get-tuple-element.24.bottom_ref, bf16[256,4096]{1,0:T(8,128)(2,1)S(1)} %get-tuple-element.17.second_ref, f32[88,4096]{1,0:T(8,128)S(1)} %get-tuple-element.18.first_ref, ...), custom_call_target="tpu_custom_call" | custom-call | tf_op jit(solution)/shard_map/finish/pallas_call | solution.py:239
  (28 shorter events, 0.8 us)
Async XLA Ops:
  6.2 5.8 %collective-permute-start = (f32[162,1024]{1,0:T(8,128)}, f32[162,1024]{1,0:T(8,128)S(1)}, u32[]{:S(2)}, u32[]{:S(2)}) collective-permute-start(f32[162,1024]{1,0:T(8,128)} %get-tuple-element.13), channel_id=1, source_target_pairs={{0,2},{1,3},{2,0},{3,1},{4,6},{5,7},{6,4},{7,5},{8,10},{9,11},{10,... | collective-permute-start | bytes 1990664 | tf_op jit(solution)/shard_map/ppermute | solution.py:297
  13.3 38.1 %copy-start = (s32[3,4096]{1,0:T(4,128)S(1)}, s32[3,4096]{1,0:T(4,128)}, u32[]{:S(2)}) copy-start(s32[3,4096]{1,0:T(4,128)} %index_ref) | copy-start | bytes 147460
  13.3 38.1 %copy-start.1 = (f32[4096]{0:T(1024)S(1)}, f32[4096]{0:T(1024)}, u32[]{:S(2)}) copy-start(f32[4096]{0:T(1024)} %param.9) | copy-start | bytes 49156
  13.3 7.4 %collective-permute-start.1 = (f32[162,256]{1,0:T(8,128)S(1)}, f32[162,256]{1,0:T(8,128)S(1)}, u32[]{:S(2)}, u32[]{:S(2)}) collective-permute-start(f32[162,256]{1,0:T(8,128)S(1)} %get-tuple-element.22), channel_id=1, source_target_pairs={{0,6},{1,7},{2,4},{3,5},{4,2},{5,3},{6,0},{7,1},{8,14},{9,15},{10,... | collective-permute-start | bytes 497672 | tf_op jit(solution)/shard_map/ppermute | solution.py:297
  16.0 6.5 %collective-permute-start.3 = (f32[162,256]{1,0:T(8,128)S(1)}, f32[162,256]{1,0:T(8,128)S(1)}, u32[]{:S(2)}, u32[]{:S(2)}) collective-permute-start(f32[162,256]{1,0:T(8,128)S(1)} %get-tuple-element.23), channel_id=1, source_target_pairs={{0,10},{1,11},{2,8},{3,9},{4,14},{5,15},{6,12},{7,13},{8,2},{9,3},... | collective-permute-start | bytes 497672 | tf_op jit(solution)/shard_map/ppermute | solution.py:297
  22.5 4.6 %collective-permute-start.4 = (f32[162,128]{1,0:T(8,128)S(1)}, f32[162,128]{1,0:T(8,128)S(1)}, u32[]{:S(2)}, u32[]{:S(2)}) collective-permute-start(f32[162,128]{1,0:T(8,128)S(1)} %slice_select_fusion.3), channel_id=1, source_target_pairs={{0,6},{1,7},{2,4},{3,5},{4,2},{5,3},{6,0},{7,1},{8,14},{9,15},{10,... | collective-permute-start | bytes 248840 | tf_op jit(solution)/shard_map/ppermute | solution.py:297
  22.6 4.7 %collective-permute-start.2 = (f32[162,128]{1,0:T(8,128)S(1)}, f32[162,128]{1,0:T(8,128)S(1)}, u32[]{:S(2)}, u32[]{:S(2)}) collective-permute-start(f32[162,128]{1,0:T(8,128)S(1)} %slice_select_fusion.4), channel_id=1, source_target_pairs={{0,10},{1,11},{2,8},{3,9},{4,14},{5,15},{6,12},{7,13},{8,2},{9,3},... | collective-permute-start | bytes 248840 | tf_op jit(solution)/shard_map/ppermute | solution.py:297
  27.3 11.0 %collective-permute-start.5 = (f32[162,256]{1,0:T(8,128)S(1)}, f32[162,256]{1,0:T(8,128)S(1)}, u32[]{:S(2)}, u32[]{:S(2)}) collective-permute-start(f32[162,256]{1,0:T(8,128)S(1)} %pad_maximum_fusion), channel_id=1, source_target_pairs={{0,18},{1,19},{2,16},{3,17},{4,22},{5,23},{6,20},{7,21},{8,26},{9,... | collective-permute-start | bytes 497672 | tf_op jit(solution)/shard_map/ppermute | solution.py:297
  38.8 1.3 %collective-permute-start.6 = (f32[88,128]{1,0:T(8,128)S(1)}, f32[88,128]{1,0:T(8,128)S(1)}, u32[]{:S(2)}, u32[]{:S(2)}) collective-permute-start(f32[88,128]{1,0:T(8,128)S(1)} %pad_select_fusion), channel_id=1, source_target_pairs={{0,2},{1,3},{2,0},{3,1},{4,6},{5,7},{6,4},{7,5},{8,10},{9,11},{10,... | collective-permute-start | bytes 135176 | tf_op jit(solution)/shard_map/ppermute | solution.py:297
  40.1 3.7 %collective-permute-start.7 = (f32[88,128]{1,0:T(8,128)S(1)}, f32[88,128]{1,0:T(8,128)S(1)}, u32[]{:S(2)}, u32[]{:S(2)}) collective-permute-start(f32[88,128]{1,0:T(8,128)S(1)} %select_add_fusion.4), channel_id=1, source_target_pairs={{0,3},{1,2},{2,1},{3,0},{4,7},{5,6},{6,5},{7,4},{8,11},{9,10},{10,... | collective-permute-start | bytes 135176 | tf_op jit(solution)/shard_map/ppermute | solution.py:297
  43.8 3.7 %collective-permute-start.8 = (f32[88,128]{1,0:T(8,128)S(1)}, f32[88,128]{1,0:T(8,128)S(1)}, u32[]{:S(2)}, u32[]{:S(2)}) collective-permute-start(f32[88,128]{1,0:T(8,128)S(1)} %add.69), channel_id=1, source_target_pairs={{0,6},{1,7},{2,4},{3,5},{4,2},{5,3},{6,0},{7,1},{8,14},{9,15},{10,... | collective-permute-start | bytes 135176 | tf_op jit(solution)/shard_map/ppermute | solution.py:297
  47.5 3.7 %collective-permute-start.9 = (f32[88,128]{1,0:T(8,128)S(1)}, f32[88,128]{1,0:T(8,128)S(1)}, u32[]{:S(2)}, u32[]{:S(2)}) collective-permute-start(f32[88,128]{1,0:T(8,128)S(1)} %add.70), channel_id=1, source_target_pairs={{0,10},{1,11},{2,8},{3,9},{4,14},{5,15},{6,12},{7,13},{8,2},{9,3},... | collective-permute-start | bytes 135176 | tf_op jit(solution)/shard_map/ppermute | solution.py:297
  51.2 1.8 %collective-permute-start.10 = (f32[88,128]{1,0:T(8,128)S(1)}, f32[88,128]{1,0:T(8,128)S(1)}, u32[]{:S(2)}, u32[]{:S(2)}) collective-permute-start(f32[88,128]{1,0:T(8,128)S(1)} %add.71), channel_id=1, source_target_pairs={{0,2},{1,3},{2,0},{3,1},{4,6},{5,7},{6,4},{7,5},{8,10},{9,11},{10,... | collective-permute-start | bytes 135176 | tf_op jit(solution)/shard_map/ppermute | solution.py:297

commit v3 on v2

--- a/solution.py
+++ b/solution.py
@@ -8,7 +8,7 @@
 from jax.sharding import PartitionSpec as P
 
 LANES = 128
-VMEM_LIMIT = 55 * 2**20
+VMEM_LIMIT = 52 * 2**20
 
 
 def weighted_pairs(coeffs, band_weights):
@@ -65,7 +65,7 @@
     first = pltpu.make_async_copy(matching_hbm, matching, sems.at[0])
     upper = pltpu.make_async_copy(mine.at[:middle], vectors.at[:middle], sems.at[1])
     lower = pltpu.make_async_copy(mine.at[middle:], vectors.at[middle:], sems.at[2])
-    later = pltpu.make_async_copy(other.at[:middle], ahead, sems.at[3])
+    later = pltpu.make_async_copy(other.at[: ahead.shape[0]], ahead, sems.at[3])
     first.start()
     upper.start()
     lower.start()
@@ -93,6 +93,10 @@
 HBM = pl.BlockSpec(memory_space=pltpu.HBM)
 
 
+def rows_ahead(depth):
+    return depth * 2 // 5 // LANES * LANES
+
+
 def cost(channels, depth, columns):
     return pl.CostEstimate(
         flops=2 * channels * depth * columns,
@@ -108,7 +112,7 @@
         out_shape=(
             jax.ShapeDtypeStruct((channels, columns), jnp.float32),
             jax.ShapeDtypeStruct(matching.shape, matching.dtype),
-            jax.ShapeDtypeStruct((depth // 2, columns), vectors.dtype),
+            jax.ShapeDtypeStruct((rows_ahead(depth), columns), vectors.dtype),
         ),
         in_specs=[SMEM, HBM, HBM],
         out_specs=(VMEM, VMEM, VMEM),
@@ -130,7 +134,7 @@
         in_specs=[SMEM, VMEM, VMEM, HBM],
         out_specs=VMEM,
         scratch_shapes=[
-            pltpu.VMEM((depth - depth // 2, columns), vectors.dtype),
+            pltpu.VMEM((depth - rows_ahead(depth), columns), vectors.dtype),
             pltpu.SemaphoreType.DMA,
         ],
         compiler_params=pltpu.CompilerParams(vmem_limit_bytes=VMEM_LIMIT),
@@ -323,7 +327,9 @@
         block_weights = jnp.where(bits[level] == 1, block_weights[middle:], block_weights[:middle])
     tied = lax.optimization_barrier((block, gaunt_index, gaunt_value))
     tables = gaunt_tables(tied[1], tied[2], channels // 2)
-    block = block + exchange(tied[0], 1 | (1 << (levels - 1)))
+    come = exchange(tied[0], 1 | (1 << (levels - 1)))
+    come, tables = lax.optimization_barrier((come, tables))
+    block = block + come
 
     top, bottom = pack(weighted_pairs(block, block_weights))
     which = own

time: 56.9 us -> 53.5 us (0.940)
  Pallas kernels: 16.1 us -> 14.3 us
  other arithmetic: 1.53 us -> 0.44 us
    add x1, other arithmetic: 1.19 us -> 0.1 us  [body(): total = staying + arriving]
    pallas_call x1, Pallas kernels: 5.27 us -> 4.23 us  [staying_product(): pl.pallas_call(functools.partial(staying_kernel, columns), out_shape=jax....]
    pallas_call x1, Pallas kernels: 5.57 us -> 4.83 us  [leaving_product(): pl.pallas_call(functools.partial(leaving_kernel, columns), out_shape=(jax...]
  transfers between devices with their start and end apart: 11 -> 11, of which waited for: 9 -> 10; matrix products, arithmetic and copies ran while one was open for 2% -> 2% of each run, Pallas kernels for 12% -> 11%
where the time goes in v3:
time: 53.5 us; the launch traced here: 53.3 us
  waiting for transfers between devices  24.1 us (45%)
  Pallas kernels  14.3 us (27%)
  starting transfers between devices  12.4 us (23%)
  local copies, waits for them, and re-layouts  0.86 us (2%)
  between operations  0.81 us (2%)
    ppermute x11, waiting for transfers between devices, exchange(): return lax.ppermute(block, ('basis', 'band'), pairs)  24.1 us
    ppermute x11, starting transfers between devices, exchange(): return lax.ppermute(block, ('basis', 'band'), pairs)  12.4 us
    pallas_call x1, Pallas kernels, leaving_product(): pl.pallas_call(functools.partial(leaving_kernel, columns), out_shape=(jax...  4.83 us
    pallas_call x1, Pallas kernels, staying_product(): pl.pallas_call(functools.partial(staying_kernel, columns), out_shape=jax....  4.23 us
    pallas_call x1, Pallas kernels, finish(): pl.pallas_call(functools.partial(finish_kernel, tile), out_shape=(jax.Sha...  3.7 us
    pallas_call x1, Pallas kernels, gaunt_tables(): pl.pallas_call(functools.partial(tables_kernel, harmonics), out_shape=sha...  1.53 us
  transfers between devices with their start and end apart: 11, of which 10 were waited for; matrix products, arithmetic and copies ran while one was open for 2% of the time, Pallas kernels for 11%

profile of v3, /device:TPU:0, one launch (start us, length us, event | category | flops | bytes accessed | tf_op | source)
XLA Modules:
  0.0 53.3 jit_solution(9324016971544121832)
XLA Ops:
  0.6 4.8 %leaving_product.1 = (f32[162,1024]{1,0:T(8,128)S(1)}, bf16[162,2560]{1,0:T(8,128)(2,1)S(1)}, bf16[1024,1024]{1,0:T(8,128)(2,1)}) custom-call(s32[1]{0:T(128)} %bitcast.1.part_ref, bf16[162,2560]{1,0:T(8,128)(2,1)} %matching_hbm.1, bf16[2560,2048]{1,0:T(8,128)(2,1)} %vectors_hbm.3), custom_call_target="tpu_custom_call" | custom-call | flops 849346560 | bytes 6735872 | tf_op jit(solution)/shard_map/leaving_product/pallas_call | solution.py:110
  5.5 0.5 collective-permute-start
  6.0 4.2 %staying_product.1 = f32[162,1024]{1,0:T(8,128)S(1)} custom-call(s32[1]{0:T(128)} %bitcast.part_ref, bf16[162,2560]{1,0:T(8,128)(2,1)S(1)} %get-tuple-element.15.matching, bf16[1024,1024]{1,0:T(8,128)(2,1)} %get-tuple-element.16.ahead, bf16[2560,2048]{1,0:T(8,128)(2,1)} %vectors_hbm.3), custom_call_target="tpu_custom_call" | custom-call | flops 849346560 | bytes 6735872 | tf_op jit(solution)/shard_map/staying_product/pallas_call | solution.py:131
  10.4 2.7 %collective-permute-start.1 = (f32[162,256]{1,0:T(8,128)S(1)}, f32[162,256]{1,0:T(8,128)S(1)}, u32[]{:S(2)}, u32[]{:S(2)}) collective-permute-start(f32[162,256]{1,0:T(8,128)S(1)} %get-tuple-element.30), channel_id=1, source_target_pairs={{0,6},{1,7},{2,4},{3,5},{4,2},{5,3},{6,0},{7,1},{8,14},{9,15},{10,... | collective-permute-start | bytes 497672 | tf_op jit(solution)/shard_map/ppermute | solution.py:301
  13.1 1.2 %collective-permute-start.3 = (f32[162,256]{1,0:T(8,128)S(1)}, f32[162,256]{1,0:T(8,128)S(1)}, u32[]{:S(2)}, u32[]{:S(2)}) collective-permute-start(f32[162,256]{1,0:T(8,128)S(1)} %get-tuple-element.31), channel_id=1, source_target_pairs={{0,10},{1,11},{2,8},{3,9},{4,14},{5,15},{6,12},{7,13},{8,2},{9,3},... | collective-permute-start | bytes 497672 | tf_op jit(solution)/shard_map/ppermute | solution.py:301
  14.3 0.8 %fusion.4 = (f32[128]{0:T(128)S(1)}, f32[128]{0:T(128)S(1)}) fusion(f32[2048]{0:T(1024)} %param.7, s32[]{:T(128)S(6)} %select_n.87, s32[]{:T(128)S(6)} %select_n.88), kind=kLoop, calls=%fused_computation.22 | loop fusion | bytes 2056 | tf_op jit(solution)/shard_map/dynamic_slice | solution.py:319
  15.1 2.7 %collective-permute-done.1 = f32[162,256]{1,0:T(8,128)S(1)} collective-permute-done((f32[162,256]{1,0:T(8,128)S(1)}, f32[162,256]{1,0:T(8,128)S(1)}, u32[]{:S(2)}, u32[]{:S(2)}) %collective-permute-start.1) | collective-permute-done | bytes 165920 | tf_op jit(solution)/shard_map/ppermute | solution.py:301
  17.8 1.7 %collective-permute-done.3 = f32[162,256]{1,0:T(8,128)S(1)} collective-permute-done((f32[162,256]{1,0:T(8,128)S(1)}, f32[162,256]{1,0:T(8,128)S(1)}, u32[]{:S(2)}, u32[]{:S(2)}) %collective-permute-start.3) | collective-permute-done | bytes 165920 | tf_op jit(solution)/shard_map/ppermute | solution.py:301
  19.8 1.9 %collective-permute-start.2 = (f32[162,128]{1,0:T(8,128)S(1)}, f32[162,128]{1,0:T(8,128)S(1)}, u32[]{:S(2)}, u32[]{:S(2)}) collective-permute-start(f32[162,128]{1,0:T(8,128)S(1)} %slice_select_fusion.4), channel_id=1, source_target_pairs={{0,10},{1,11},{2,8},{3,9},{4,14},{5,15},{6,12},{7,13},{8,2},{9,3},... | collective-permute-start | bytes 248840 | tf_op jit(solution)/shard_map/ppermute | solution.py:301
  21.7 2.6 %collective-permute-done.4 = f32[162,128]{1,0:T(8,128)S(1)} collective-permute-done((f32[162,128]{1,0:T(8,128)S(1)}, f32[162,128]{1,0:T(8,128)S(1)}, u32[]{:S(2)}, u32[]{:S(2)}) %collective-permute-start.4) | collective-permute-done | bytes 82976 | tf_op jit(solution)/shard_map/ppermute | solution.py:301
  24.5 2.5 %collective-permute-start.5 = (f32[162,256]{1,0:T(8,128)S(1)}, f32[162,256]{1,0:T(8,128)S(1)}, u32[]{:S(2)}, u32[]{:S(2)}) collective-permute-start(f32[162,256]{1,0:T(8,128)S(1)} %pad_maximum_fusion), channel_id=1, source_target_pairs={{0,18},{1,19},{2,16},{3,17},{4,22},{5,23},{6,20},{7,21},{8,26},{9,... | collective-permute-start | bytes 497672 | tf_op jit(solution)/shard_map/ppermute | solution.py:301
  27.0 1.5 %gaunt_tables.1 = (bf16[256,4096]{1,0:T(8,128)(2,1)S(1)}, f32[88,4096]{1,0:T(8,128)S(1)}, bf16[128,4096]{1,0:T(8,128)(2,1)S(1)}) custom-call(s32[3,4096]{1,0:T(4,128)S(1)} %copy-done, f32[1,4096]{1,0:T(1,128)S(1)} %bitcast.3), custom_call_target="tpu_custom_call" | custom-call | flops 8388608 | bytes 5242880 | tf_op jit(solution)/shard_map/gaunt_tables/pallas_call | solution.py:172
  28.6 6.9 %collective-permute-done.5 = f32[162,256]{1,0:T(8,128)S(1)} collective-permute-done((f32[162,256]{1,0:T(8,128)S(1)}, f32[162,256]{1,0:T(8,128)S(1)}, u32[]{:S(2)}, u32[]{:S(2)}) %collective-permute-start.5) | collective-permute-done | bytes 165920 | tf_op jit(solution)/shard_map/ppermute | solution.py:301
  35.5 0.3 fusion
  36.2 1.1 %collective-permute-done.6 = f32[88,128]{1,0:T(8,128)S(1)} collective-permute-done((f32[88,128]{1,0:T(8,128)S(1)}, f32[88,128]{1,0:T(8,128)S(1)}, u32[]{:S(2)}, u32[]{:S(2)}) %collective-permute-start.6) | collective-permute-done | bytes 45088 | tf_op jit(solution)/shard_map/ppermute | solution.py:301
  37.3 1.3 %collective-permute-start.7 = (f32[88,128]{1,0:T(8,128)S(1)}, f32[88,128]{1,0:T(8,128)S(1)}, u32[]{:S(2)}, u32[]{:S(2)}) collective-permute-start(f32[88,128]{1,0:T(8,128)S(1)} %select_add_fusion.4), channel_id=1, source_target_pairs={{0,3},{1,2},{2,1},{3,0},{4,7},{5,6},{6,5},{7,4},{8,11},{9,10},{10,... | collective-permute-start | bytes 135176 | tf_op jit(solution)/shard_map/ppermute | solution.py:301
  38.5 2.4 %collective-permute-done.7 = f32[88,128]{1,0:T(8,128)S(1)} collective-permute-done((f32[88,128]{1,0:T(8,128)S(1)}, f32[88,128]{1,0:T(8,128)S(1)}, u32[]{:S(2)}, u32[]{:S(2)}) %collective-permute-start.7) | collective-permute-done | bytes 45088 | tf_op jit(solution)/shard_map/ppermute | solution.py:301
  40.9 1.1 %collective-permute-start.8 = (f32[88,128]{1,0:T(8,128)S(1)}, f32[88,128]{1,0:T(8,128)S(1)}, u32[]{:S(2)}, u32[]{:S(2)}) collective-permute-start(f32[88,128]{1,0:T(8,128)S(1)} %add.69), channel_id=1, source_target_pairs={{0,6},{1,7},{2,4},{3,5},{4,2},{5,3},{6,0},{7,1},{8,14},{9,15},{10,... | collective-permute-start | bytes 135176 | tf_op jit(solution)/shard_map/ppermute | solution.py:301
  42.0 2.6 %collective-permute-done.8 = f32[88,128]{1,0:T(8,128)S(1)} collective-permute-done((f32[88,128]{1,0:T(8,128)S(1)}, f32[88,128]{1,0:T(8,128)S(1)}, u32[]{:S(2)}, u32[]{:S(2)}) %collective-permute-start.8) | collective-permute-done | bytes 45088 | tf_op jit(solution)/shard_map/ppermute | solution.py:301
  44.6 0.8 %collective-permute-start.9 = (f32[88,128]{1,0:T(8,128)S(1)}, f32[88,128]{1,0:T(8,128)S(1)}, u32[]{:S(2)}, u32[]{:S(2)}) collective-permute-start(f32[88,128]{1,0:T(8,128)S(1)} %add.70), channel_id=1, source_target_pairs={{0,10},{1,11},{2,8},{3,9},{4,14},{5,15},{6,12},{7,13},{8,2},{9,3},... | collective-permute-start | bytes 135176 | tf_op jit(solution)/shard_map/ppermute | solution.py:301
  45.4 2.9 %collective-permute-done.9 = f32[88,128]{1,0:T(8,128)S(1)} collective-permute-done((f32[88,128]{1,0:T(8,128)S(1)}, f32[88,128]{1,0:T(8,128)S(1)}, u32[]{:S(2)}, u32[]{:S(2)}) %collective-permute-start.9) | collective-permute-done | bytes 45088 | tf_op jit(solution)/shard_map/ppermute | solution.py:301
  48.3 0.2 collective-permute-start.10
  48.5 1.1 %collective-permute-done.10 = f32[88,128]{1,0:T(8,128)S(1)} collective-permute-done((f32[88,128]{1,0:T(8,128)S(1)}, f32[88,128]{1,0:T(8,128)S(1)}, u32[]{:S(2)}, u32[]{:S(2)}) %collective-permute-start.10) | collective-permute-done | bytes 45088 | tf_op jit(solution)/shard_map/ppermute | solution.py:301
  49.6 3.7 %finish.1 = (f32[162,162]{1,0:T(8,128)}, f32[4,81]{1,0:T(4,128)}) custom-call(f32[88,128]{1,0:T(8,128)S(1)} %get-tuple-element.33.top_ref, f32[88,128]{1,0:T(8,128)S(1)} %get-tuple-element.32.bottom_ref, bf16[256,4096]{1,0:T(8,128)(2,1)S(1)} %get-tuple-element.25.second_ref, f32[88,4096]{1,0:T(8,128)S(1)} %get-tuple-element.26.first_ref, ...), custom_call_target="tpu_custom_call" | custom-call | tf_op jit(solution)/shard_map/finish/pallas_call | solution.py:243
  (28 shorter events, 0.9 us)
Async XLA Ops:
  5.5 4.8 %collective-permute-start = (f32[162,1024]{1,0:T(8,128)S(1)}, f32[162,1024]{1,0:T(8,128)S(1)}, u32[]{:S(2)}, u32[]{:S(2)}) collective-permute-start(f32[162,1024]{1,0:T(8,128)S(1)} %get-tuple-element.17), channel_id=1, source_target_pairs={{0,2},{1,3},{2,0},{3,1},{4,6},{5,7},{6,4},{7,5},{8,10},{9,11},{10,... | collective-permute-start | bytes 1990664 | tf_op jit(solution)/shard_map/ppermute | solution.py:301
  10.4 16.7 %copy-start = (s32[3,4096]{1,0:T(4,128)S(1)}, s32[3,4096]{1,0:T(4,128)}, u32[]{:S(2)}) copy-start(s32[3,4096]{1,0:T(4,128)} %index_ref) | copy-start | bytes 147460
  10.4 16.7 %copy-start.1 = (f32[4096]{0:T(1024)S(1)}, f32[4096]{0:T(1024)}, u32[]{:S(2)}) copy-start(f32[4096]{0:T(1024)} %param.9) | copy-start | bytes 49156
  10.4 7.4 %collective-permute-start.1 = (f32[162,256]{1,0:T(8,128)S(1)}, f32[162,256]{1,0:T(8,128)S(1)}, u32[]{:S(2)}, u32[]{:S(2)}) collective-permute-start(f32[162,256]{1,0:T(8,128)S(1)} %get-tuple-element.30), channel_id=1, source_target_pairs={{0,6},{1,7},{2,4},{3,5},{4,2},{5,3},{6,0},{7,1},{8,14},{9,15},{10,... | collective-permute-start | bytes 497672 | tf_op jit(solution)/shard_map/ppermute | solution.py:301
  13.1 6.5 %collective-permute-start.3 = (f32[162,256]{1,0:T(8,128)S(1)}, f32[162,256]{1,0:T(8,128)S(1)}, u32[]{:S(2)}, u32[]{:S(2)}) collective-permute-start(f32[162,256]{1,0:T(8,128)S(1)} %get-tuple-element.31), channel_id=1, source_target_pairs={{0,10},{1,11},{2,8},{3,9},{4,14},{5,15},{6,12},{7,13},{8,2},{9,3},... | collective-permute-start | bytes 497672 | tf_op jit(solution)/shard_map/ppermute | solution.py:301
  19.7 4.6 %collective-permute-start.4 = (f32[162,128]{1,0:T(8,128)S(1)}, f32[162,128]{1,0:T(8,128)S(1)}, u32[]{:S(2)}, u32[]{:S(2)}) collective-permute-start(f32[162,128]{1,0:T(8,128)S(1)} %slice_select_fusion.3), channel_id=1, source_target_pairs={{0,6},{1,7},{2,4},{3,5},{4,2},{5,3},{6,0},{7,1},{8,14},{9,15},{10,... | collective-permute-start | bytes 248840 | tf_op jit(solution)/shard_map/ppermute | solution.py:301
  19.8 4.7 %collective-permute-start.2 = (f32[162,128]{1,0:T(8,128)S(1)}, f32[162,128]{1,0:T(8,128)S(1)}, u32[]{:S(2)}, u32[]{:S(2)}) collective-permute-start(f32[162,128]{1,0:T(8,128)S(1)} %slice_select_fusion.4), channel_id=1, source_target_pairs={{0,10},{1,11},{2,8},{3,9},{4,14},{5,15},{6,12},{7,13},{8,2},{9,3},... | collective-permute-start | bytes 248840 | tf_op jit(solution)/shard_map/ppermute | solution.py:301
  24.5 11.0 %collective-permute-start.5 = (f32[162,256]{1,0:T(8,128)S(1)}, f32[162,256]{1,0:T(8,128)S(1)}, u32[]{:S(2)}, u32[]{:S(2)}) collective-permute-start(f32[162,256]{1,0:T(8,128)S(1)} %pad_maximum_fusion), channel_id=1, source_target_pairs={{0,18},{1,19},{2,16},{3,17},{4,22},{5,23},{6,20},{7,21},{8,26},{9,... | collective-permute-start | bytes 497672 | tf_op jit(solution)/shard_map/ppermute | solution.py:301
  35.9 1.3 %collective-permute-start.6 = (f32[88,128]{1,0:T(8,128)S(1)}, f32[88,128]{1,0:T(8,128)S(1)}, u32[]{:S(2)}, u32[]{:S(2)}) collective-permute-start(f32[88,128]{1,0:T(8,128)S(1)} %pad_select_fusion), channel_id=1, source_target_pairs={{0,2},{1,3},{2,0},{3,1},{4,6},{5,7},{6,4},{7,5},{8,10},{9,11},{10,... | collective-permute-start | bytes 135176 | tf_op jit(solution)/shard_map/ppermute | solution.py:301
  37.3 3.7 %collective-permute-start.7 = (f32[88,128]{1,0:T(8,128)S(1)}, f32[88,128]{1,0:T(8,128)S(1)}, u32[]{:S(2)}, u32[]{:S(2)}) collective-permute-start(f32[88,128]{1,0:T(8,128)S(1)} %select_add_fusion.4), channel_id=1, source_target_pairs={{0,3},{1,2},{2,1},{3,0},{4,7},{5,6},{6,5},{7,4},{8,11},{9,10},{10,... | collective-permute-start | bytes 135176 | tf_op jit(solution)/shard_map/ppermute | solution.py:301
  40.9 3.7 %collective-permute-start.8 = (f32[88,128]{1,0:T(8,128)S(1)}, f32[88,128]{1,0:T(8,128)S(1)}, u32[]{:S(2)}, u32[]{:S(2)}) collective-permute-start(f32[88,128]{1,0:T(8,128)S(1)} %add.69), channel_id=1, source_target_pairs={{0,6},{1,7},{2,4},{3,5},{4,2},{5,3},{6,0},{7,1},{8,14},{9,15},{10,... | collective-permute-start | bytes 135176 | tf_op jit(solution)/shard_map/ppermute | solution.py:301
  44.6 3.7 %collective-permute-start.9 = (f32[88,128]{1,0:T(8,128)S(1)}, f32[88,128]{1,0:T(8,128)S(1)}, u32[]{:S(2)}, u32[]{:S(2)}) collective-permute-start(f32[88,128]{1,0:T(8,128)S(1)} %add.70), channel_id=1, source_target_pairs={{0,10},{1,11},{2,8},{3,9},{4,14},{5,15},{6,12},{7,13},{8,2},{9,3},... | collective-permute-start | bytes 135176 | tf_op jit(solution)/shard_map/ppermute | solution.py:301
  48.3 1.3 %collective-permute-start.10 = (f32[88,128]{1,0:T(8,128)S(1)}, f32[88,128]{1,0:T(8,128)S(1)}, u32[]{:S(2)}, u32[]{:S(2)}) collective-permute-start(f32[88,128]{1,0:T(8,128)S(1)} %add.71), channel_id=1, source_target_pairs={{0,2},{1,3},{2,0},{3,1},{4,6},{5,7},{6,4},{7,5},{8,10},{9,11},{10,... | collective-permute-start | bytes 135176 | tf_op jit(solution)/shard_map/ppermute | solution.py:301

commit v4 on v3

v4 whole, which is shorter than its diff:
```python
import functools

import jax
import jax.numpy as jnp
from jax import lax
from jax.experimental import pallas as pl
from jax.experimental.pallas import tpu as pltpu
from jax.sharding import PartitionSpec as P

LANES = 128
TILE = 1024
LEAVING_STEPS, STAYING_STEPS, LAST_STEPS = 2, 1, 2
VMEM_LIMIT = 52 * 2**20


def weighted_pairs(coeffs, band_weights):
    scaled = coeffs * band_weights[None, :]
    return lax.dot_general(
        scaled,
        coeffs,
        (((1,), (1,)), ((), ())),
        precision=lax.Precision.HIGHEST,
        preferred_element_type=jnp.float32,
    )


def gaunt_density(density_matrix, gaunt_index, gaunt_value):
    harmonics = density_matrix.shape[0] // 2
    codes = jnp.arange(harmonics, dtype=jnp.int32)[:, None]
    first_table = (gaunt_index[0][None, :] == codes).astype(jnp.float32)
    second_table = (gaunt_index[1][None, :] == codes).astype(jnp.float32)
    target_table = (gaunt_index[2][None, :] == codes).astype(jnp.float32)
    collected = []
    for radial in range(2):
        for other in range(2):
            block = density_matrix[
                radial * harmonics : (radial + 1) * harmonics,
                other * harmonics : (other + 1) * harmonics,
            ]
            spread = jnp.dot(
                block,
                second_table,
                precision=lax.Precision.HIGHEST,
                preferred_element_type=jnp.float32,
            )
            picked = jnp.sum(spread * first_table, axis=0)
            collected.append(picked * gaunt_value)
    values = jnp.stack(collected)
    return lax.dot_general(
        values,
        target_table,
        (((1,), (1,)), ((), ())),
        precision=lax.Precision.HIGHEST,
        preferred_element_type=jnp.float32,
    )


def columns_of(ref, start, columns):
    return ref.at[:, pl.ds(pl.multiple_of(start, LANES), columns)]


def multiply(matching, pieces, out_ref):
    for at, (arrived, begin, end, vectors) in enumerate(pieces):
        arrived.wait()
        term = jnp.dot(matching[:, begin:end], vectors[begin:end, :], preferred_element_type=jnp.float32)
        if at == 0:
            out_ref[...] = term
        else:
            out_ref[...] += term


def fetch(source, target, sems, first, steps):
    depth = target.shape[0]
    pieces = []
    for step in range(steps):
        begin, end = depth * step // steps, depth * (step + 1) // steps
        copy = pltpu.make_async_copy(source.at[begin:end], target.at[begin:end], sems.at[first + step])
        copy.start()
        pieces.append((copy, begin, end, target))
    return pieces


def first_kernel(
    columns, own_ref, matching_hbm, vectors_hbm, leaving_ref, staying_ref, matching, vectors, vectors_a, sems
):
    own = own_ref[0]
    copy = pltpu.make_async_copy(matching_hbm, matching, sems.at[0])
    copy.start()
    leaving = fetch(columns_of(vectors_hbm, (1 - own) * columns, columns), vectors, sems, 1, LEAVING_STEPS)
    staying = fetch(
        columns_of(vectors_hbm, own * columns, columns // 2), vectors_a, sems, 1 + LEAVING_STEPS, STAYING_STEPS
    )
    copy.wait()
    multiply(matching, leaving, leaving_ref)
    multiply(matching, staying, staying_ref)


def second_kernel(columns, own_ref, matching, vectors_hbm, staying_ref, vectors, sems):
    start = own_ref[0] * columns + columns // 2
    multiply(matching, fetch(columns_of(vectors_hbm, start, columns // 2), vectors, sems, 0, LAST_STEPS), staying_ref)


VMEM = pl.BlockSpec(memory_space=pltpu.VMEM)
SMEM = pl.BlockSpec(memory_space=pltpu.SMEM)
HBM = pl.BlockSpec(memory_space=pltpu.HBM)


def cost(channels, depth, columns):
    return pl.CostEstimate(
        flops=2 * channels * depth * columns,
        bytes_accessed=2 * depth * (columns + channels) + 4 * channels * columns,
        transcendentals=0,
    )


def first_products(matching, vectors, own, columns):
    channels, depth = matching.shape
    return pl.pallas_call(
        functools.partial(first_kernel, columns),
        out_shape=(
            jax.ShapeDtypeStruct((channels, columns), jnp.float32),
            jax.ShapeDtypeStruct((channels, columns // 2), jnp.float32),
            jax.ShapeDtypeStruct(matching.shape, matching.dtype),
        ),
        in_specs=[SMEM, HBM, HBM],
        out_specs=(VMEM, VMEM, VMEM),
        scratch_shapes=[
            pltpu.VMEM((depth, columns), vectors.dtype),
            pltpu.VMEM((depth, columns // 2), vectors.dtype),
            pltpu.SemaphoreType.DMA((1 + LEAVING_STEPS + STAYING_STEPS,)),
        ],
        compiler_params=pltpu.CompilerParams(vmem_limit_bytes=VMEM_LIMIT),
        cost_estimate=cost(channels, depth, columns * 3 // 2),
        name="first_products",
    )(own.reshape(1), matching, vectors)


def second_products(matching, vectors, own, columns):
    channels, depth = matching.shape
    return pl.pallas_call(
        functools.partial(second_kernel, columns),
        out_shape=jax.ShapeDtypeStruct((channels, columns // 2), jnp.float32),
        in_specs=[SMEM, VMEM, HBM],
        out_specs=VMEM,
        scratch_shapes=[
            pltpu.VMEM((depth, columns // 2), vectors.dtype),
            pltpu.SemaphoreType.DMA((LAST_STEPS,)),
        ],
        compiler_params=pltpu.CompilerParams(vmem_limit_bytes=VMEM_LIMIT),
        cost_estimate=cost(channels, depth, columns // 2),
        name="second_products",
    )(own.reshape(1), matching, vectors)


def round_up(value, unit):
    return -(-value // unit) * unit


def tables_kernel(index_ref, value_ref, second_ref, first_ref, target_ref):
    entries = index_ref.shape[1]
    rows = lax.broadcasted_iota(jnp.int32, (LANES, entries), 0)
    hit = jnp.where(rows == index_ref[1:2, :], 1.0, 0.0).astype(jnp.bfloat16)
    second_ref[:LANES, :] = hit
    second_ref[LANES:, :] = hit
    first_rows = lax.broadcasted_iota(jnp.int32, (first_ref.shape[0], entries), 0)
    first_ref[...] = jnp.where(first_rows == index_ref[0:1, :], value_ref[...], 0.0)
    target_ref[...] = jnp.transpose(jnp.where(rows == index_ref[2:3, :], 1.0, 0.0)).astype(jnp.bfloat16)


def gaunt_tables(gaunt_index, gaunt_value, harmonics):
    entries = gaunt_value.shape[0]
    shapes = (
        jax.ShapeDtypeStruct((2 * LANES, entries), jnp.bfloat16),
        jax.ShapeDtypeStruct((round_up(harmonics, 8), entries), jnp.float32),
        jax.ShapeDtypeStruct((entries, LANES), jnp.bfloat16),
    )
    return pl.pallas_call(
        tables_kernel,
        out_shape=shapes,
        in_specs=[VMEM, VMEM],
        out_specs=(VMEM, VMEM, VMEM),
        compiler_params=pltpu.CompilerParams(vmem_limit_bytes=32 * 2**20),
        cost_estimate=pl.CostEstimate(flops=8 * 2**20, bytes_accessed=5 * 2**20, transcendentals=0),
        name="gaunt_tables",
    )(gaunt_index, gaunt_value.reshape(1, entries))


def two_parts(value):
    high = value.astype(jnp.bfloat16)
    return high, (value - high.astype(jnp.float32)).astype(jnp.bfloat16)


def finish_kernel(tile, top_ref, bottom_ref, second_ref, first_ref, target_ref, matrix_ref, density_ref, full):
    channels = matrix_ref.shape[0]
    harmonics = channels // 2
    extra = channels - LANES
    half = top_ref.shape[0]
    upper = jnp.concatenate([top_ref[...], bottom_ref[: LANES - half, :]], axis=0)
    rest = bottom_ref[LANES - half :, :]
    rows = lax.broadcasted_iota(jnp.int32, (LANES, LANES), 0)
    lanes = lax.broadcasted_iota(jnp.int32, (LANES, LANES), 1)
    corner_there = (rows < extra) & (lanes >= LANES // 2) & (lanes < LANES // 2 + extra)
    tall = jnp.concatenate([rest, jnp.zeros((LANES - rest.shape[0], LANES), jnp.float32)], axis=0)
    corner = pltpu.roll(upper, LANES // 2, 1)
    full[:LANES, :LANES] = jnp.where(corner_there, jnp.transpose(upper), upper)
    full[:LANES, LANES:] = jnp.transpose(tall)
    full[LANES:, :LANES] = jnp.zeros((full.shape[0] - LANES, LANES), jnp.float32)
    full[LANES : LANES + rest.shape[0], :LANES] = rest
    full[LANES:, LANES:] = jnp.zeros((full.shape[0] - LANES, LANES), jnp.float32)
    full[LANES:channels, LANES:] = corner[:extra]
    matrix_ref[...] = full[:channels, :channels]

    height = first_ref.shape[0]
    entries = second_ref.shape[1]
    blocks = []
    for radial in range(2):
        strip = full[radial * harmonics : radial * harmonics + height, :]
        blocks.append(strip[:, :LANES])
        blocks.append(pltpu.roll(strip, 2 * LANES - harmonics, 1)[:, :LANES])
    stacked = jnp.concatenate(two_parts(jnp.concatenate(blocks, axis=0)), axis=1)
    kept = []
    for start in range(0, entries, tile):
        columns = slice(start, start + tile)
        spread = jnp.dot(stacked, second_ref[:, columns], preferred_element_type=jnp.float32)
        picked = []
        for pair in range(4):
            partial_sum = jnp.zeros((8, tile), jnp.float32)
            for at in range(0, height, 8):
                here = spread[pair * height + at : pair * height + at + 8, :]
                partial_sum = partial_sum + here * first_ref[at : at + 8, columns]
            picked.append(partial_sum)
        kept.append(jnp.concatenate(two_parts(jnp.concatenate(picked, axis=0)), axis=0))
    total = jnp.dot(jnp.concatenate(kept, axis=1), target_ref[...], preferred_element_type=jnp.float32)
    for pair in range(4):
        both = total[8 * pair : 8 * pair + 8] + total[32 + 8 * pair : 40 + 8 * pair]
        density_ref[pair : pair + 1, :] = jnp.sum(both, axis=0, keepdims=True)[:, :harmonics]


def finish(top, bottom, tables, channels):
    second, first, target = tables
    entries = second.shape[1]
    harmonics = channels // 2
    tile = TILE if entries % TILE == 0 else entries
    return pl.pallas_call(
        functools.partial(finish_kernel, tile),
        out_shape=(
            jax.ShapeDtypeStruct((channels, channels), jnp.float32),
            jax.ShapeDtypeStruct((4, harmonics), jnp.float32),
        ),
        in_specs=[VMEM] * 5,
        out_specs=(VMEM, VMEM),
        scratch_shapes=[pltpu.VMEM((round_up(harmonics + first.shape[0], 16), 2 * LANES), jnp.float32)],
        compiler_params=pltpu.CompilerParams(vmem_limit_bytes=32 * 2**20),
        name="finish",
    )(top, bottom, second, first, target)


def pack(matrix):
    channels = matrix.shape[0]
    extra = channels - LANES
    half = LANES // 2
    corner = jnp.pad(matrix[LANES:, LANES:], ((0, channels - extra), (half, LANES - half - extra)))
    rows = lax.broadcasted_iota(jnp.int32, (channels, LANES), 0)
    lanes = lax.broadcasted_iota(jnp.int32, (channels, LANES), 1)
    there = (rows < extra) & (lanes >= half) & (lanes < half + extra)
    packed = jnp.where(there, corner, matrix[:, :LANES])
    height = round_up(channels, 16) // 2
    height = round_up(height, 8)
    return packed[:height], jnp.pad(packed[height:], ((0, 2 * height - channels), (0, 0)))


def plain_body(matching, vectors, weights, gaunt_index, gaunt_value):
    partial_value = jnp.dot(matching, vectors, preferred_element_type=jnp.float32)
    summed = lax.psum(partial_value, "basis")
    local_terms = weighted_pairs(summed, weights)
    density_matrix = lax.psum(local_terms, "band")
    return (density_matrix, gaunt_density(density_matrix, gaunt_index, gaunt_value))


def halves(block, bit):
    middle = block.shape[1] // 2
    low, high = block[:, :middle], block[:, middle:]
    return jnp.where(bit == 1, low, high), jnp.where(bit == 1, high, low)


def body(basis, band, matching, vectors, weights, gaunt_index, gaunt_value):
    index = lax.axis_index("basis")
    levels = basis.bit_length() - 1
    channels, columns = matching.shape[0], vectors.shape[1]
    bits = [(index >> level) & 1 for level in range(levels)]
    own = functools.reduce(jnp.bitwise_xor, bits)

    def exchange(block, mask, band_mask=0):
        pairs = [
            (i * band + j, (i ^ mask) * band + (j ^ band_mask))
            for i in range(basis)
            for j in range(band)
        ]
        return lax.ppermute(block, ("basis", "band"), pairs)

    leaving, staying_a, matching = first_products(matching, vectors, own, columns // 2)
    arriving = exchange(leaving, 1)
    staying_b = second_products(matching, vectors, own, columns // 2)
    width = columns // 4
    sent_a, kept_a = halves(staying_a + arriving[:, :width], bits[1])
    sent_b, kept_b = halves(staying_b + arriving[:, width:], bits[2])
    come_a, come_b = exchange(sent_a, 3), exchange(sent_b, 5)
    sent_a, kept_a = halves(kept_a + come_a, bits[2])
    sent_b, kept_b = halves(kept_b + come_b, bits[1])
    come_a, come_b = exchange(sent_a, 5), exchange(sent_b, 3)
    block = jnp.concatenate([kept_a + come_a, kept_b + come_b], axis=1)
    for level in range(3, levels - 1):
        sent, kept = halves(block, bits[level])
        block = kept + exchange(sent, 1 | (1 << level))
    block, weights, gaunt_index, gaunt_value = lax.optimization_barrier((block, weights, gaunt_index, gaunt_value))
    come = exchange(block, 1 | (1 << (levels - 1)))
    tables = gaunt_tables(gaunt_index, gaunt_value, channels // 2)
    width = columns // 16
    begin = own * (columns // 2)
    block_weights = jnp.concatenate(
        [
            lax.dynamic_slice_in_dim(weights, begin + (2 * bits[1] + bits[2]) * width, width),
            lax.dynamic_slice_in_dim(weights, begin + columns // 4 + (2 * bits[2] + bits[1]) * width, width),
        ]
    )
    for level in range(3, levels - 1):
        middle = block_weights.shape[0] // 2
        block_weights = jnp.where(bits[level] == 1, block_weights[middle:], block_weights[:middle])
    come, tables, block_weights = lax.optimization_barrier((come, tables, block_weights))
    block = block + come

    top, bottom = pack(weighted_pairs(block, block_weights))
    which = own
    for level in range(band.bit_length() - 1):
        which = which ^ ((lax.axis_index("band") >> level) & 1)
    sent = jnp.where(which == 1, top, bottom)
    terms = jnp.where(which == 1, bottom, top) + exchange(sent, 1)
    step = 1
    while step < band:
        terms = terms + exchange(terms, 1, step)
        step *= 2
    for level in range(1, levels - 1):
        terms = terms + exchange(terms, 1 | (1 << level))
    other = exchange(terms, 1)
    top = jnp.where(which == 1, other, terms)
    bottom = jnp.where(which == 1, terms, other)
    return finish(top, bottom, tables, channels)


def solution(mesh):
    basis, band = mesh.shape["basis"], mesh.shape["band"]

    def choose(*arrays):
        channels, depth = arrays[0].shape
        columns = arrays[1].shape[1]
        powers = basis & (basis - 1) == 0 and band & (band - 1) == 0 and basis >= 16
        sizes = columns % (16 * LANES) == 0 and depth % 256 == 0
        if powers and sizes and channels % 2 == 0 and LANES < channels <= LANES + LANES // 2:
            return body(basis, band, *arrays)
        return plain_body(*arrays)

    return jax.shard_map(
        choose,
        mesh=mesh,
        in_specs=(P(None, "basis"), P("basis", "band"), P("band"), P(), P()),
        out_specs=(P(), P()),
        check_vma=False,
    )
```

time: 53.5 us -> 49.1 us (0.918)
  Pallas kernels: 14.3 us -> 9.51 us
  starting transfers between devices: 12.4 us -> 13.9 us
  waiting for transfers between devices: 24.1 us -> 23.1 us
    pallas_call x3, Pallas kernels: 10.6 us -> 7.64 us  [the longest x1 4.38 us: first_products(): pl.pallas_call(functools.partial(first_kernel, columns), out_shape=(jax.S...]
    pallas_call x1, Pallas kernels: 3.7 us -> 1.87 us  [finish(): pl.pallas_call(functools.partial(finish_kernel, tile), out_shape=(jax.Sha...]
    ppermute x11, starting transfers between devices: 12.4 us -> 13.9 us  [exchange(): return lax.ppermute(block, ('basis', 'band'), pairs)]
    ppermute x11, waiting for transfers between devices: 24.1 us -> 23.1 us  [exchange(): return lax.ppermute(block, ('basis', 'band'), pairs)]
  transfers between devices with their start and end apart: 11 -> 11, of which waited for: 10 -> 9; matrix products, arithmetic and copies ran while one was open for 2% -> 2% of each run, Pallas kernels for 11% -> 7%
where the time goes in v4:
time: 49.1 us; the launch traced here: 48.9 us
  waiting for transfers between devices  23.1 us (47%)
  starting transfers between devices  13.9 us (28%)
  Pallas kernels  9.51 us (19%)
  local copies, waits for them, and re-layouts  0.86 us (2%)
  between operations  0.82 us (2%)
    ppermute x11, waiting for transfers between devices, exchange(): return lax.ppermute(block, ('basis', 'band'), pairs)  23.1 us
    ppermute x11, starting transfers between devices, exchange(): return lax.ppermute(block, ('basis', 'band'), pairs)  13.9 us
    pallas_call x1, Pallas kernels, first_products(): pl.pallas_call(functools.partial(first_kernel, columns), out_shape=(jax.S...  4.38 us
    pallas_call x1, Pallas kernels, second_products(): pl.pallas_call(functools.partial(second_kernel, columns), out_shape=jax.S...  2.15 us
    pallas_call x1, Pallas kernels, finish(): pl.pallas_call(functools.partial(finish_kernel, tile), out_shape=(jax.Sha...  1.87 us
    pallas_call x1, Pallas kernels, gaunt_tables(): pl.pallas_call(tables_kernel, out_shape=shapes, in_specs=[VMEM, VMEM], ou...  1.11 us
  transfers between devices with their start and end apart: 11, of which 9 were waited for; matrix products, arithmetic and copies ran while one was open for 2% of the time, Pallas kernels for 7%

profile of v4, /device:TPU:0, one launch (start us, length us, event | category | flops | bytes accessed | tf_op | source)
XLA Modules:
  0.0 48.9 jit_solution(10461724568411769340)
XLA Ops:
  0.6 4.4 %first_products.1 = (f32[162,1024]{1,0:T(8,128)S(1)}, f32[162,512]{1,0:T(8,128)S(1)}, bf16[162,2560]{1,0:T(8,128)(2,1)S(1)}) custom-call(s32[1]{0:T(128)} %bitcast.own_ref, bf16[162,2560]{1,0:T(8,128)(2,1)} %matching_hbm.1, bf16[2560,2048]{1,0:T(8,128)(2,1)} %vectors_hbm.3), custom_call_target="tpu_custom_call" | custom-call | flops 1274019840 | bytes 9689088 | tf_op jit(solution)/shard_map/first_products/pallas_call | solution.py:118
  5.0 0.5 collective-permute-start
  5.5 2.1 %second_products.1 = f32[162,512]{1,0:T(8,128)S(1)} custom-call(s32[1]{0:T(128)} %bitcast.own_ref, bf16[162,2560]{1,0:T(8,128)(2,1)S(1)} %get-tuple-element.19.matching, bf16[2560,2048]{1,0:T(8,128)(2,1)} %vectors_hbm.3), custom_call_target="tpu_custom_call" | custom-call | flops 424673280 | bytes 3782656 | tf_op jit(solution)/shard_map/second_products/pallas_call | solution.py:140
  7.9 2.7 %collective-permute-start.1 = (f32[162,256]{1,0:T(8,128)S(1)}, f32[162,256]{1,0:T(8,128)S(1)}, u32[]{:S(2)}, u32[]{:S(2)}) collective-permute-start(f32[162,256]{1,0:T(8,128)S(1)} %slice_select_fusion.1), channel_id=1, source_target_pairs={{0,6},{1,7},{2,4},{3,5},{4,2},{5,3},{6,0},{7,1},{8,14},{9,15},{10,... | collective-permute-start | bytes 497672 | tf_op jit(solution)/shard_map/ppermute | solution.py:299
  10.6 1.4 %collective-permute-start.3 = (f32[162,256]{1,0:T(8,128)S(1)}, f32[162,256]{1,0:T(8,128)S(1)}, u32[]{:S(2)}, u32[]{:S(2)}) collective-permute-start(f32[162,256]{1,0:T(8,128)S(1)} %slice_select_fusion), channel_id=1, source_target_pairs={{0,10},{1,11},{2,8},{3,9},{4,14},{5,15},{6,12},{7,13},{8,2},{9,3},... | collective-permute-start | bytes 497672 | tf_op jit(solution)/shard_map/ppermute | solution.py:299
  11.9 3.3 %collective-permute-done.1 = f32[162,256]{1,0:T(8,128)S(1)} collective-permute-done((f32[162,256]{1,0:T(8,128)S(1)}, f32[162,256]{1,0:T(8,128)S(1)}, u32[]{:S(2)}, u32[]{:S(2)}) %collective-permute-start.1) | collective-permute-done | bytes 165920 | tf_op jit(solution)/shard_map/ppermute | solution.py:299
  15.3 1.8 %collective-permute-start.2 = (f32[162,128]{1,0:T(8,128)S(1)}, f32[162,128]{1,0:T(8,128)S(1)}, u32[]{:S(2)}, u32[]{:S(2)}) collective-permute-start(f32[162,128]{1,0:T(8,128)S(1)} %slice_select_fusion.4), channel_id=1, source_target_pairs={{0,10},{1,11},{2,8},{3,9},{4,14},{5,15},{6,12},{7,13},{8,2},{9,3},... | collective-permute-start | bytes 248840 | tf_op jit(solution)/shard_map/ppermute | solution.py:299
  17.1 1.0 %collective-permute-start.4 = (f32[162,128]{1,0:T(8,128)S(1)}, f32[162,128]{1,0:T(8,128)S(1)}, u32[]{:S(2)}, u32[]{:S(2)}) collective-permute-start(f32[162,128]{1,0:T(8,128)S(1)} %slice_select_fusion.3), channel_id=1, source_target_pairs={{0,6},{1,7},{2,4},{3,5},{4,2},{5,3},{6,0},{7,1},{8,14},{9,15},{10,... | collective-permute-start | bytes 248840 | tf_op jit(solution)/shard_map/ppermute | solution.py:299
  18.2 1.6 %collective-permute-done.2 = f32[162,128]{1,0:T(8,128)S(1)} collective-permute-done((f32[162,128]{1,0:T(8,128)S(1)}, f32[162,128]{1,0:T(8,128)S(1)}, u32[]{:S(2)}, u32[]{:S(2)}) %collective-permute-start.2) | collective-permute-done | bytes 82976 | tf_op jit(solution)/shard_map/ppermute | solution.py:299
  19.7 2.0 %collective-permute-done.4 = f32[162,128]{1,0:T(8,128)S(1)} collective-permute-done((f32[162,128]{1,0:T(8,128)S(1)}, f32[162,128]{1,0:T(8,128)S(1)}, u32[]{:S(2)}, u32[]{:S(2)}) %collective-permute-start.4) | collective-permute-done | bytes 82976 | tf_op jit(solution)/shard_map/ppermute | solution.py:299
  21.8 2.4 %collective-permute-start.5 = (f32[162,256]{1,0:T(8,128)S(1)}, f32[162,256]{1,0:T(8,128)S(1)}, u32[]{:S(2)}, u32[]{:S(2)}) collective-permute-start(f32[162,256]{1,0:T(8,128)S(1)} %pad_maximum_fusion), channel_id=1, source_target_pairs={{0,18},{1,19},{2,16},{3,17},{4,22},{5,23},{6,20},{7,21},{8,26},{9,... | collective-permute-start | bytes 497672 | tf_op jit(solution)/shard_map/ppermute | solution.py:299
  24.2 0.8 %fusion.4 = (f32[128]{0:T(128)S(1)}, f32[128]{0:T(128)S(1)}) fusion(f32[2048]{0:T(1024)} %param.7, s32[]{:T(128)S(6)} %select_n.87, s32[]{:T(128)S(6)} %select_n.88), kind=kLoop, calls=%fused_computation.24 | loop fusion | bytes 2056 | tf_op jit(solution)/shard_map/dynamic_slice | solution.py:322
  25.1 1.1 %gaunt_tables.1 = (bf16[256,4096]{1,0:T(8,128)(2,1)S(1)}, f32[88,4096]{1,0:T(8,128)S(1)}, bf16[4096,128]{1,0:T(8,128)(2,1)S(1)}) custom-call(s32[3,4096]{1,0:T(4,128)S(1)} %copy-done, f32[1,4096]{1,0:T(1,128)S(1)} %bitcast.2), custom_call_target="tpu_custom_call" | custom-call | flops 8388608 | bytes 5242880 | tf_op jit(solution)/shard_map/gaunt_tables/pallas_call | solution.py:177
  26.2 6.6 %collective-permute-done.5 = f32[162,256]{1,0:T(8,128)S(1)} collective-permute-done((f32[162,256]{1,0:T(8,128)S(1)}, f32[162,256]{1,0:T(8,128)S(1)}, u32[]{:S(2)}, u32[]{:S(2)}) %collective-permute-start.5) | collective-permute-done | bytes 165920 | tf_op jit(solution)/shard_map/ppermute | solution.py:299
  32.8 0.3 fusion
  33.5 1.1 %collective-permute-done.6 = f32[88,128]{1,0:T(8,128)S(1)} collective-permute-done((f32[88,128]{1,0:T(8,128)S(1)}, f32[88,128]{1,0:T(8,128)S(1)}, u32[]{:S(2)}, u32[]{:S(2)}) %collective-permute-start.6) | collective-permute-done | bytes 45088 | tf_op jit(solution)/shard_map/ppermute | solution.py:299
  34.6 1.4 %collective-permute-start.7 = (f32[88,128]{1,0:T(8,128)S(1)}, f32[88,128]{1,0:T(8,128)S(1)}, u32[]{:S(2)}, u32[]{:S(2)}) collective-permute-start(f32[88,128]{1,0:T(8,128)S(1)} %select_add_fusion.4), channel_id=1, source_target_pairs={{0,3},{1,2},{2,1},{3,0},{4,7},{5,6},{6,5},{7,4},{8,11},{9,10},{10,... | collective-permute-start | bytes 135176 | tf_op jit(solution)/shard_map/ppermute | solution.py:299
  35.9 2.3 %collective-permute-done.7 = f32[88,128]{1,0:T(8,128)S(1)} collective-permute-done((f32[88,128]{1,0:T(8,128)S(1)}, f32[88,128]{1,0:T(8,128)S(1)}, u32[]{:S(2)}, u32[]{:S(2)}) %collective-permute-start.7) | collective-permute-done | bytes 45088 | tf_op jit(solution)/shard_map/ppermute | solution.py:299
  38.3 1.6 %collective-permute-start.8 = (f32[88,128]{1,0:T(8,128)S(1)}, f32[88,128]{1,0:T(8,128)S(1)}, u32[]{:S(2)}, u32[]{:S(2)}) collective-permute-start(f32[88,128]{1,0:T(8,128)S(1)} %add.73), channel_id=1, source_target_pairs={{0,6},{1,7},{2,4},{3,5},{4,2},{5,3},{6,0},{7,1},{8,14},{9,15},{10,... | collective-permute-start | bytes 135176 | tf_op jit(solution)/shard_map/ppermute | solution.py:299
  39.9 2.1 %collective-permute-done.8 = f32[88,128]{1,0:T(8,128)S(1)} collective-permute-done((f32[88,128]{1,0:T(8,128)S(1)}, f32[88,128]{1,0:T(8,128)S(1)}, u32[]{:S(2)}, u32[]{:S(2)}) %collective-permute-start.8) | collective-permute-done | bytes 45088 | tf_op jit(solution)/shard_map/ppermute | solution.py:299
  42.0 0.8 %collective-permute-start.9 = (f32[88,128]{1,0:T(8,128)S(1)}, f32[88,128]{1,0:T(8,128)S(1)}, u32[]{:S(2)}, u32[]{:S(2)}) collective-permute-start(f32[88,128]{1,0:T(8,128)S(1)} %add.74), channel_id=1, source_target_pairs={{0,10},{1,11},{2,8},{3,9},{4,14},{5,15},{6,12},{7,13},{8,2},{9,3},... | collective-permute-start | bytes 135176 | tf_op jit(solution)/shard_map/ppermute | solution.py:299
  42.8 2.9 %collective-permute-done.9 = f32[88,128]{1,0:T(8,128)S(1)} collective-permute-done((f32[88,128]{1,0:T(8,128)S(1)}, f32[88,128]{1,0:T(8,128)S(1)}, u32[]{:S(2)}, u32[]{:S(2)}) %collective-permute-start.9) | collective-permute-done | bytes 45088 | tf_op jit(solution)/shard_map/ppermute | solution.py:299
  45.9 1.1 %collective-permute-done.10 = f32[88,128]{1,0:T(8,128)S(1)} collective-permute-done((f32[88,128]{1,0:T(8,128)S(1)}, f32[88,128]{1,0:T(8,128)S(1)}, u32[]{:S(2)}, u32[]{:S(2)}) %collective-permute-start.10) | collective-permute-done | bytes 45088 | tf_op jit(solution)/shard_map/ppermute | solution.py:299
  47.0 1.9 %finish.1 = (f32[162,162]{1,0:T(8,128)}, f32[4,81]{1,0:T(4,128)}) custom-call(f32[88,128]{1,0:T(8,128)S(1)} %get-tuple-element.35.top_ref, f32[88,128]{1,0:T(8,128)S(1)} %get-tuple-element.34.bottom_ref, bf16[256,4096]{1,0:T(8,128)(2,1)S(1)} %get-tuple-element.29.second_ref, f32[88,4096]{1,0:T(8,128)S(1)} %get-tuple-element.30.first_ref, ...), custom_call_target="tpu_custom_call" | custom-call | tf_op jit(solution)/shard_map/finish/pallas_call | solution.py:244
  (30 shorter events, 0.9 us)
Async XLA Ops:
  5.0 2.6 %collective-permute-start = (f32[162,1024]{1,0:T(8,128)S(1)}, f32[162,1024]{1,0:T(8,128)S(1)}, u32[]{:S(2)}, u32[]{:S(2)}) collective-permute-start(f32[162,1024]{1,0:T(8,128)S(1)} %get-tuple-element.18), channel_id=1, source_target_pairs={{0,2},{1,3},{2,0},{3,1},{4,6},{5,7},{6,4},{7,5},{8,10},{9,11},{10,... | collective-permute-start | bytes 1990664 | tf_op jit(solution)/shard_map/ppermute | solution.py:299
  7.8 17.2 %copy-start = (s32[3,4096]{1,0:T(4,128)S(1)}, s32[3,4096]{1,0:T(4,128)}, u32[]{:S(2)}) copy-start(s32[3,4096]{1,0:T(4,128)} %index_ref) | copy-start | bytes 147460
  7.8 17.2 %copy-start.1 = (f32[4096]{0:T(1024)S(1)}, f32[4096]{0:T(1024)}, u32[]{:S(2)}) copy-start(f32[4096]{0:T(1024)} %param.9) | copy-start | bytes 49156
  7.9 7.4 %collective-permute-start.1 = (f32[162,256]{1,0:T(8,128)S(1)}, f32[162,256]{1,0:T(8,128)S(1)}, u32[]{:S(2)}, u32[]{:S(2)}) collective-permute-start(f32[162,256]{1,0:T(8,128)S(1)} %slice_select_fusion.1), channel_id=1, source_target_pairs={{0,6},{1,7},{2,4},{3,5},{4,2},{5,3},{6,0},{7,1},{8,14},{9,15},{10,... | collective-permute-start | bytes 497672 | tf_op jit(solution)/shard_map/ppermute | solution.py:299
  10.6 6.5 %collective-permute-start.3 = (f32[162,256]{1,0:T(8,128)S(1)}, f32[162,256]{1,0:T(8,128)S(1)}, u32[]{:S(2)}, u32[]{:S(2)}) collective-permute-start(f32[162,256]{1,0:T(8,128)S(1)} %slice_select_fusion), channel_id=1, source_target_pairs={{0,10},{1,11},{2,8},{3,9},{4,14},{5,15},{6,12},{7,13},{8,2},{9,3},... | collective-permute-start | bytes 497672 | tf_op jit(solution)/shard_map/ppermute | solution.py:299
  15.3 4.4 %collective-permute-start.2 = (f32[162,128]{1,0:T(8,128)S(1)}, f32[162,128]{1,0:T(8,128)S(1)}, u32[]{:S(2)}, u32[]{:S(2)}) collective-permute-start(f32[162,128]{1,0:T(8,128)S(1)} %slice_select_fusion.4), channel_id=1, source_target_pairs={{0,10},{1,11},{2,8},{3,9},{4,14},{5,15},{6,12},{7,13},{8,2},{9,3},... | collective-permute-start | bytes 248840 | tf_op jit(solution)/shard_map/ppermute | solution.py:299
  17.1 4.6 %collective-permute-start.4 = (f32[162,128]{1,0:T(8,128)S(1)}, f32[162,128]{1,0:T(8,128)S(1)}, u32[]{:S(2)}, u32[]{:S(2)}) collective-permute-start(f32[162,128]{1,0:T(8,128)S(1)} %slice_select_fusion.3), channel_id=1, source_target_pairs={{0,6},{1,7},{2,4},{3,5},{4,2},{5,3},{6,0},{7,1},{8,14},{9,15},{10,... | collective-permute-start | bytes 248840 | tf_op jit(solution)/shard_map/ppermute | solution.py:299
  21.8 11.0 %collective-permute-start.5 = (f32[162,256]{1,0:T(8,128)S(1)}, f32[162,256]{1,0:T(8,128)S(1)}, u32[]{:S(2)}, u32[]{:S(2)}) collective-permute-start(f32[162,256]{1,0:T(8,128)S(1)} %pad_maximum_fusion), channel_id=1, source_target_pairs={{0,18},{1,19},{2,16},{3,17},{4,22},{5,23},{6,20},{7,21},{8,26},{9,... | collective-permute-start | bytes 497672 | tf_op jit(solution)/shard_map/ppermute | solution.py:299
  33.3 1.3 %collective-permute-start.6 = (f32[88,128]{1,0:T(8,128)S(1)}, f32[88,128]{1,0:T(8,128)S(1)}, u32[]{:S(2)}, u32[]{:S(2)}) collective-permute-start(f32[88,128]{1,0:T(8,128)S(1)} %pad_select_fusion), channel_id=1, source_target_pairs={{0,2},{1,3},{2,0},{3,1},{4,6},{5,7},{6,4},{7,5},{8,10},{9,11},{10,... | collective-permute-start | bytes 135176 | tf_op jit(solution)/shard_map/ppermute | solution.py:299
  34.6 3.7 %collective-permute-start.7 = (f32[88,128]{1,0:T(8,128)S(1)}, f32[88,128]{1,0:T(8,128)S(1)}, u32[]{:S(2)}, u32[]{:S(2)}) collective-permute-start(f32[88,128]{1,0:T(8,128)S(1)} %select_add_fusion.4), channel_id=1, source_target_pairs={{0,3},{1,2},{2,1},{3,0},{4,7},{5,6},{6,5},{7,4},{8,11},{9,10},{10,... | collective-permute-start | bytes 135176 | tf_op jit(solution)/shard_map/ppermute | solution.py:299
  38.3 3.7 %collective-permute-start.8 = (f32[88,128]{1,0:T(8,128)S(1)}, f32[88,128]{1,0:T(8,128)S(1)}, u32[]{:S(2)}, u32[]{:S(2)}) collective-permute-start(f32[88,128]{1,0:T(8,128)S(1)} %add.73), channel_id=1, source_target_pairs={{0,6},{1,7},{2,4},{3,5},{4,2},{5,3},{6,0},{7,1},{8,14},{9,15},{10,... | collective-permute-start | bytes 135176 | tf_op jit(solution)/shard_map/ppermute | solution.py:299
  42.0 3.7 %collective-permute-start.9 = (f32[88,128]{1,0:T(8,128)S(1)}, f32[88,128]{1,0:T(8,128)S(1)}, u32[]{:S(2)}, u32[]{:S(2)}) collective-permute-start(f32[88,128]{1,0:T(8,128)S(1)} %add.74), channel_id=1, source_target_pairs={{0,10},{1,11},{2,8},{3,9},{4,14},{5,15},{6,12},{7,13},{8,2},{9,3},... | collective-permute-start | bytes 135176 | tf_op jit(solution)/shard_map/ppermute | solution.py:299
  45.7 1.3 %collective-permute-start.10 = (f32[88,128]{1,0:T(8,128)S(1)}, f32[88,128]{1,0:T(8,128)S(1)}, u32[]{:S(2)}, u32[]{:S(2)}) collective-permute-start(f32[88,128]{1,0:T(8,128)S(1)} %add.75), channel_id=1, source_target_pairs={{0,2},{1,3},{2,0},{3,1},{4,6},{5,7},{6,4},{7,5},{8,10},{9,11},{10,... | collective-permute-start | bytes 135176 | tf_op jit(solution)/shard_map/ppermute | solution.py:299

commit v5 on v4

--- a/solution.py
+++ b/solution.py
@@ -10,6 +10,7 @@
 LANES = 128
 TILE = 1024
 LEAVING_STEPS, STAYING_STEPS, LAST_STEPS = 2, 1, 2
+GROUP = 1
 VMEM_LIMIT = 52 * 2**20
 
 
@@ -283,6 +284,20 @@
     return jnp.where(bit == 1, low, high), jnp.where(bit == 1, high, low)
 
 
+def direct_sum(block, steps, exchange):
+    arrived = [block]
+    for which in range(1, 1 << len(steps)):
+        mask = band_mask = 0
+        for at, (on_basis, on_band) in enumerate(steps):
+            if which >> at & 1:
+                mask, band_mask = mask ^ on_basis, band_mask ^ on_band
+        odd = (mask.bit_count() + band_mask.bit_count()) & 1
+        arrived.append(exchange(block, mask | odd, band_mask))
+    while len(arrived) > 1:
+        arrived = [first + second for first, second in zip(arrived[::2], arrived[1::2])]
+    return arrived[0]
+
+
 def body(basis, band, matching, vectors, weights, gaunt_index, gaunt_value):
     index = lax.axis_index("basis")
     levels = basis.bit_length() - 1
@@ -301,28 +316,25 @@
     leaving, staying_a, matching = first_products(matching, vectors, own, columns // 2)
     arriving = exchange(leaving, 1)
     staying_b = second_products(matching, vectors, own, columns // 2)
-    width = columns // 4
-    sent_a, kept_a = halves(staying_a + arriving[:, :width], bits[1])
-    sent_b, kept_b = halves(staying_b + arriving[:, width:], bits[2])
-    come_a, come_b = exchange(sent_a, 3), exchange(sent_b, 5)
-    sent_a, kept_a = halves(kept_a + come_a, bits[2])
-    sent_b, kept_b = halves(kept_b + come_b, bits[1])
-    come_a, come_b = exchange(sent_a, 5), exchange(sent_b, 3)
-    block = jnp.concatenate([kept_a + come_a, kept_b + come_b], axis=1)
+    width = columns // 8
+    low, high = staying_a + arriving[:, : 2 * width], staying_b + arriving[:, 2 * width :]
+
+    def quarter(first, second):
+        pair = jnp.where(first == 1, high, low)
+        return jnp.where(second == 1, pair[:, width:], pair[:, :width])
+
+    come_b = exchange(quarter(1 - bits[1], 1 - bits[2]), 6)
+    come_x = exchange(quarter(1 - bits[1], bits[2]), 3)
+    come_z = exchange(quarter(bits[1], 1 - bits[2]), 5)
+    block = quarter(bits[1], bits[2]) + come_x + come_z + come_b
     for level in range(3, levels - 1):
         sent, kept = halves(block, bits[level])
         block = kept + exchange(sent, 1 | (1 << level))
     block, weights, gaunt_index, gaunt_value = lax.optimization_barrier((block, weights, gaunt_index, gaunt_value))
     come = exchange(block, 1 | (1 << (levels - 1)))
     tables = gaunt_tables(gaunt_index, gaunt_value, channels // 2)
-    width = columns // 16
-    begin = own * (columns // 2)
-    block_weights = jnp.concatenate(
-        [
-            lax.dynamic_slice_in_dim(weights, begin + (2 * bits[1] + bits[2]) * width, width),
-            lax.dynamic_slice_in_dim(weights, begin + columns // 4 + (2 * bits[2] + bits[1]) * width, width),
-        ]
-    )
+    begin = own * (columns // 2) + (2 * bits[1] + bits[2]) * width
+    block_weights = lax.dynamic_slice_in_dim(weights, begin, width)
     for level in range(3, levels - 1):
         middle = block_weights.shape[0] // 2
         block_weights = jnp.where(bits[level] == 1, block_weights[middle:], block_weights[:middle])
@@ -335,12 +347,10 @@
         which = which ^ ((lax.axis_index("band") >> level) & 1)
     sent = jnp.where(which == 1, top, bottom)
     terms = jnp.where(which == 1, bottom, top) + exchange(sent, 1)
-    step = 1
-    while step < band:
-        terms = terms + exchange(terms, 1, step)
-        step *= 2
-    for level in range(1, levels - 1):
-        terms = terms + exchange(terms, 1 | (1 << level))
+    steps = [(0, 1 << level) for level in range(band.bit_length() - 1)]
+    steps += [(1 << level, 0) for level in range(1, levels - 1)]
+    for at in range(0, len(steps), GROUP):
+        terms = direct_sum(terms, steps[at : at + GROUP], exchange)
     other = exchange(terms, 1)
     top = jnp.where(which == 1, other, terms)
     bottom = jnp.where(which == 1, terms, other)

time: 49.1 us -> 46.6 us (0.949)
  starting transfers between devices: 13.9 us -> 12.3 us
  waiting for transfers between devices: 23.1 us -> 22.3 us
    ppermute x11 -> x10, starting transfers between devices: 13.9 us -> 12.3 us  [exchange(): return lax.ppermute(block, ('basis', 'band'), pairs)]
    ppermute x11 -> x10, waiting for transfers between devices: 23.1 us -> 22.3 us  [exchange(): return lax.ppermute(block, ('basis', 'band'), pairs)]
  transfers between devices with their start and end apart: 11 -> 10, of which waited for: 9 -> 8; matrix products, arithmetic and copies ran while one was open for 2% -> 2% of each run, Pallas kernels for 7% -> 7%
where the time goes in v5:
time: 46.6 us; the launch traced here: 46.4 us
  waiting for transfers between devices  22.3 us (48%)
  starting transfers between devices  12.3 us (26%)
  Pallas kernels  9.51 us (20%)
  local copies, waits for them, and re-layouts  0.79 us (2%)
  between operations  0.77 us (2%)
    ppermute x10, waiting for transfers between devices, exchange(): return lax.ppermute(block, ('basis', 'band'), pairs)  22.3 us
    ppermute x10, starting transfers between devices, exchange(): return lax.ppermute(block, ('basis', 'band'), pairs)  12.3 us
    pallas_call x1, Pallas kernels, first_products(): pl.pallas_call(functools.partial(first_kernel, columns), out_shape=(jax.S...  4.38 us
    pallas_call x1, Pallas kernels, second_products(): pl.pallas_call(functools.partial(second_kernel, columns), out_shape=jax.S...  2.15 us
    pallas_call x1, Pallas kernels, finish(): pl.pallas_call(functools.partial(finish_kernel, tile), out_shape=(jax.Sha...  1.87 us
    pallas_call x1, Pallas kernels, gaunt_tables(): pl.pallas_call(tables_kernel, out_shape=shapes, in_specs=[VMEM, VMEM], ou...  1.11 us
  transfers between devices with their start and end apart: 10, of which 8 were waited for; matrix products, arithmetic and copies ran while one was open for 2% of the time, Pallas kernels for 7%

profile of v5, /device:TPU:0, one launch (start us, length us, event | category | flops | bytes accessed | tf_op | source)
XLA Modules:
  0.0 46.4 jit_solution(7437258316165458734)
XLA Ops:
  0.6 4.4 %first_products.1 = (f32[162,1024]{1,0:T(8,128)S(1)}, f32[162,512]{1,0:T(8,128)S(1)}, bf16[162,2560]{1,0:T(8,128)(2,1)S(1)}) custom-call(s32[1]{0:T(128)} %bitcast.own_ref, bf16[162,2560]{1,0:T(8,128)(2,1)} %matching_hbm.1, bf16[2560,2048]{1,0:T(8,128)(2,1)} %vectors_hbm.3), custom_call_target="tpu_custom_call" | custom-call | flops 1274019840 | bytes 9689088 | tf_op jit(solution)/shard_map/first_products/pallas_call | solution.py:119
  5.0 0.5 collective-permute-start
  5.5 2.1 %second_products.1 = f32[162,512]{1,0:T(8,128)S(1)} custom-call(s32[1]{0:T(128)} %bitcast.own_ref, bf16[162,2560]{1,0:T(8,128)(2,1)S(1)} %get-tuple-element.17.matching, bf16[2560,2048]{1,0:T(8,128)(2,1)} %vectors_hbm.3), custom_call_target="tpu_custom_call" | custom-call | flops 424673280 | bytes 3782656 | tf_op jit(solution)/shard_map/second_products/pallas_call | solution.py:141
  7.7 0.1 broadcast_select_fusion.1
  7.9 2.7 %collective-permute-start.1 = (f32[162,256]{1,0:T(8,128)S(1)}, f32[162,256]{1,0:T(8,128)S(1)}, u32[]{:S(2)}, u32[]{:S(2)}) collective-permute-start(f32[162,256]{1,0:T(8,128)S(1)} %get-tuple-element.34), channel_id=1, source_target_pairs={{0,6},{1,7},{2,4},{3,5},{4,2},{5,3},{6,0},{7,1},{8,14},{9,15},{10,... | collective-permute-start | bytes 497672 | tf_op jit(solution)/shard_map/ppermute | solution.py:314
  10.5 1.5 %collective-permute-start.3 = (f32[162,256]{1,0:T(8,128)S(1)}, f32[162,256]{1,0:T(8,128)S(1)}, u32[]{:S(2)}, u32[]{:S(2)}) collective-permute-start(f32[162,256]{1,0:T(8,128)S(1)} %get-tuple-element.35), channel_id=1, source_target_pairs={{0,12},{1,13},{2,14},{3,15},{4,8},{5,9},{6,10},{7,11},{8,4},{9,5},... | collective-permute-start | bytes 497672 | tf_op jit(solution)/shard_map/ppermute | solution.py:314
  12.2 6.8 %collective-permute-done.1 = f32[162,256]{1,0:T(8,128)S(1)} collective-permute-done((f32[162,256]{1,0:T(8,128)S(1)}, f32[162,256]{1,0:T(8,128)S(1)}, u32[]{:S(2)}, u32[]{:S(2)}) %collective-permute-start.1) | collective-permute-done | bytes 165920 | tf_op jit(solution)/shard_map/ppermute | solution.py:314
  18.9 0.9 %collective-permute-done.2 = f32[162,256]{1,0:T(8,128)S(1)} collective-permute-done((f32[162,256]{1,0:T(8,128)S(1)}, f32[162,256]{1,0:T(8,128)S(1)}, u32[]{:S(2)}, u32[]{:S(2)}) %collective-permute-start.2) | collective-permute-done | bytes 165920 | tf_op jit(solution)/shard_map/ppermute | solution.py:314
  19.9 2.8 %collective-permute-start.4 = (f32[162,256]{1,0:T(8,128)S(1)}, f32[162,256]{1,0:T(8,128)S(1)}, u32[]{:S(2)}, u32[]{:S(2)}) collective-permute-start(f32[162,256]{1,0:T(8,128)S(1)} %add_add_fusion), channel_id=1, source_target_pairs={{0,18},{1,19},{2,16},{3,17},{4,22},{5,23},{6,20},{7,21},{8,26},{9,... | collective-permute-start | bytes 497672 | tf_op jit(solution)/shard_map/ppermute | solution.py:314
  22.7 0.8 %dynamic_slice.3 = f32[256]{0:T(256)S(1)} dynamic-slice(f32[2048]{0:T(1024)} %param.7, s32[]{:T(128)S(6)} %select_n.78), dynamic_slice_sizes={256} | dynamic-slice | bytes 2052 | tf_op jit(solution)/shard_map/dynamic_slice | solution.py:337
  23.5 1.1 %gaunt_tables.1 = (bf16[256,4096]{1,0:T(8,128)(2,1)S(1)}, f32[88,4096]{1,0:T(8,128)S(1)}, bf16[4096,128]{1,0:T(8,128)(2,1)S(1)}) custom-call(s32[3,4096]{1,0:T(4,128)S(1)} %copy-done, f32[1,4096]{1,0:T(1,128)S(1)} %bitcast.2), custom_call_target="tpu_custom_call" | custom-call | flops 8388608 | bytes 5242880 | tf_op jit(solution)/shard_map/gaunt_tables/pallas_call | solution.py:178
  24.6 6.2 %collective-permute-done.4 = f32[162,256]{1,0:T(8,128)S(1)} collective-permute-done((f32[162,256]{1,0:T(8,128)S(1)}, f32[162,256]{1,0:T(8,128)S(1)}, u32[]{:S(2)}, u32[]{:S(2)}) %collective-permute-start.4) | collective-permute-done | bytes 165920 | tf_op jit(solution)/shard_map/ppermute | solution.py:314
  30.8 0.3 fusion
  31.3 0.4 collective-permute-start.5
  31.7 0.9 %collective-permute-done.5 = f32[88,128]{1,0:T(8,128)S(1)} collective-permute-done((f32[88,128]{1,0:T(8,128)S(1)}, f32[88,128]{1,0:T(8,128)S(1)}, u32[]{:S(2)}, u32[]{:S(2)}) %collective-permute-start.5) | collective-permute-done | bytes 45088 | tf_op jit(solution)/shard_map/ppermute | solution.py:314
  32.6 1.5 %collective-permute-start.6 = (f32[88,128]{1,0:T(8,128)S(1)}, f32[88,128]{1,0:T(8,128)S(1)}, u32[]{:S(2)}, u32[]{:S(2)}) collective-permute-start(f32[88,128]{1,0:T(8,128)S(1)} %select_add_fusion), channel_id=1, source_target_pairs={{0,3},{1,2},{2,1},{3,0},{4,7},{5,6},{6,5},{7,4},{8,11},{9,10},{10,... | collective-permute-start | bytes 135176 | tf_op jit(solution)/shard_map/ppermute | solution.py:314
  34.1 2.0 %collective-permute-done.6 = f32[88,128]{1,0:T(8,128)S(1)} collective-permute-done((f32[88,128]{1,0:T(8,128)S(1)}, f32[88,128]{1,0:T(8,128)S(1)}, u32[]{:S(2)}, u32[]{:S(2)}) %collective-permute-start.6) | collective-permute-done | bytes 45088 | tf_op jit(solution)/shard_map/ppermute | solution.py:314
  36.2 1.5 %collective-permute-start.7 = (f32[88,128]{1,0:T(8,128)S(1)}, f32[88,128]{1,0:T(8,128)S(1)}, u32[]{:S(2)}, u32[]{:S(2)}) collective-permute-start(f32[88,128]{1,0:T(8,128)S(1)} %add.53), channel_id=1, source_target_pairs={{0,6},{1,7},{2,4},{3,5},{4,2},{5,3},{6,0},{7,1},{8,14},{9,15},{10,... | collective-permute-start | bytes 135176 | tf_op jit(solution)/shard_map/ppermute | solution.py:314
  37.7 2.0 %collective-permute-done.7 = f32[88,128]{1,0:T(8,128)S(1)} collective-permute-done((f32[88,128]{1,0:T(8,128)S(1)}, f32[88,128]{1,0:T(8,128)S(1)}, u32[]{:S(2)}, u32[]{:S(2)}) %collective-permute-start.7) | collective-permute-done | bytes 45088 | tf_op jit(solution)/shard_map/ppermute | solution.py:314
  39.7 1.0 %collective-permute-start.8 = (f32[88,128]{1,0:T(8,128)S(1)}, f32[88,128]{1,0:T(8,128)S(1)}, u32[]{:S(2)}, u32[]{:S(2)}) collective-permute-start(f32[88,128]{1,0:T(8,128)S(1)} %add.54), channel_id=1, source_target_pairs={{0,10},{1,11},{2,8},{3,9},{4,14},{5,15},{6,12},{7,13},{8,2},{9,3},... | collective-permute-start | bytes 135176 | tf_op jit(solution)/shard_map/ppermute | solution.py:314
  40.7 2.5 %collective-permute-done.8 = f32[88,128]{1,0:T(8,128)S(1)} collective-permute-done((f32[88,128]{1,0:T(8,128)S(1)}, f32[88,128]{1,0:T(8,128)S(1)}, u32[]{:S(2)}, u32[]{:S(2)}) %collective-permute-start.8) | collective-permute-done | bytes 45088 | tf_op jit(solution)/shard_map/ppermute | solution.py:314
  43.2 0.4 collective-permute-start.9
  43.6 0.9 %collective-permute-done.9 = f32[88,128]{1,0:T(8,128)S(1)} collective-permute-done((f32[88,128]{1,0:T(8,128)S(1)}, f32[88,128]{1,0:T(8,128)S(1)}, u32[]{:S(2)}, u32[]{:S(2)}) %collective-permute-start.9) | collective-permute-done | bytes 45088 | tf_op jit(solution)/shard_map/ppermute | solution.py:314
  44.5 1.9 %finish.1 = (f32[162,162]{1,0:T(8,128)}, f32[4,81]{1,0:T(4,128)}) custom-call(f32[88,128]{1,0:T(8,128)S(1)} %get-tuple-element.37.top_ref, f32[88,128]{1,0:T(8,128)S(1)} %get-tuple-element.36.bottom_ref, bf16[256,4096]{1,0:T(8,128)(2,1)S(1)} %get-tuple-element.29.second_ref, f32[88,4096]{1,0:T(8,128)S(1)} %get-tuple-element.30.first_ref, ...), custom_call_target="tpu_custom_call" | custom-call | tf_op jit(solution)/shard_map/finish/pallas_call | solution.py:245
  (21 shorter events, 0.4 us)
Async XLA Ops:
  5.0 2.6 %collective-permute-start = (f32[162,1024]{1,0:T(8,128)S(1)}, f32[162,1024]{1,0:T(8,128)S(1)}, u32[]{:S(2)}, u32[]{:S(2)}) collective-permute-start(f32[162,1024]{1,0:T(8,128)S(1)} %get-tuple-element.18), channel_id=1, source_target_pairs={{0,2},{1,3},{2,0},{3,1},{4,6},{5,7},{6,4},{7,5},{8,10},{9,11},{10,... | collective-permute-start | bytes 1990664 | tf_op jit(solution)/shard_map/ppermute | solution.py:314
  7.7 15.8 %copy-start = (s32[3,4096]{1,0:T(4,128)S(1)}, s32[3,4096]{1,0:T(4,128)}, u32[]{:S(2)}) copy-start(s32[3,4096]{1,0:T(4,128)} %index_ref) | copy-start | bytes 147460
  7.7 15.8 %copy-start.1 = (f32[4096]{0:T(1024)S(1)}, f32[4096]{0:T(1024)}, u32[]{:S(2)}) copy-start(f32[4096]{0:T(1024)} %param.9) | copy-start | bytes 49156
  7.9 11.1 %collective-permute-start.1 = (f32[162,256]{1,0:T(8,128)S(1)}, f32[162,256]{1,0:T(8,128)S(1)}, u32[]{:S(2)}, u32[]{:S(2)}) collective-permute-start(f32[162,256]{1,0:T(8,128)S(1)} %get-tuple-element.34), channel_id=1, source_target_pairs={{0,6},{1,7},{2,4},{3,5},{4,2},{5,3},{6,0},{7,1},{8,14},{9,15},{10,... | collective-permute-start | bytes 497672 | tf_op jit(solution)/shard_map/ppermute | solution.py:314
  10.5 8.4 %collective-permute-start.3 = (f32[162,256]{1,0:T(8,128)S(1)}, f32[162,256]{1,0:T(8,128)S(1)}, u32[]{:S(2)}, u32[]{:S(2)}) collective-permute-start(f32[162,256]{1,0:T(8,128)S(1)} %get-tuple-element.35), channel_id=1, source_target_pairs={{0,12},{1,13},{2,14},{3,15},{4,8},{5,9},{6,10},{7,11},{8,4},{9,5},... | collective-permute-start | bytes 497672 | tf_op jit(solution)/shard_map/ppermute | solution.py:314
  12.1 7.7 %collective-permute-start.2 = (f32[162,256]{1,0:T(8,128)S(1)}, f32[162,256]{1,0:T(8,128)S(1)}, u32[]{:S(2)}, u32[]{:S(2)}) collective-permute-start(f32[162,256]{1,0:T(8,128)S(1)} %slice_select_fusion.2), channel_id=1, source_target_pairs={{0,10},{1,11},{2,8},{3,9},{4,14},{5,15},{6,12},{7,13},{8,2},{9,3},... | collective-permute-start | bytes 497672 | tf_op jit(solution)/shard_map/ppermute | solution.py:314
  19.9 10.9 %collective-permute-start.4 = (f32[162,256]{1,0:T(8,128)S(1)}, f32[162,256]{1,0:T(8,128)S(1)}, u32[]{:S(2)}, u32[]{:S(2)}) collective-permute-start(f32[162,256]{1,0:T(8,128)S(1)} %add_add_fusion), channel_id=1, source_target_pairs={{0,18},{1,19},{2,16},{3,17},{4,22},{5,23},{6,20},{7,21},{8,26},{9,... | collective-permute-start | bytes 497672 | tf_op jit(solution)/shard_map/ppermute | solution.py:314
  31.3 1.3 %collective-permute-start.5 = (f32[88,128]{1,0:T(8,128)S(1)}, f32[88,128]{1,0:T(8,128)S(1)}, u32[]{:S(2)}, u32[]{:S(2)}) collective-permute-start(f32[88,128]{1,0:T(8,128)S(1)} %pad_select_fusion), channel_id=1, source_target_pairs={{0,2},{1,3},{2,0},{3,1},{4,6},{5,7},{6,4},{7,5},{8,10},{9,11},{10,... | collective-permute-start | bytes 135176 | tf_op jit(solution)/shard_map/ppermute | solution.py:314
  32.6 3.5 %collective-permute-start.6 = (f32[88,128]{1,0:T(8,128)S(1)}, f32[88,128]{1,0:T(8,128)S(1)}, u32[]{:S(2)}, u32[]{:S(2)}) collective-permute-start(f32[88,128]{1,0:T(8,128)S(1)} %select_add_fusion), channel_id=1, source_target_pairs={{0,3},{1,2},{2,1},{3,0},{4,7},{5,6},{6,5},{7,4},{8,11},{9,10},{10,... | collective-permute-start | bytes 135176 | tf_op jit(solution)/shard_map/ppermute | solution.py:314
  36.2 3.5 %collective-permute-start.7 = (f32[88,128]{1,0:T(8,128)S(1)}, f32[88,128]{1,0:T(8,128)S(1)}, u32[]{:S(2)}, u32[]{:S(2)}) collective-permute-start(f32[88,128]{1,0:T(8,128)S(1)} %add.53), channel_id=1, source_target_pairs={{0,6},{1,7},{2,4},{3,5},{4,2},{5,3},{6,0},{7,1},{8,14},{9,15},{10,... | collective-permute-start | bytes 135176 | tf_op jit(solution)/shard_map/ppermute | solution.py:314
  39.7 3.5 %collective-permute-start.8 = (f32[88,128]{1,0:T(8,128)S(1)}, f32[88,128]{1,0:T(8,128)S(1)}, u32[]{:S(2)}, u32[]{:S(2)}) collective-permute-start(f32[88,128]{1,0:T(8,128)S(1)} %add.54), channel_id=1, source_target_pairs={{0,10},{1,11},{2,8},{3,9},{4,14},{5,15},{6,12},{7,13},{8,2},{9,3},... | collective-permute-start | bytes 135176 | tf_op jit(solution)/shard_map/ppermute | solution.py:314
  43.2 1.3 %collective-permute-start.9 = (f32[88,128]{1,0:T(8,128)S(1)}, f32[88,128]{1,0:T(8,128)S(1)}, u32[]{:S(2)}, u32[]{:S(2)}) collective-permute-start(f32[88,128]{1,0:T(8,128)S(1)} %add.55), channel_id=1, source_target_pairs={{0,2},{1,3},{2,0},{3,1},{4,6},{5,7},{6,4},{7,5},{8,10},{9,11},{10,... | collective-permute-start | bytes 135176 | tf_op jit(solution)/shard_map/ppermute | solution.py:314

commit v6 on v5

--- a/solution.py
+++ b/solution.py
@@ -10,7 +10,7 @@
 LANES = 128
 TILE = 1024
 LEAVING_STEPS, STAYING_STEPS, LAST_STEPS = 2, 1, 2
-GROUP = 1
+GROUP = 2
 VMEM_LIMIT = 52 * 2**20
 
 
@@ -291,7 +291,7 @@
         for at, (on_basis, on_band) in enumerate(steps):
             if which >> at & 1:
                 mask, band_mask = mask ^ on_basis, band_mask ^ on_band
-        odd = (mask.bit_count() + band_mask.bit_count()) & 1
+        odd = mask.bit_count() & 1
         arrived.append(exchange(block, mask | odd, band_mask))
     while len(arrived) > 1:
         arrived = [first + second for first, second in zip(arrived[::2], arrived[1::2])]
@@ -343,11 +343,11 @@
 
     top, bottom = pack(weighted_pairs(block, block_weights))
     which = own
-    for level in range(band.bit_length() - 1):
-        which = which ^ ((lax.axis_index("band") >> level) & 1)
-    sent = jnp.where(which == 1, top, bottom)
-    terms = jnp.where(which == 1, bottom, top) + exchange(sent, 1)
-    steps = [(0, 1 << level) for level in range(band.bit_length() - 1)]
+    mine, rest = jnp.where(which == 1, bottom, top), jnp.where(which == 1, top, bottom)
+    terms = mine + exchange(rest, 1)
+    if band > 1:
+        terms = terms + (exchange(mine, 0, 1) + exchange(rest, 1, 1))
+    steps = [(0, 1 << level) for level in range(1, band.bit_length() - 1)]
     steps += [(1 << level, 0) for level in range(1, levels - 1)]
     for at in range(0, len(steps), GROUP):
         terms = direct_sum(terms, steps[at : at + GROUP], exchange)

time: 46.6 us -> 46.3 us (level)
  waiting for transfers between devices: 22.3 us -> 21.4 us
  starting transfers between devices: 12.3 us -> 12.9 us
    ppermute x10 -> x12, waiting for transfers between devices: 22.3 us -> 21.4 us  [exchange(): return lax.ppermute(block, ('basis', 'band'), pairs)]
    ppermute x10 -> x12, starting transfers between devices: 12.3 us -> 12.9 us  [exchange(): return lax.ppermute(block, ('basis', 'band'), pairs)]
  transfers between devices with their start and end apart: 10 -> 12, of which waited for: 8 -> 8; matrix products, arithmetic and copies ran while one was open for 2% -> 2% of each run, Pallas kernels for 7% -> 7%
where the time goes in v6:
time: 46.3 us; the launch traced here: 46.1 us
  waiting for transfers between devices  21.4 us (46%)
  starting transfers between devices  12.9 us (28%)
  Pallas kernels  9.51 us (21%)
  local copies, waits for them, and re-layouts  0.79 us (2%)
  between operations  0.77 us (2%)
    ppermute x12, waiting for transfers between devices, exchange(): return lax.ppermute(block, ('basis', 'band'), pairs)  21.4 us
    ppermute x12, starting transfers between devices, exchange(): return lax.ppermute(block, ('basis', 'band'), pairs)  12.9 us
    pallas_call x1, Pallas kernels, first_products(): pl.pallas_call(functools.partial(first_kernel, columns), out_shape=(jax.S...  4.38 us
    pallas_call x1, Pallas kernels, second_products(): pl.pallas_call(functools.partial(second_kernel, columns), out_shape=jax.S...  2.15 us
    pallas_call x1, Pallas kernels, finish(): pl.pallas_call(functools.partial(finish_kernel, tile), out_shape=(jax.Sha...  1.87 us
    pallas_call x1, Pallas kernels, gaunt_tables(): pl.pallas_call(tables_kernel, out_shape=shapes, in_specs=[VMEM, VMEM], ou...  1.11 us
  transfers between devices with their start and end apart: 12, of which 8 were waited for; matrix products, arithmetic and copies ran while one was open for 2% of the time, Pallas kernels for 7%

profile of v6, /device:TPU:0, one launch (start us, length us, event | category | flops | bytes accessed | tf_op | source)
XLA Modules:
  0.0 46.1 jit_solution(8317328114176048020)
XLA Ops:
  0.6 4.4 %first_products.1 = (f32[162,1024]{1,0:T(8,128)S(1)}, f32[162,512]{1,0:T(8,128)S(1)}, bf16[162,2560]{1,0:T(8,128)(2,1)S(1)}) custom-call(s32[1]{0:T(128)} %bitcast.own_ref, bf16[162,2560]{1,0:T(8,128)(2,1)} %matching_hbm.1, bf16[2560,2048]{1,0:T(8,128)(2,1)} %vectors_hbm.3), custom_call_target="tpu_custom_call" | custom-call | flops 1274019840 | bytes 9689088 | tf_op jit(solution)/shard_map/first_products/pallas_call | solution.py:119
  5.0 0.5 %collective-permute-start = (f32[162,1024]{1,0:T(8,128)S(1)}, f32[162,1024]{1,0:T(8,128)S(1)}, u32[]{:S(2)}, u32[]{:S(2)}) collective-permute-start(f32[162,1024]{1,0:T(8,128)S(1)} %get-tuple-element.18), channel_id=1, source_target_pairs={{0,2},{1,3},{2,0},{3,1},{4,6},{5,7},{6,4},{7,5},{8,10},{9,11},{10,... | collective-permute-start | bytes 1990664 | tf_op jit(solution)/shard_map/ppermute | solution.py:314
  5.5 2.1 %second_products.1 = f32[162,512]{1,0:T(8,128)S(1)} custom-call(s32[1]{0:T(128)} %bitcast.own_ref, bf16[162,2560]{1,0:T(8,128)(2,1)S(1)} %get-tuple-element.17.matching, bf16[2560,2048]{1,0:T(8,128)(2,1)} %vectors_hbm.3), custom_call_target="tpu_custom_call" | custom-call | flops 424673280 | bytes 3782656 | tf_op jit(solution)/shard_map/second_products/pallas_call | solution.py:141
  7.7 0.1 broadcast_select_fusion.1
  7.9 2.7 %collective-permute-start.1 = (f32[162,256]{1,0:T(8,128)S(1)}, f32[162,256]{1,0:T(8,128)S(1)}, u32[]{:S(2)}, u32[]{:S(2)}) collective-permute-start(f32[162,256]{1,0:T(8,128)S(1)} %get-tuple-element.34), channel_id=1, source_target_pairs={{0,6},{1,7},{2,4},{3,5},{4,2},{5,3},{6,0},{7,1},{8,14},{9,15},{10,... | collective-permute-start | bytes 497672 | tf_op jit(solution)/shard_map/ppermute | solution.py:314
  10.5 1.5 %collective-permute-start.3 = (f32[162,256]{1,0:T(8,128)S(1)}, f32[162,256]{1,0:T(8,128)S(1)}, u32[]{:S(2)}, u32[]{:S(2)}) collective-permute-start(f32[162,256]{1,0:T(8,128)S(1)} %get-tuple-element.35), channel_id=1, source_target_pairs={{0,12},{1,13},{2,14},{3,15},{4,8},{5,9},{6,10},{7,11},{8,4},{9,5},... | collective-permute-start | bytes 497672 | tf_op jit(solution)/shard_map/ppermute | solution.py:314
  12.2 6.8 %collective-permute-done.1 = f32[162,256]{1,0:T(8,128)S(1)} collective-permute-done((f32[162,256]{1,0:T(8,128)S(1)}, f32[162,256]{1,0:T(8,128)S(1)}, u32[]{:S(2)}, u32[]{:S(2)}) %collective-permute-start.1) | collective-permute-done | bytes 165920 | tf_op jit(solution)/shard_map/ppermute | solution.py:314
  18.9 0.9 %collective-permute-done.2 = f32[162,256]{1,0:T(8,128)S(1)} collective-permute-done((f32[162,256]{1,0:T(8,128)S(1)}, f32[162,256]{1,0:T(8,128)S(1)}, u32[]{:S(2)}, u32[]{:S(2)}) %collective-permute-start.2) | collective-permute-done | bytes 165920 | tf_op jit(solution)/shard_map/ppermute | solution.py:314
  19.9 2.8 %collective-permute-start.4 = (f32[162,256]{1,0:T(8,128)S(1)}, f32[162,256]{1,0:T(8,128)S(1)}, u32[]{:S(2)}, u32[]{:S(2)}) collective-permute-start(f32[162,256]{1,0:T(8,128)S(1)} %add_add_fusion), channel_id=1, source_target_pairs={{0,18},{1,19},{2,16},{3,17},{4,22},{5,23},{6,20},{7,21},{8,26},{9,... | collective-permute-start | bytes 497672 | tf_op jit(solution)/shard_map/ppermute | solution.py:314
  22.7 0.8 %dynamic_slice.3 = f32[256]{0:T(256)S(1)} dynamic-slice(f32[2048]{0:T(1024)} %param.7, s32[]{:T(128)S(6)} %select_n.78), dynamic_slice_sizes={256} | dynamic-slice | bytes 2052 | tf_op jit(solution)/shard_map/dynamic_slice | solution.py:337
  23.5 1.1 %gaunt_tables.1 = (bf16[256,4096]{1,0:T(8,128)(2,1)S(1)}, f32[88,4096]{1,0:T(8,128)S(1)}, bf16[4096,128]{1,0:T(8,128)(2,1)S(1)}) custom-call(s32[3,4096]{1,0:T(4,128)S(1)} %copy-done, f32[1,4096]{1,0:T(1,128)S(1)} %bitcast.2), custom_call_target="tpu_custom_call" | custom-call | flops 8388608 | bytes 5242880 | tf_op jit(solution)/shard_map/gaunt_tables/pallas_call | solution.py:178
  24.6 6.2 %collective-permute-done.4 = f32[162,256]{1,0:T(8,128)S(1)} collective-permute-done((f32[162,256]{1,0:T(8,128)S(1)}, f32[162,256]{1,0:T(8,128)S(1)}, u32[]{:S(2)}, u32[]{:S(2)}) %collective-permute-start.4) | collective-permute-done | bytes 165920 | tf_op jit(solution)/shard_map/ppermute | solution.py:314
  30.8 0.3 fusion
  31.3 0.4 collective-permute-start.5
  31.7 1.5 %collective-permute-start.6 = (f32[88,128]{1,0:T(8,128)S(1)}, f32[88,128]{1,0:T(8,128)S(1)}, u32[]{:S(2)}, u32[]{:S(2)}) collective-permute-start(f32[88,128]{1,0:T(8,128)S(1)} %get-tuple-element.37), channel_id=1, source_target_pairs={{0,1},{1,0},{2,3},{3,2},{4,5},{5,4},{6,7},{7,6},{8,9},{9,8},{10,11... | collective-permute-start | bytes 135176 | tf_op jit(solution)/shard_map/ppermute | solution.py:314
  33.3 2.5 %collective-permute-done.6 = f32[88,128]{1,0:T(8,128)S(1)} collective-permute-done((f32[88,128]{1,0:T(8,128)S(1)}, f32[88,128]{1,0:T(8,128)S(1)}, u32[]{:S(2)}, u32[]{:S(2)}) %collective-permute-start.6) | collective-permute-done | bytes 45088 | tf_op jit(solution)/shard_map/ppermute | solution.py:314
  35.7 1.4 %collective-permute-done.7 = f32[88,128]{1,0:T(8,128)S(1)} collective-permute-done((f32[88,128]{1,0:T(8,128)S(1)}, f32[88,128]{1,0:T(8,128)S(1)}, u32[]{:S(2)}, u32[]{:S(2)}) %collective-permute-start.7) | collective-permute-done | bytes 45088 | tf_op jit(solution)/shard_map/ppermute | solution.py:314
  37.2 1.3 %collective-permute-start.10 = (f32[88,128]{1,0:T(8,128)S(1)}, f32[88,128]{1,0:T(8,128)S(1)}, u32[]{:S(2)}, u32[]{:S(2)}) collective-permute-start(f32[88,128]{1,0:T(8,128)S(1)} %add_add_fusion.2), channel_id=1, source_target_pairs={{0,12},{1,13},{2,14},{3,15},{4,8},{5,9},{6,10},{7,11},{8,4},{9,5},... | collective-permute-start | bytes 135176 | tf_op jit(solution)/shard_map/ppermute | solution.py:314
  38.6 1.9 %collective-permute-start.9 = (f32[88,128]{1,0:T(8,128)S(1)}, f32[88,128]{1,0:T(8,128)S(1)}, u32[]{:S(2)}, u32[]{:S(2)}) collective-permute-start(f32[88,128]{1,0:T(8,128)S(1)} %add_add_fusion.2), channel_id=1, source_target_pairs={{0,10},{1,11},{2,8},{3,9},{4,14},{5,15},{6,12},{7,13},{8,2},{9,3},... | collective-permute-start | bytes 135176 | tf_op jit(solution)/shard_map/ppermute | solution.py:314
  40.4 1.8 %collective-permute-done.10 = f32[88,128]{1,0:T(8,128)S(1)} collective-permute-done((f32[88,128]{1,0:T(8,128)S(1)}, f32[88,128]{1,0:T(8,128)S(1)}, u32[]{:S(2)}, u32[]{:S(2)}) %collective-permute-start.10) | collective-permute-done | bytes 45088 | tf_op jit(solution)/shard_map/ppermute | solution.py:314
  42.3 0.6 %collective-permute-done.8 = f32[88,128]{1,0:T(8,128)S(1)} collective-permute-done((f32[88,128]{1,0:T(8,128)S(1)}, f32[88,128]{1,0:T(8,128)S(1)}, u32[]{:S(2)}, u32[]{:S(2)}) %collective-permute-start.8) | collective-permute-done | bytes 45088 | tf_op jit(solution)/shard_map/ppermute | solution.py:314
  42.9 0.2 collective-permute-start.11
  43.1 1.1 %collective-permute-done.11 = f32[88,128]{1,0:T(8,128)S(1)} collective-permute-done((f32[88,128]{1,0:T(8,128)S(1)}, f32[88,128]{1,0:T(8,128)S(1)}, u32[]{:S(2)}, u32[]{:S(2)}) %collective-permute-start.11) | collective-permute-done | bytes 45088 | tf_op jit(solution)/shard_map/ppermute | solution.py:314
  44.2 1.9 %finish.1 = (f32[162,162]{1,0:T(8,128)}, f32[4,81]{1,0:T(4,128)}) custom-call(f32[88,128]{1,0:T(8,128)S(1)} %get-tuple-element.39.top_ref, f32[88,128]{1,0:T(8,128)S(1)} %get-tuple-element.38.bottom_ref, bf16[256,4096]{1,0:T(8,128)(2,1)S(1)} %get-tuple-element.29.second_ref, f32[88,4096]{1,0:T(8,128)S(1)} %get-tuple-element.30.first_ref, ...), custom_call_target="tpu_custom_call" | custom-call | tf_op jit(solution)/shard_map/finish/pallas_call | solution.py:245
  (23 shorter events, 0.5 us)
Async XLA Ops:
  5.0 2.6 %collective-permute-start = (f32[162,1024]{1,0:T(8,128)S(1)}, f32[162,1024]{1,0:T(8,128)S(1)}, u32[]{:S(2)}, u32[]{:S(2)}) collective-permute-start(f32[162,1024]{1,0:T(8,128)S(1)} %get-tuple-element.18), channel_id=1, source_target_pairs={{0,2},{1,3},{2,0},{3,1},{4,6},{5,7},{6,4},{7,5},{8,10},{9,11},{10,... | collective-permute-start | bytes 1990664 | tf_op jit(solution)/shard_map/ppermute | solution.py:314
  7.7 15.8 %copy-start = (s32[3,4096]{1,0:T(4,128)S(1)}, s32[3,4096]{1,0:T(4,128)}, u32[]{:S(2)}) copy-start(s32[3,4096]{1,0:T(4,128)} %index_ref) | copy-start | bytes 147460
  7.7 15.8 %copy-start.1 = (f32[4096]{0:T(1024)S(1)}, f32[4096]{0:T(1024)}, u32[]{:S(2)}) copy-start(f32[4096]{0:T(1024)} %param.9) | copy-start | bytes 49156
  7.9 11.1 %collective-permute-start.1 = (f32[162,256]{1,0:T(8,128)S(1)}, f32[162,256]{1,0:T(8,128)S(1)}, u32[]{:S(2)}, u32[]{:S(2)}) collective-permute-start(f32[162,256]{1,0:T(8,128)S(1)} %get-tuple-element.34), channel_id=1, source_target_pairs={{0,6},{1,7},{2,4},{3,5},{4,2},{5,3},{6,0},{7,1},{8,14},{9,15},{10,... | collective-permute-start | bytes 497672 | tf_op jit(solution)/shard_map/ppermute | solution.py:314
  10.5 8.4 %collective-permute-start.3 = (f32[162,256]{1,0:T(8,128)S(1)}, f32[162,256]{1,0:T(8,128)S(1)}, u32[]{:S(2)}, u32[]{:S(2)}) collective-permute-start(f32[162,256]{1,0:T(8,128)S(1)} %get-tuple-element.35), channel_id=1, source_target_pairs={{0,12},{1,13},{2,14},{3,15},{4,8},{5,9},{6,10},{7,11},{8,4},{9,5},... | collective-permute-start | bytes 497672 | tf_op jit(solution)/shard_map/ppermute | solution.py:314
  12.1 7.7 %collective-permute-start.2 = (f32[162,256]{1,0:T(8,128)S(1)}, f32[162,256]{1,0:T(8,128)S(1)}, u32[]{:S(2)}, u32[]{:S(2)}) collective-permute-start(f32[162,256]{1,0:T(8,128)S(1)} %slice_select_fusion.2), channel_id=1, source_target_pairs={{0,10},{1,11},{2,8},{3,9},{4,14},{5,15},{6,12},{7,13},{8,2},{9,3},... | collective-permute-start | bytes 497672 | tf_op jit(solution)/shard_map/ppermute | solution.py:314
  19.9 10.9 %collective-permute-start.4 = (f32[162,256]{1,0:T(8,128)S(1)}, f32[162,256]{1,0:T(8,128)S(1)}, u32[]{:S(2)}, u32[]{:S(2)}) collective-permute-start(f32[162,256]{1,0:T(8,128)S(1)} %add_add_fusion), channel_id=1, source_target_pairs={{0,18},{1,19},{2,16},{3,17},{4,22},{5,23},{6,20},{7,21},{8,26},{9,... | collective-permute-start | bytes 497672 | tf_op jit(solution)/shard_map/ppermute | solution.py:314
  31.3 1.9 %collective-permute-start.5 = (f32[88,128]{1,0:T(8,128)S(1)}, f32[88,128]{1,0:T(8,128)S(1)}, u32[]{:S(2)}, u32[]{:S(2)}) collective-permute-start(f32[88,128]{1,0:T(8,128)S(1)} %get-tuple-element.36), channel_id=1, source_target_pairs={{0,2},{1,3},{2,0},{3,1},{4,6},{5,7},{6,4},{7,5},{8,10},{9,11},{10,... | collective-permute-start | bytes 135176 | tf_op jit(solution)/shard_map/ppermute | solution.py:314
  31.7 4.0 %collective-permute-start.6 = (f32[88,128]{1,0:T(8,128)S(1)}, f32[88,128]{1,0:T(8,128)S(1)}, u32[]{:S(2)}, u32[]{:S(2)}) collective-permute-start(f32[88,128]{1,0:T(8,128)S(1)} %get-tuple-element.37), channel_id=1, source_target_pairs={{0,1},{1,0},{2,3},{3,2},{4,5},{5,4},{6,7},{7,6},{8,9},{9,8},{10,11... | collective-permute-start | bytes 135176 | tf_op jit(solution)/shard_map/ppermute | solution.py:314
  33.2 3.9 %collective-permute-start.7 = (f32[88,128]{1,0:T(8,128)S(1)}, f32[88,128]{1,0:T(8,128)S(1)}, u32[]{:S(2)}, u32[]{:S(2)}) collective-permute-start(f32[88,128]{1,0:T(8,128)S(1)} %get-tuple-element.36), channel_id=1, source_target_pairs={{0,3},{1,2},{2,1},{3,0},{4,7},{5,6},{6,5},{7,4},{8,11},{9,10},{10,... | collective-permute-start | bytes 135176 | tf_op jit(solution)/shard_map/ppermute | solution.py:314
  37.2 5.1 %collective-permute-start.10 = (f32[88,128]{1,0:T(8,128)S(1)}, f32[88,128]{1,0:T(8,128)S(1)}, u32[]{:S(2)}, u32[]{:S(2)}) collective-permute-start(f32[88,128]{1,0:T(8,128)S(1)} %add_add_fusion.2), channel_id=1, source_target_pairs={{0,12},{1,13},{2,14},{3,15},{4,8},{5,9},{6,10},{7,11},{8,4},{9,5},... | collective-permute-start | bytes 135176 | tf_op jit(solution)/shard_map/ppermute | solution.py:314
  38.5 4.4 %collective-permute-start.8 = (f32[88,128]{1,0:T(8,128)S(1)}, f32[88,128]{1,0:T(8,128)S(1)}, u32[]{:S(2)}, u32[]{:S(2)}) collective-permute-start(f32[88,128]{1,0:T(8,128)S(1)} %add_add_fusion.2), channel_id=1, source_target_pairs={{0,6},{1,7},{2,4},{3,5},{4,2},{5,3},{6,0},{7,1},{8,14},{9,15},{10,... | collective-permute-start | bytes 135176 | tf_op jit(solution)/shard_map/ppermute | solution.py:314
  38.6 4.3 %collective-permute-start.9 = (f32[88,128]{1,0:T(8,128)S(1)}, f32[88,128]{1,0:T(8,128)S(1)}, u32[]{:S(2)}, u32[]{:S(2)}) collective-permute-start(f32[88,128]{1,0:T(8,128)S(1)} %add_add_fusion.2), channel_id=1, source_target_pairs={{0,10},{1,11},{2,8},{3,9},{4,14},{5,15},{6,12},{7,13},{8,2},{9,3},... | collective-permute-start | bytes 135176 | tf_op jit(solution)/shard_map/ppermute | solution.py:314
  42.9 1.3 %collective-permute-start.11 = (f32[88,128]{1,0:T(8,128)S(1)}, f32[88,128]{1,0:T(8,128)S(1)}, u32[]{:S(2)}, u32[]{:S(2)}) collective-permute-start(f32[88,128]{1,0:T(8,128)S(1)} %add_add_fusion.1), channel_id=1, source_target_pairs={{0,2},{1,3},{2,0},{3,1},{4,6},{5,7},{6,4},{7,5},{8,10},{9,11},{10,... | collective-permute-start | bytes 135176 | tf_op jit(solution)/shard_map/ppermute | solution.py:314

commit v7 on v6

--- a/solution.py
+++ b/solution.py
@@ -8,6 +8,7 @@
 from jax.sharding import PartitionSpec as P
 
 LANES = 128
+SPILL_LOW, SPILL_HIGH = 48, 56
 TILE = 1024
 LEAVING_STEPS, STAYING_STEPS, LAST_STEPS = 2, 1, 2
 GROUP = 2
@@ -196,19 +197,22 @@
     harmonics = channels // 2
     extra = channels - LANES
     half = top_ref.shape[0]
+    spill = channels - 2 * half
     upper = jnp.concatenate([top_ref[...], bottom_ref[: LANES - half, :]], axis=0)
     rest = bottom_ref[LANES - half :, :]
     rows = lax.broadcasted_iota(jnp.int32, (LANES, LANES), 0)
     lanes = lax.broadcasted_iota(jnp.int32, (LANES, LANES), 1)
-    corner_there = (rows < extra) & (lanes >= LANES // 2) & (lanes < LANES // 2 + extra)
-    tall = jnp.concatenate([rest, jnp.zeros((LANES - rest.shape[0], LANES), jnp.float32)], axis=0)
-    corner = pltpu.roll(upper, LANES // 2, 1)
-    full[:LANES, :LANES] = jnp.where(corner_there, jnp.transpose(upper), upper)
+    borrowed = (rows < LANES // 2) & (lanes >= LANES // 2)
+    turned = pltpu.roll(upper, LANES // 2, 1)
+    last = jnp.where(lanes[:8] < LANES // 2, turned[SPILL_LOW : SPILL_LOW + 8], upper[SPILL_HIGH : SPILL_HIGH + 8])
+    last = jnp.where(rows[:8] < spill, last, 0.0)
+    blank = jnp.zeros((LANES - rest.shape[0] - 8, LANES), jnp.float32)
+    tall = jnp.concatenate([rest, last, blank], axis=0)
+    full[:LANES, :LANES] = jnp.where(borrowed, jnp.transpose(upper), upper)
     full[:LANES, LANES:] = jnp.transpose(tall)
-    full[LANES:, :LANES] = jnp.zeros((full.shape[0] - LANES, LANES), jnp.float32)
-    full[LANES : LANES + rest.shape[0], :LANES] = rest
+    full[LANES:, :LANES] = tall[: full.shape[0] - LANES]
     full[LANES:, LANES:] = jnp.zeros((full.shape[0] - LANES, LANES), jnp.float32)
-    full[LANES:channels, LANES:] = corner[:extra]
+    full[LANES:channels, LANES:] = turned[:extra]
     matrix_ref[...] = full[:channels, :channels]
 
     height = first_ref.shape[0]
@@ -258,16 +262,23 @@
 
 def pack(matrix):
     channels = matrix.shape[0]
-    extra = channels - LANES
     half = LANES // 2
-    corner = jnp.pad(matrix[LANES:, LANES:], ((0, channels - extra), (half, LANES - half - extra)))
-    rows = lax.broadcasted_iota(jnp.int32, (channels, LANES), 0)
-    lanes = lax.broadcasted_iota(jnp.int32, (channels, LANES), 1)
-    there = (rows < extra) & (lanes >= half) & (lanes < half + extra)
-    packed = jnp.where(there, corner, matrix[:, :LANES])
-    height = round_up(channels, 16) // 2
-    height = round_up(height, 8)
-    return packed[:height], jnp.pad(packed[height:], ((0, 2 * height - channels), (0, 0)))
+    height = channels // 16 * 8
+
+    def placed(part, row, lane):
+        sizes = ((row, 2 * height - row - part.shape[0]), (lane, LANES - lane - part.shape[1]))
+        return jnp.pad(part, sizes)
+
+    last = matrix[2 * height :, :LANES]
+    moved = (
+        placed(matrix[LANES:, LANES:], 0, half)
+        + placed(last[:, :half], SPILL_LOW, half)
+        + placed(last[:, half:], SPILL_HIGH, half)
+    )
+    rows = lax.broadcasted_iota(jnp.int32, moved.shape, 0)
+    lanes = lax.broadcasted_iota(jnp.int32, moved.shape, 1)
+    packed = jnp.where((rows < half) & (lanes >= half), moved, matrix[: 2 * height, :LANES])
+    return packed[:height], packed[height:]
 
 
 def plain_body(matching, vectors, weights, gaunt_index, gaunt_value):
@@ -365,7 +376,7 @@
         columns = arrays[1].shape[1]
         powers = basis & (basis - 1) == 0 and band & (band - 1) == 0 and basis >= 16
         sizes = columns % (16 * LANES) == 0 and depth % 256 == 0
-        if powers and sizes and channels % 2 == 0 and LANES < channels <= LANES + LANES // 2:
+        if powers and sizes and channels % 2 == 0 and LANES + 16 <= channels <= LANES + 40 and channels % 16 <= 8:
             return body(basis, band, *arrays)
         return plain_body(*arrays)
 

time: 46.3 us -> 46.1 us (level)
  no operation moved by 1% of the time
where the time goes in v7:
time: 46.1 us; the launch traced here: 45.9 us
  waiting for transfers between devices  21.1 us (46%)
  starting transfers between devices  12.9 us (28%)
  Pallas kernels  9.48 us (21%)
  local copies, waits for them, and re-layouts  0.85 us (2%)
  between operations  0.76 us (2%)
    ppermute x12, waiting for transfers between devices, exchange(): return lax.ppermute(block, ('basis', 'band'), pairs)  21.1 us
    ppermute x12, starting transfers between devices, exchange(): return lax.ppermute(block, ('basis', 'band'), pairs)  12.9 us
    pallas_call x1, Pallas kernels, first_products(): pl.pallas_call(functools.partial(first_kernel, columns), out_shape=(jax.S...  4.38 us
    pallas_call x1, Pallas kernels, second_products(): pl.pallas_call(functools.partial(second_kernel, columns), out_shape=jax.S...  2.15 us
    pallas_call x1, Pallas kernels, finish(): pl.pallas_call(functools.partial(finish_kernel, tile), out_shape=(jax.Sha...  1.84 us
    pallas_call x1, Pallas kernels, gaunt_tables(): pl.pallas_call(tables_kernel, out_shape=shapes, in_specs=[VMEM, VMEM], ou...  1.11 us
  transfers between devices with their start and end apart: 12, of which 8 were waited for; matrix products, arithmetic and copies ran while one was open for 2% of the time, Pallas kernels for 7%

profile of v7, /device:TPU:0, one launch (start us, length us, event | category | flops | bytes accessed | tf_op | source)
XLA Modules:
  0.0 45.9 jit_solution(9387531557552441972)
XLA Ops:
  0.6 4.4 %first_products.1 = (f32[162,1024]{1,0:T(8,128)S(1)}, f32[162,512]{1,0:T(8,128)S(1)}, bf16[162,2560]{1,0:T(8,128)(2,1)S(1)}) custom-call(s32[1]{0:T(128)} %bitcast.own_ref, bf16[162,2560]{1,0:T(8,128)(2,1)} %matching_hbm.1, bf16[2560,2048]{1,0:T(8,128)(2,1)} %vectors_hbm.3), custom_call_target="tpu_custom_call" | custom-call | flops 1274019840 | bytes 9689088 | tf_op jit(solution)/shard_map/first_products/pallas_call | solution.py:120
  5.0 0.5 %collective-permute-start = (f32[162,1024]{1,0:T(8,128)S(1)}, f32[162,1024]{1,0:T(8,128)S(1)}, u32[]{:S(2)}, u32[]{:S(2)}) collective-permute-start(f32[162,1024]{1,0:T(8,128)S(1)} %get-tuple-element.18), channel_id=1, source_target_pairs={{0,2},{1,3},{2,0},{3,1},{4,6},{5,7},{6,4},{7,5},{8,10},{9,11},{10,... | collective-permute-start | bytes 1990664 | tf_op jit(solution)/shard_map/ppermute | solution.py:325
  5.5 2.1 %second_products.1 = f32[162,512]{1,0:T(8,128)S(1)} custom-call(s32[1]{0:T(128)} %bitcast.own_ref, bf16[162,2560]{1,0:T(8,128)(2,1)S(1)} %get-tuple-element.17.matching, bf16[2560,2048]{1,0:T(8,128)(2,1)} %vectors_hbm.3), custom_call_target="tpu_custom_call" | custom-call | flops 424673280 | bytes 3782656 | tf_op jit(solution)/shard_map/second_products/pallas_call | solution.py:142
  7.7 0.1 broadcast_select_fusion.1
  7.9 2.7 %collective-permute-start.1 = (f32[162,256]{1,0:T(8,128)S(1)}, f32[162,256]{1,0:T(8,128)S(1)}, u32[]{:S(2)}, u32[]{:S(2)}) collective-permute-start(f32[162,256]{1,0:T(8,128)S(1)} %get-tuple-element.34), channel_id=1, source_target_pairs={{0,6},{1,7},{2,4},{3,5},{4,2},{5,3},{6,0},{7,1},{8,14},{9,15},{10,... | collective-permute-start | bytes 497672 | tf_op jit(solution)/shard_map/ppermute | solution.py:325
  10.5 1.5 %collective-permute-start.3 = (f32[162,256]{1,0:T(8,128)S(1)}, f32[162,256]{1,0:T(8,128)S(1)}, u32[]{:S(2)}, u32[]{:S(2)}) collective-permute-start(f32[162,256]{1,0:T(8,128)S(1)} %get-tuple-element.35), channel_id=1, source_target_pairs={{0,12},{1,13},{2,14},{3,15},{4,8},{5,9},{6,10},{7,11},{8,4},{9,5},... | collective-permute-start | bytes 497672 | tf_op jit(solution)/shard_map/ppermute | solution.py:325
  12.2 6.8 %collective-permute-done.1 = f32[162,256]{1,0:T(8,128)S(1)} collective-permute-done((f32[162,256]{1,0:T(8,128)S(1)}, f32[162,256]{1,0:T(8,128)S(1)}, u32[]{:S(2)}, u32[]{:S(2)}) %collective-permute-start.1) | collective-permute-done | bytes 165920 | tf_op jit(solution)/shard_map/ppermute | solution.py:325
  18.9 0.9 %collective-permute-done.2 = f32[162,256]{1,0:T(8,128)S(1)} collective-permute-done((f32[162,256]{1,0:T(8,128)S(1)}, f32[162,256]{1,0:T(8,128)S(1)}, u32[]{:S(2)}, u32[]{:S(2)}) %collective-permute-start.2) | collective-permute-done | bytes 165920 | tf_op jit(solution)/shard_map/ppermute | solution.py:325
  19.9 2.8 %collective-permute-start.4 = (f32[162,256]{1,0:T(8,128)S(1)}, f32[162,256]{1,0:T(8,128)S(1)}, u32[]{:S(2)}, u32[]{:S(2)}) collective-permute-start(f32[162,256]{1,0:T(8,128)S(1)} %add_add_fusion), channel_id=1, source_target_pairs={{0,18},{1,19},{2,16},{3,17},{4,22},{5,23},{6,20},{7,21},{8,26},{9,... | collective-permute-start | bytes 497672 | tf_op jit(solution)/shard_map/ppermute | solution.py:325
  22.7 0.8 %dynamic_slice.3 = f32[256]{0:T(256)S(1)} dynamic-slice(f32[2048]{0:T(1024)} %param.7, s32[]{:T(128)S(6)} %select_n.78), dynamic_slice_sizes={256} | dynamic-slice | bytes 2052 | tf_op jit(solution)/shard_map/dynamic_slice | solution.py:348
  23.5 1.1 %gaunt_tables.1 = (bf16[256,4096]{1,0:T(8,128)(2,1)S(1)}, f32[88,4096]{1,0:T(8,128)S(1)}, bf16[4096,128]{1,0:T(8,128)(2,1)S(1)}) custom-call(s32[3,4096]{1,0:T(4,128)S(1)} %copy-done, f32[1,4096]{1,0:T(1,128)S(1)} %bitcast.2), custom_call_target="tpu_custom_call" | custom-call | flops 8388608 | bytes 5242880 | tf_op jit(solution)/shard_map/gaunt_tables/pallas_call | solution.py:179
  24.6 6.2 %collective-permute-done.4 = f32[162,256]{1,0:T(8,128)S(1)} collective-permute-done((f32[162,256]{1,0:T(8,128)S(1)}, f32[162,256]{1,0:T(8,128)S(1)}, u32[]{:S(2)}, u32[]{:S(2)}) %collective-permute-start.4) | collective-permute-done | bytes 165920 | tf_op jit(solution)/shard_map/ppermute | solution.py:325
  30.8 0.3 fusion
  31.4 0.4 collective-permute-start.5
  31.7 1.5 %collective-permute-start.6 = (f32[80,128]{1,0:T(8,128)S(1)}, f32[80,128]{1,0:T(8,128)S(1)}, u32[]{:S(2)}, u32[]{:S(2)}) collective-permute-start(f32[80,128]{1,0:T(8,128)S(1)} %get-tuple-element.41), channel_id=1, source_target_pairs={{0,1},{1,0},{2,3},{3,2},{4,5},{5,4},{6,7},{7,6},{8,9},{9,8},{10,11... | collective-permute-start | bytes 122888 | tf_op jit(solution)/shard_map/ppermute | solution.py:325
  33.3 2.4 %collective-permute-done.6 = f32[80,128]{1,0:T(8,128)S(1)} collective-permute-done((f32[80,128]{1,0:T(8,128)S(1)}, f32[80,128]{1,0:T(8,128)S(1)}, u32[]{:S(2)}, u32[]{:S(2)}) %collective-permute-start.6) | collective-permute-done | bytes 40992 | tf_op jit(solution)/shard_map/ppermute | solution.py:325
  35.7 1.4 %collective-permute-done.7 = f32[80,128]{1,0:T(8,128)S(1)} collective-permute-done((f32[80,128]{1,0:T(8,128)S(1)}, f32[80,128]{1,0:T(8,128)S(1)}, u32[]{:S(2)}, u32[]{:S(2)}) %collective-permute-start.7) | collective-permute-done | bytes 40992 | tf_op jit(solution)/shard_map/ppermute | solution.py:325
  37.1 1.3 %collective-permute-start.10 = (f32[80,128]{1,0:T(8,128)S(1)}, f32[80,128]{1,0:T(8,128)S(1)}, u32[]{:S(2)}, u32[]{:S(2)}) collective-permute-start(f32[80,128]{1,0:T(8,128)S(1)} %add_add_fusion.2), channel_id=1, source_target_pairs={{0,12},{1,13},{2,14},{3,15},{4,8},{5,9},{6,10},{7,11},{8,4},{9,5},... | collective-permute-start | bytes 122888 | tf_op jit(solution)/shard_map/ppermute | solution.py:325
  38.5 1.9 %collective-permute-start.9 = (f32[80,128]{1,0:T(8,128)S(1)}, f32[80,128]{1,0:T(8,128)S(1)}, u32[]{:S(2)}, u32[]{:S(2)}) collective-permute-start(f32[80,128]{1,0:T(8,128)S(1)} %add_add_fusion.2), channel_id=1, source_target_pairs={{0,10},{1,11},{2,8},{3,9},{4,14},{5,15},{6,12},{7,13},{8,2},{9,3},... | collective-permute-start | bytes 122888 | tf_op jit(solution)/shard_map/ppermute | solution.py:325
  40.4 1.8 %collective-permute-done.10 = f32[80,128]{1,0:T(8,128)S(1)} collective-permute-done((f32[80,128]{1,0:T(8,128)S(1)}, f32[80,128]{1,0:T(8,128)S(1)}, u32[]{:S(2)}, u32[]{:S(2)}) %collective-permute-start.10) | collective-permute-done | bytes 40992 | tf_op jit(solution)/shard_map/ppermute | solution.py:325
  42.2 0.5 %collective-permute-done.8 = f32[80,128]{1,0:T(8,128)S(1)} collective-permute-done((f32[80,128]{1,0:T(8,128)S(1)}, f32[80,128]{1,0:T(8,128)S(1)}, u32[]{:S(2)}, u32[]{:S(2)}) %collective-permute-start.8) | collective-permute-done | bytes 40992 | tf_op jit(solution)/shard_map/ppermute | solution.py:325
  42.7 0.2 collective-permute-start.11
  42.9 1.1 %collective-permute-done.11 = f32[80,128]{1,0:T(8,128)S(1)} collective-permute-done((f32[80,128]{1,0:T(8,128)S(1)}, f32[80,128]{1,0:T(8,128)S(1)}, u32[]{:S(2)}, u32[]{:S(2)}) %collective-permute-start.11) | collective-permute-done | bytes 40992 | tf_op jit(solution)/shard_map/ppermute | solution.py:325
  44.0 1.8 %finish.1 = (f32[162,162]{1,0:T(8,128)}, f32[4,81]{1,0:T(4,128)}) custom-call(f32[80,128]{1,0:T(8,128)S(1)} %get-tuple-element.39.top_ref, f32[80,128]{1,0:T(8,128)S(1)} %get-tuple-element.38.bottom_ref, bf16[256,4096]{1,0:T(8,128)(2,1)S(1)} %get-tuple-element.29.second_ref, f32[88,4096]{1,0:T(8,128)S(1)} %get-tuple-element.30.first_ref, ...), custom_call_target="tpu_custom_call" | custom-call | tf_op jit(solution)/shard_map/finish/pallas_call | solution.py:249
  (23 shorter events, 0.5 us)
Async XLA Ops:
  5.0 2.6 %collective-permute-start = (f32[162,1024]{1,0:T(8,128)S(1)}, f32[162,1024]{1,0:T(8,128)S(1)}, u32[]{:S(2)}, u32[]{:S(2)}) collective-permute-start(f32[162,1024]{1,0:T(8,128)S(1)} %get-tuple-element.18), channel_id=1, source_target_pairs={{0,2},{1,3},{2,0},{3,1},{4,6},{5,7},{6,4},{7,5},{8,10},{9,11},{10,... | collective-permute-start | bytes 1990664 | tf_op jit(solution)/shard_map/ppermute | solution.py:325
  7.7 15.8 %copy-start = (s32[3,4096]{1,0:T(4,128)S(1)}, s32[3,4096]{1,0:T(4,128)}, u32[]{:S(2)}) copy-start(s32[3,4096]{1,0:T(4,128)} %index_ref) | copy-start | bytes 147460
  7.7 15.8 %copy-start.1 = (f32[4096]{0:T(1024)S(1)}, f32[4096]{0:T(1024)}, u32[]{:S(2)}) copy-start(f32[4096]{0:T(1024)} %param.9) | copy-start | bytes 49156
  7.9 11.1 %collective-permute-start.1 = (f32[162,256]{1,0:T(8,128)S(1)}, f32[162,256]{1,0:T(8,128)S(1)}, u32[]{:S(2)}, u32[]{:S(2)}) collective-permute-start(f32[162,256]{1,0:T(8,128)S(1)} %get-tuple-element.34), channel_id=1, source_target_pairs={{0,6},{1,7},{2,4},{3,5},{4,2},{5,3},{6,0},{7,1},{8,14},{9,15},{10,... | collective-permute-start | bytes 497672 | tf_op jit(solution)/shard_map/ppermute | solution.py:325
  10.5 8.4 %collective-permute-start.3 = (f32[162,256]{1,0:T(8,128)S(1)}, f32[162,256]{1,0:T(8,128)S(1)}, u32[]{:S(2)}, u32[]{:S(2)}) collective-permute-start(f32[162,256]{1,0:T(8,128)S(1)} %get-tuple-element.35), channel_id=1, source_target_pairs={{0,12},{1,13},{2,14},{3,15},{4,8},{5,9},{6,10},{7,11},{8,4},{9,5},... | collective-permute-start | bytes 497672 | tf_op jit(solution)/shard_map/ppermute | solution.py:325
  12.1 7.7 %collective-permute-start.2 = (f32[162,256]{1,0:T(8,128)S(1)}, f32[162,256]{1,0:T(8,128)S(1)}, u32[]{:S(2)}, u32[]{:S(2)}) collective-permute-start(f32[162,256]{1,0:T(8,128)S(1)} %slice_select_fusion.2), channel_id=1, source_target_pairs={{0,10},{1,11},{2,8},{3,9},{4,14},{5,15},{6,12},{7,13},{8,2},{9,3},... | collective-permute-start | bytes 497672 | tf_op jit(solution)/shard_map/ppermute | solution.py:325
  19.9 10.9 %collective-permute-start.4 = (f32[162,256]{1,0:T(8,128)S(1)}, f32[162,256]{1,0:T(8,128)S(1)}, u32[]{:S(2)}, u32[]{:S(2)}) collective-permute-start(f32[162,256]{1,0:T(8,128)S(1)} %add_add_fusion), channel_id=1, source_target_pairs={{0,18},{1,19},{2,16},{3,17},{4,22},{5,23},{6,20},{7,21},{8,26},{9,... | collective-permute-start | bytes 497672 | tf_op jit(solution)/shard_map/ppermute | solution.py:325
  31.4 1.9 %collective-permute-start.5 = (f32[80,128]{1,0:T(8,128)S(1)}, f32[80,128]{1,0:T(8,128)S(1)}, u32[]{:S(2)}, u32[]{:S(2)}) collective-permute-start(f32[80,128]{1,0:T(8,128)S(1)} %get-tuple-element.40), channel_id=1, source_target_pairs={{0,2},{1,3},{2,0},{3,1},{4,6},{5,7},{6,4},{7,5},{8,10},{9,11},{10,... | collective-permute-start | bytes 122888 | tf_op jit(solution)/shard_map/ppermute | solution.py:325
  31.7 4.0 %collective-permute-start.6 = (f32[80,128]{1,0:T(8,128)S(1)}, f32[80,128]{1,0:T(8,128)S(1)}, u32[]{:S(2)}, u32[]{:S(2)}) collective-permute-start(f32[80,128]{1,0:T(8,128)S(1)} %get-tuple-element.41), channel_id=1, source_target_pairs={{0,1},{1,0},{2,3},{3,2},{4,5},{5,4},{6,7},{7,6},{8,9},{9,8},{10,11... | collective-permute-start | bytes 122888 | tf_op jit(solution)/shard_map/ppermute | solution.py:325
  33.3 3.8 %collective-permute-start.7 = (f32[80,128]{1,0:T(8,128)S(1)}, f32[80,128]{1,0:T(8,128)S(1)}, u32[]{:S(2)}, u32[]{:S(2)}) collective-permute-start(f32[80,128]{1,0:T(8,128)S(1)} %get-tuple-element.40), channel_id=1, source_target_pairs={{0,3},{1,2},{2,1},{3,0},{4,7},{5,6},{6,5},{7,4},{8,11},{9,10},{10,... | collective-permute-start | bytes 122888 | tf_op jit(solution)/shard_map/ppermute | solution.py:325
  37.1 5.1 %collective-permute-start.10 = (f32[80,128]{1,0:T(8,128)S(1)}, f32[80,128]{1,0:T(8,128)S(1)}, u32[]{:S(2)}, u32[]{:S(2)}) collective-permute-start(f32[80,128]{1,0:T(8,128)S(1)} %add_add_fusion.2), channel_id=1, source_target_pairs={{0,12},{1,13},{2,14},{3,15},{4,8},{5,9},{6,10},{7,11},{8,4},{9,5},... | collective-permute-start | bytes 122888 | tf_op jit(solution)/shard_map/ppermute | solution.py:325
  38.5 4.2 %collective-permute-start.8 = (f32[80,128]{1,0:T(8,128)S(1)}, f32[80,128]{1,0:T(8,128)S(1)}, u32[]{:S(2)}, u32[]{:S(2)}) collective-permute-start(f32[80,128]{1,0:T(8,128)S(1)} %add_add_fusion.2), channel_id=1, source_target_pairs={{0,6},{1,7},{2,4},{3,5},{4,2},{5,3},{6,0},{7,1},{8,14},{9,15},{10,... | collective-permute-start | bytes 122888 | tf_op jit(solution)/shard_map/ppermute | solution.py:325
  38.5 4.2 %collective-permute-start.9 = (f32[80,128]{1,0:T(8,128)S(1)}, f32[80,128]{1,0:T(8,128)S(1)}, u32[]{:S(2)}, u32[]{:S(2)}) collective-permute-start(f32[80,128]{1,0:T(8,128)S(1)} %add_add_fusion.2), channel_id=1, source_target_pairs={{0,10},{1,11},{2,8},{3,9},{4,14},{5,15},{6,12},{7,13},{8,2},{9,3},... | collective-permute-start | bytes 122888 | tf_op jit(solution)/shard_map/ppermute | solution.py:325
  42.7 1.3 %collective-permute-start.11 = (f32[80,128]{1,0:T(8,128)S(1)}, f32[80,128]{1,0:T(8,128)S(1)}, u32[]{:S(2)}, u32[]{:S(2)}) collective-permute-start(f32[80,128]{1,0:T(8,128)S(1)} %add_add_fusion.1), channel_id=1, source_target_pairs={{0,2},{1,3},{2,0},{3,1},{4,6},{5,7},{6,4},{7,5},{8,10},{9,11},{10,... | collective-permute-start | bytes 122888 | tf_op jit(solution)/shard_map/ppermute | solution.py:325

commit v8 on v7

--- a/solution.py
+++ b/solution.py
@@ -10,7 +10,7 @@
 LANES = 128
 SPILL_LOW, SPILL_HIGH = 48, 56
 TILE = 1024
-LEAVING_STEPS, STAYING_STEPS, LAST_STEPS = 2, 1, 2
+LEAVING_STEPS, STAYING_STEPS, LAST_STEPS = 2, 2, 2
 GROUP = 2
 VMEM_LIMIT = 52 * 2**20
 

time: 46.1 us -> 46 us (level)
  no operation moved by 1% of the time
where the time goes in v8:
time: 46 us; the launch traced here: 45.8 us
  waiting for transfers between devices  21.2 us (46%)
  starting transfers between devices  12.9 us (28%)
  Pallas kernels  9.41 us (20%)
  local copies, waits for them, and re-layouts  0.85 us (2%)
  between operations  0.76 us (2%)
    ppermute x12, waiting for transfers between devices, exchange(): return lax.ppermute(block, ('basis', 'band'), pairs)  21.2 us
    ppermute x12, starting transfers between devices, exchange(): return lax.ppermute(block, ('basis', 'band'), pairs)  12.9 us
    pallas_call x1, Pallas kernels, first_products(): pl.pallas_call(functools.partial(first_kernel, columns), out_shape=(jax.S...  4.32 us
    pallas_call x1, Pallas kernels, second_products(): pl.pallas_call(functools.partial(second_kernel, columns), out_shape=jax.S...  2.15 us
    pallas_call x1, Pallas kernels, finish(): pl.pallas_call(functools.partial(finish_kernel, tile), out_shape=(jax.Sha...  1.84 us
    pallas_call x1, Pallas kernels, gaunt_tables(): pl.pallas_call(tables_kernel, out_shape=shapes, in_specs=[VMEM, VMEM], ou...  1.11 us
  transfers between devices with their start and end apart: 12, of which 8 were waited for; matrix products, arithmetic and copies ran while one was open for 2% of the time, Pallas kernels for 7%

profile of v8, /device:TPU:0, one launch (start us, length us, event | category | flops | bytes accessed | tf_op | source)
XLA Modules:
  0.0 45.8 jit_solution(7677081699541369896)
XLA Ops:
  0.6 4.3 %first_products.1 = (f32[162,1024]{1,0:T(8,128)S(1)}, f32[162,512]{1,0:T(8,128)S(1)}, bf16[162,2560]{1,0:T(8,128)(2,1)S(1)}) custom-call(s32[1]{0:T(128)} %bitcast.own_ref, bf16[162,2560]{1,0:T(8,128)(2,1)} %matching_hbm.1, bf16[2560,2048]{1,0:T(8,128)(2,1)} %vectors_hbm.3), custom_call_target="tpu_custom_call" | custom-call | flops 1274019840 | bytes 9689088 | tf_op jit(solution)/shard_map/first_products/pallas_call | solution.py:120
  5.0 0.5 %collective-permute-start = (f32[162,1024]{1,0:T(8,128)S(1)}, f32[162,1024]{1,0:T(8,128)S(1)}, u32[]{:S(2)}, u32[]{:S(2)}) collective-permute-start(f32[162,1024]{1,0:T(8,128)S(1)} %get-tuple-element.18), channel_id=1, source_target_pairs={{0,2},{1,3},{2,0},{3,1},{4,6},{5,7},{6,4},{7,5},{8,10},{9,11},{10,... | collective-permute-start | bytes 1990664 | tf_op jit(solution)/shard_map/ppermute | solution.py:325
  5.5 2.1 %second_products.1 = f32[162,512]{1,0:T(8,128)S(1)} custom-call(s32[1]{0:T(128)} %bitcast.own_ref, bf16[162,2560]{1,0:T(8,128)(2,1)S(1)} %get-tuple-element.17.matching, bf16[2560,2048]{1,0:T(8,128)(2,1)} %vectors_hbm.3), custom_call_target="tpu_custom_call" | custom-call | flops 424673280 | bytes 3782656 | tf_op jit(solution)/shard_map/second_products/pallas_call | solution.py:142
  7.7 0.1 broadcast_select_fusion.1
  7.9 2.7 %collective-permute-start.1 = (f32[162,256]{1,0:T(8,128)S(1)}, f32[162,256]{1,0:T(8,128)S(1)}, u32[]{:S(2)}, u32[]{:S(2)}) collective-permute-start(f32[162,256]{1,0:T(8,128)S(1)} %get-tuple-element.34), channel_id=1, source_target_pairs={{0,6},{1,7},{2,4},{3,5},{4,2},{5,3},{6,0},{7,1},{8,14},{9,15},{10,... | collective-permute-start | bytes 497672 | tf_op jit(solution)/shard_map/ppermute | solution.py:325
  10.5 1.6 %collective-permute-start.3 = (f32[162,256]{1,0:T(8,128)S(1)}, f32[162,256]{1,0:T(8,128)S(1)}, u32[]{:S(2)}, u32[]{:S(2)}) collective-permute-start(f32[162,256]{1,0:T(8,128)S(1)} %get-tuple-element.35), channel_id=1, source_target_pairs={{0,12},{1,13},{2,14},{3,15},{4,8},{5,9},{6,10},{7,11},{8,4},{9,5},... | collective-permute-start | bytes 497672 | tf_op jit(solution)/shard_map/ppermute | solution.py:325
  12.2 6.8 %collective-permute-done.1 = f32[162,256]{1,0:T(8,128)S(1)} collective-permute-done((f32[162,256]{1,0:T(8,128)S(1)}, f32[162,256]{1,0:T(8,128)S(1)}, u32[]{:S(2)}, u32[]{:S(2)}) %collective-permute-start.1) | collective-permute-done | bytes 165920 | tf_op jit(solution)/shard_map/ppermute | solution.py:325
  18.9 1.0 %collective-permute-done.2 = f32[162,256]{1,0:T(8,128)S(1)} collective-permute-done((f32[162,256]{1,0:T(8,128)S(1)}, f32[162,256]{1,0:T(8,128)S(1)}, u32[]{:S(2)}, u32[]{:S(2)}) %collective-permute-start.2) | collective-permute-done | bytes 165920 | tf_op jit(solution)/shard_map/ppermute | solution.py:325
  20.0 2.7 %collective-permute-start.4 = (f32[162,256]{1,0:T(8,128)S(1)}, f32[162,256]{1,0:T(8,128)S(1)}, u32[]{:S(2)}, u32[]{:S(2)}) collective-permute-start(f32[162,256]{1,0:T(8,128)S(1)} %add_add_fusion), channel_id=1, source_target_pairs={{0,18},{1,19},{2,16},{3,17},{4,22},{5,23},{6,20},{7,21},{8,26},{9,... | collective-permute-start | bytes 497672 | tf_op jit(solution)/shard_map/ppermute | solution.py:325
  22.7 0.8 %dynamic_slice.3 = f32[256]{0:T(256)S(1)} dynamic-slice(f32[2048]{0:T(1024)} %param.7, s32[]{:T(128)S(6)} %select_n.78), dynamic_slice_sizes={256} | dynamic-slice | bytes 2052 | tf_op jit(solution)/shard_map/dynamic_slice | solution.py:348
  23.5 1.1 %gaunt_tables.1 = (bf16[256,4096]{1,0:T(8,128)(2,1)S(1)}, f32[88,4096]{1,0:T(8,128)S(1)}, bf16[4096,128]{1,0:T(8,128)(2,1)S(1)}) custom-call(s32[3,4096]{1,0:T(4,128)S(1)} %copy-done, f32[1,4096]{1,0:T(1,128)S(1)} %bitcast.2), custom_call_target="tpu_custom_call" | custom-call | flops 8388608 | bytes 5242880 | tf_op jit(solution)/shard_map/gaunt_tables/pallas_call | solution.py:179
  24.6 6.3 %collective-permute-done.4 = f32[162,256]{1,0:T(8,128)S(1)} collective-permute-done((f32[162,256]{1,0:T(8,128)S(1)}, f32[162,256]{1,0:T(8,128)S(1)}, u32[]{:S(2)}, u32[]{:S(2)}) %collective-permute-start.4) | collective-permute-done | bytes 165920 | tf_op jit(solution)/shard_map/ppermute | solution.py:325
  30.8 0.3 fusion
  31.4 0.4 collective-permute-start.5
  31.7 1.5 %collective-permute-start.6 = (f32[80,128]{1,0:T(8,128)S(1)}, f32[80,128]{1,0:T(8,128)S(1)}, u32[]{:S(2)}, u32[]{:S(2)}) collective-permute-start(f32[80,128]{1,0:T(8,128)S(1)} %get-tuple-element.41), channel_id=1, source_target_pairs={{0,1},{1,0},{2,3},{3,2},{4,5},{5,4},{6,7},{7,6},{8,9},{9,8},{10,11... | collective-permute-start | bytes 122888 | tf_op jit(solution)/shard_map/ppermute | solution.py:325
  33.3 2.4 %collective-permute-done.6 = f32[80,128]{1,0:T(8,128)S(1)} collective-permute-done((f32[80,128]{1,0:T(8,128)S(1)}, f32[80,128]{1,0:T(8,128)S(1)}, u32[]{:S(2)}, u32[]{:S(2)}) %collective-permute-start.6) | collective-permute-done | bytes 40992 | tf_op jit(solution)/shard_map/ppermute | solution.py:325
  35.7 1.4 %collective-permute-done.7 = f32[80,128]{1,0:T(8,128)S(1)} collective-permute-done((f32[80,128]{1,0:T(8,128)S(1)}, f32[80,128]{1,0:T(8,128)S(1)}, u32[]{:S(2)}, u32[]{:S(2)}) %collective-permute-start.7) | collective-permute-done | bytes 40992 | tf_op jit(solution)/shard_map/ppermute | solution.py:325
  37.1 1.3 %collective-permute-start.10 = (f32[80,128]{1,0:T(8,128)S(1)}, f32[80,128]{1,0:T(8,128)S(1)}, u32[]{:S(2)}, u32[]{:S(2)}) collective-permute-start(f32[80,128]{1,0:T(8,128)S(1)} %add_add_fusion.2), channel_id=1, source_target_pairs={{0,12},{1,13},{2,14},{3,15},{4,8},{5,9},{6,10},{7,11},{8,4},{9,5},... | collective-permute-start | bytes 122888 | tf_op jit(solution)/shard_map/ppermute | solution.py:325
  38.5 1.9 %collective-permute-start.9 = (f32[80,128]{1,0:T(8,128)S(1)}, f32[80,128]{1,0:T(8,128)S(1)}, u32[]{:S(2)}, u32[]{:S(2)}) collective-permute-start(f32[80,128]{1,0:T(8,128)S(1)} %add_add_fusion.2), channel_id=1, source_target_pairs={{0,10},{1,11},{2,8},{3,9},{4,14},{5,15},{6,12},{7,13},{8,2},{9,3},... | collective-permute-start | bytes 122888 | tf_op jit(solution)/shard_map/ppermute | solution.py:325
  40.4 1.8 %collective-permute-done.10 = f32[80,128]{1,0:T(8,128)S(1)} collective-permute-done((f32[80,128]{1,0:T(8,128)S(1)}, f32[80,128]{1,0:T(8,128)S(1)}, u32[]{:S(2)}, u32[]{:S(2)}) %collective-permute-start.10) | collective-permute-done | bytes 40992 | tf_op jit(solution)/shard_map/ppermute | solution.py:325
  42.2 0.5 %collective-permute-done.8 = f32[80,128]{1,0:T(8,128)S(1)} collective-permute-done((f32[80,128]{1,0:T(8,128)S(1)}, f32[80,128]{1,0:T(8,128)S(1)}, u32[]{:S(2)}, u32[]{:S(2)}) %collective-permute-start.8) | collective-permute-done | bytes 40992 | tf_op jit(solution)/shard_map/ppermute | solution.py:325
  42.7 0.2 collective-permute-start.11
  42.9 1.1 %collective-permute-done.11 = f32[80,128]{1,0:T(8,128)S(1)} collective-permute-done((f32[80,128]{1,0:T(8,128)S(1)}, f32[80,128]{1,0:T(8,128)S(1)}, u32[]{:S(2)}, u32[]{:S(2)}) %collective-permute-start.11) | collective-permute-done | bytes 40992 | tf_op jit(solution)/shard_map/ppermute | solution.py:325
  44.0 1.8 %finish.1 = (f32[162,162]{1,0:T(8,128)}, f32[4,81]{1,0:T(4,128)}) custom-call(f32[80,128]{1,0:T(8,128)S(1)} %get-tuple-element.39.top_ref, f32[80,128]{1,0:T(8,128)S(1)} %get-tuple-element.38.bottom_ref, bf16[256,4096]{1,0:T(8,128)(2,1)S(1)} %get-tuple-element.29.second_ref, f32[88,4096]{1,0:T(8,128)S(1)} %get-tuple-element.30.first_ref, ...), custom_call_target="tpu_custom_call" | custom-call | tf_op jit(solution)/shard_map/finish/pallas_call | solution.py:249
  (23 shorter events, 0.5 us)
Async XLA Ops:
  5.0 2.7 %collective-permute-start = (f32[162,1024]{1,0:T(8,128)S(1)}, f32[162,1024]{1,0:T(8,128)S(1)}, u32[]{:S(2)}, u32[]{:S(2)}) collective-permute-start(f32[162,1024]{1,0:T(8,128)S(1)} %get-tuple-element.18), channel_id=1, source_target_pairs={{0,2},{1,3},{2,0},{3,1},{4,6},{5,7},{6,4},{7,5},{8,10},{9,11},{10,... | collective-permute-start | bytes 1990664 | tf_op jit(solution)/shard_map/ppermute | solution.py:325
  7.7 15.8 %copy-start = (s32[3,4096]{1,0:T(4,128)S(1)}, s32[3,4096]{1,0:T(4,128)}, u32[]{:S(2)}) copy-start(s32[3,4096]{1,0:T(4,128)} %index_ref) | copy-start | bytes 147460
  7.7 15.8 %copy-start.1 = (f32[4096]{0:T(1024)S(1)}, f32[4096]{0:T(1024)}, u32[]{:S(2)}) copy-start(f32[4096]{0:T(1024)} %param.9) | copy-start | bytes 49156
  7.9 11.1 %collective-permute-start.1 = (f32[162,256]{1,0:T(8,128)S(1)}, f32[162,256]{1,0:T(8,128)S(1)}, u32[]{:S(2)}, u32[]{:S(2)}) collective-permute-start(f32[162,256]{1,0:T(8,128)S(1)} %get-tuple-element.34), channel_id=1, source_target_pairs={{0,6},{1,7},{2,4},{3,5},{4,2},{5,3},{6,0},{7,1},{8,14},{9,15},{10,... | collective-permute-start | bytes 497672 | tf_op jit(solution)/shard_map/ppermute | solution.py:325
  10.5 8.4 %collective-permute-start.3 = (f32[162,256]{1,0:T(8,128)S(1)}, f32[162,256]{1,0:T(8,128)S(1)}, u32[]{:S(2)}, u32[]{:S(2)}) collective-permute-start(f32[162,256]{1,0:T(8,128)S(1)} %get-tuple-element.35), channel_id=1, source_target_pairs={{0,12},{1,13},{2,14},{3,15},{4,8},{5,9},{6,10},{7,11},{8,4},{9,5},... | collective-permute-start | bytes 497672 | tf_op jit(solution)/shard_map/ppermute | solution.py:325
  12.1 7.8 %collective-permute-start.2 = (f32[162,256]{1,0:T(8,128)S(1)}, f32[162,256]{1,0:T(8,128)S(1)}, u32[]{:S(2)}, u32[]{:S(2)}) collective-permute-start(f32[162,256]{1,0:T(8,128)S(1)} %slice_select_fusion.2), channel_id=1, source_target_pairs={{0,10},{1,11},{2,8},{3,9},{4,14},{5,15},{6,12},{7,13},{8,2},{9,3},... | collective-permute-start | bytes 497672 | tf_op jit(solution)/shard_map/ppermute | solution.py:325
  20.0 10.9 %collective-permute-start.4 = (f32[162,256]{1,0:T(8,128)S(1)}, f32[162,256]{1,0:T(8,128)S(1)}, u32[]{:S(2)}, u32[]{:S(2)}) collective-permute-start(f32[162,256]{1,0:T(8,128)S(1)} %add_add_fusion), channel_id=1, source_target_pairs={{0,18},{1,19},{2,16},{3,17},{4,22},{5,23},{6,20},{7,21},{8,26},{9,... | collective-permute-start | bytes 497672 | tf_op jit(solution)/shard_map/ppermute | solution.py:325
  31.4 1.9 %collective-permute-start.5 = (f32[80,128]{1,0:T(8,128)S(1)}, f32[80,128]{1,0:T(8,128)S(1)}, u32[]{:S(2)}, u32[]{:S(2)}) collective-permute-start(f32[80,128]{1,0:T(8,128)S(1)} %get-tuple-element.40), channel_id=1, source_target_pairs={{0,2},{1,3},{2,0},{3,1},{4,6},{5,7},{6,4},{7,5},{8,10},{9,11},{10,... | collective-permute-start | bytes 122888 | tf_op jit(solution)/shard_map/ppermute | solution.py:325
  31.7 4.0 %collective-permute-start.6 = (f32[80,128]{1,0:T(8,128)S(1)}, f32[80,128]{1,0:T(8,128)S(1)}, u32[]{:S(2)}, u32[]{:S(2)}) collective-permute-start(f32[80,128]{1,0:T(8,128)S(1)} %get-tuple-element.41), channel_id=1, source_target_pairs={{0,1},{1,0},{2,3},{3,2},{4,5},{5,4},{6,7},{7,6},{8,9},{9,8},{10,11... | collective-permute-start | bytes 122888 | tf_op jit(solution)/shard_map/ppermute | solution.py:325
  33.3 3.8 %collective-permute-start.7 = (f32[80,128]{1,0:T(8,128)S(1)}, f32[80,128]{1,0:T(8,128)S(1)}, u32[]{:S(2)}, u32[]{:S(2)}) collective-permute-start(f32[80,128]{1,0:T(8,128)S(1)} %get-tuple-element.40), channel_id=1, source_target_pairs={{0,3},{1,2},{2,1},{3,0},{4,7},{5,6},{6,5},{7,4},{8,11},{9,10},{10,... | collective-permute-start | bytes 122888 | tf_op jit(solution)/shard_map/ppermute | solution.py:325
  37.1 5.1 %collective-permute-start.10 = (f32[80,128]{1,0:T(8,128)S(1)}, f32[80,128]{1,0:T(8,128)S(1)}, u32[]{:S(2)}, u32[]{:S(2)}) collective-permute-start(f32[80,128]{1,0:T(8,128)S(1)} %add_add_fusion.2), channel_id=1, source_target_pairs={{0,12},{1,13},{2,14},{3,15},{4,8},{5,9},{6,10},{7,11},{8,4},{9,5},... | collective-permute-start | bytes 122888 | tf_op jit(solution)/shard_map/ppermute | solution.py:325
  38.4 4.2 %collective-permute-start.8 = (f32[80,128]{1,0:T(8,128)S(1)}, f32[80,128]{1,0:T(8,128)S(1)}, u32[]{:S(2)}, u32[]{:S(2)}) collective-permute-start(f32[80,128]{1,0:T(8,128)S(1)} %add_add_fusion.2), channel_id=1, source_target_pairs={{0,6},{1,7},{2,4},{3,5},{4,2},{5,3},{6,0},{7,1},{8,14},{9,15},{10,... | collective-permute-start | bytes 122888 | tf_op jit(solution)/shard_map/ppermute | solution.py:325
  38.5 4.2 %collective-permute-start.9 = (f32[80,128]{1,0:T(8,128)S(1)}, f32[80,128]{1,0:T(8,128)S(1)}, u32[]{:S(2)}, u32[]{:S(2)}) collective-permute-start(f32[80,128]{1,0:T(8,128)S(1)} %add_add_fusion.2), channel_id=1, source_target_pairs={{0,10},{1,11},{2,8},{3,9},{4,14},{5,15},{6,12},{7,13},{8,2},{9,3},... | collective-permute-start | bytes 122888 | tf_op jit(solution)/shard_map/ppermute | solution.py:325
  42.7 1.3 %collective-permute-start.11 = (f32[80,128]{1,0:T(8,128)S(1)}, f32[80,128]{1,0:T(8,128)S(1)}, u32[]{:S(2)}, u32[]{:S(2)}) collective-permute-start(f32[80,128]{1,0:T(8,128)S(1)} %add_add_fusion.1), channel_id=1, source_target_pairs={{0,2},{1,3},{2,0},{3,1},{4,6},{5,7},{6,4},{7,5},{8,10},{9,11},{10,... | collective-permute-start | bytes 122888 | tf_op jit(solution)/shard_map/ppermute | solution.py:325
